TPU v7x, 128 devices: a whole 4x4x4 slice. The times are simulated.
128 devices in a mesh: pix: 64 (over x, z, y_lo, core), ch: 2 (over y_hi).
Axes of the slice: x: 4, y: 4 (y_hi: 2, y_lo: 2; y = y_hi * 2 + y_lo), z: 4, core: 2. Of those that a mesh axis runs over, the one named last changes fastest.
Arguments:
- features: bfloat16 [32, 2048, 2048], P(None, 'pix'), may hold values from -6 to 6
- grad_out: bfloat16 [32, 2048, 2048], P('ch', 'pix'), may hold values from -6 to 6
- cheb_weight: bfloat16 [4, 32, 32], P(None, None, 'ch'), may hold values from -0.5 to 0.5
- east_weight: float32 [2048, 2048], P('pix'), may hold values from 0.05 to 0.25
- south_weight: float32 [2048, 2048], P('pix'), may hold values from 0.05 to 0.25
- pixel_mask: int32 [2048, 2048], P('pix'), may hold values 0 or 1
Outputs:
- input_grad: bfloat16 [32, 2048, 2048], P('ch', 'pix')
- weight_grad: float32 [4, 32, 32], P(None, None, 'ch')
All inputs are finite; a program needn't handle non-finite values. No bound on the sum of `pixel_mask` on one device may be relied on, other than what follows from the above.
Results may differ from a plain program's by a relative error of at most 0.006.
Values may be sent and summed in bfloat16 or wider, within the bound.
No kernel may reach another device: no remote copies, remote signals or barrier semaphores. Data moves between devices by JAX's collectives and lax.ppermute only.
A program may use at most 128 MiB of HBM per device.

v0:
```python
import jax
import jax.numpy as jnp
from jax import lax
from jax.sharding import PartitionSpec as P


def padded_2(value, sides, width):
    for axis, dim in sides:
        size, length = (lax.axis_size(axis), value.shape[dim])
        up = [(i, (i + 1) % size) for i in range(size - 1)]
        down = [(j, i) for i, j in up]
        last = lax.slice_in_dim(value, length - width, length, axis=dim)
        initial = lax.slice_in_dim(value, 0, width, axis=dim)
        before = lax.ppermute(last, axis, up)
        after = lax.ppermute(initial, axis, down)
        value = jnp.concatenate([before, value, after], axis=dim)
    return value


def edge_weights(east_weight, south_weight, pixel_mask):
    rows_here, width = east_weight.shape
    maskf = pixel_mask.astype(jnp.float32)
    stacked = jnp.stack([south_weight, maskf])
    padded = padded_2(stacked.astype(jnp.bfloat16), (("pix", 1),), 1).astype(stacked.dtype)
    south_pad = padded[0]
    mask_pad = padded[1]
    globrow = lax.axis_index("pix") * rows_here + jnp.arange(rows_here + 1) - 1
    face_keep = ((globrow + 1) % width != 0).astype(jnp.float32)[:, None]
    south_full = south_pad[:-1] * mask_pad[:-1] * mask_pad[1:] * face_keep
    south_eff = south_full[1:]
    north_eff = south_full[:-1]
    columns = jnp.arange(width)
    mask_right = jnp.concatenate([maskf[:, 1:], jnp.zeros((rows_here, 1), jnp.float32)], axis=1)
    east_eff = east_weight * maskf * mask_right * (columns < width - 1).astype(jnp.float32)[None, :]
    west_eff = jnp.concatenate([jnp.zeros((rows_here, 1), jnp.float32), east_eff[:, :-1]], axis=1)
    return (east_eff, west_eff, south_eff, north_eff)


def operate(field, wts):
    east_eff, west_eff, south_eff, north_eff = wts
    padded = padded_2(field.astype(jnp.bfloat16), (("pix", 1),), 1).astype(field.dtype)
    zcol = jnp.zeros((field.shape[0], field.shape[1], 1), jnp.float32)
    right = jnp.concatenate([field[:, :, 1:], zcol], axis=2)
    left = jnp.concatenate([zcol, field[:, :, :-1]], axis=2)
    return -(
        east_eff * right + west_eff * left + south_eff * padded[:, 2:] + north_eff * padded[:, :-2]
    )


def clenshaw(parts, wts):
    clen = parts[-1]
    clen_next = jnp.zeros_like(clen)
    for order in range(len(parts) - 2, 0, -1):
        clen, clen_next = (parts[order] + 2.0 * operate(clen, wts) - clen_next, clen)
    return parts[0] + operate(clen, wts) - clen_next


def forward_grads(feats, cotangent, nterms, wts):
    grads = []
    prev_term = None
    term_now = feats.astype(jnp.float32)
    for order in range(nterms):
        if order == 1:
            prev_term, term_now = (term_now, operate(term_now, wts))
        elif order > 1:
            prev_term, term_now = (term_now, 2.0 * operate(term_now, wts) - prev_term)
        term_b = term_now.astype(jnp.bfloat16)
        grads.append(
            jnp.einsum("irn,orn->io", term_b, cotangent, preferred_element_type=jnp.float32)
        )
    return jnp.stack(grads)


def per_device(features, grad_out, cheb_weight, east_weight, south_weight, pixel_mask):
    wts = edge_weights(east_weight, south_weight, pixel_mask)
    nterms = cheb_weight.shape[0]
    total_pixels = features.shape[1] * lax.axis_size("pix") * features.shape[2]
    local_grad = forward_grads(features, grad_out, nterms, wts)
    weight_grad = lax.psum(local_grad, "pix") / jnp.sqrt(jnp.float32(total_pixels))
    parts = [
        jnp.einsum("io,orn->irn", cheb_weight[order], grad_out, preferred_element_type=jnp.float32)
        for order in range(nterms)
    ]
    summed = clenshaw(parts, wts)
    input_grad = lax.psum_scatter(summed, "ch", scatter_dimension=0, tiled=True).astype(
        jnp.bfloat16
    )
    return (input_grad, weight_grad)


def solution(mesh):
    return jax.shard_map(
        per_device,
        mesh=mesh,
        in_specs=(
            P(None, "pix", None),
            P("ch", "pix", None),
            P(None, None, "ch"),
            P("pix", None),
            P("pix", None),
            P("pix", None),
        ),
        out_specs=(P("ch", "pix", None), P(None, None, "ch")),
        check_vma=False,
    )
```

profile of v0, /device:TPU:0, one launch (start us, length us, event | category | flops | bytes accessed | tf_op | source)
XLA Modules:
  0.0 588.2 jit_solution(8841968894525062609)
XLA Ops:
  8.8 6.7 %fusion.77 = (bf16[32,32,2048]{2,0,1:T(8,128)(2,1)S(1)}, f32[32,32,2048]{2,0,1:T(8,128)}) fusion(bf16[16,32,2048]{2,1,0:T(8,128)(2,1)S(1)} %copy-done, bf16[4,32,16]{1,2,0:T(8,128)(2,1)} %param.8), kind=kOutput, calls=%fused_computation.109 | convolution fusion | flops 69206016 | bytes 14684160 | tf_op jit(solution)/shard_map/io,orn->irn/dot_general | solution.py:81
  28.9 13.4 %fusion.68 = (f32[32,32,2047]{2,0,1:T(8,128)}, f32[32,32,2047]{2,0,1:T(8,128)}) fusion(f32[32,32,2048]{2,0,1:T(8,128)} %get-tuple-element.41), kind=kLoop, calls=%fused_computation.100 | loop fusion | bytes 33538048 | tf_op jit(solution)/shard_map/slice | solution.py:43
  43.7 5.5 maximum_convert_fusion
  49.1 18.2 %fusion.78 = (bf16[32,32,2048]{2,0,1:T(8,128)(2,1)}, f32[32,32,2048]{2,0,1:T(8,128)}) fusion(f32[32,34,2048]{2,0,1:T(8,128)} %maximum_convert_fusion, f32[32,2048]{1,0:T(8,128)S(1)} %get-tuple-element.35, f32[32,2048]{1,0:T(8,128)S(1)} %get-tuple-element.34, f32[32,32,2047]{2,0,1:T(8,128)} %get-tuple-element.19, f32[32,2048]{1,0:T(8,128)S(1)} %concatenate.65, ...), kind=kOutput, calls=%fused_computation.110 | convolution fusion | flops 90177536 | bytes 49278976 | tf_op jit(solution)/shard_map/io,orn->irn/dot_general | solution.py:81
  69.7 4.2 collective-permute-start.4
  73.9 13.3 %fusion.67 = (f32[32,32,2047]{2,0,1:T(8,128)}, f32[32,32,2047]{2,0,1:T(8,128)}) fusion(f32[32,32,2048]{2,0,1:T(8,128)} %get-tuple-element.43), kind=kLoop, calls=%fused_computation.99 | loop fusion | bytes 33538048 | tf_op jit(solution)/shard_map/slice | solution.py:43
  91.1 19.7 %fusion.79 = (bf16[32,32,2048]{2,0,1:T(8,128)(2,1)S(1)}, f32[32,32,2048]{2,0,1:T(8,128)}) fusion(f32[32,32,2048]{2,0,1:T(8,128)} %get-tuple-element.41, f32[32,34,2048]{2,0,1:T(8,128)} %maximum_convert_fusion.1, f32[32,2048]{1,0:T(8,128)S(1)} %get-tuple-element.35, f32[32,2048]{1,0:T(8,128)S(1)} %get-tuple-element.34, ...), kind=kOutput, calls=%fused_computation.111 | convolution fusion | flops 92274688 | bytes 57667584 | tf_op jit(solution)/shard_map/io,orn->irn/dot_general | solution.py:81
  112.1 4.4 collective-permute-start.6
  116.5 13.4 %fusion.66 = (f32[32,32,2047]{2,0,1:T(8,128)}, f32[32,32,2047]{2,0,1:T(8,128)}) fusion(f32[32,32,2048]{2,0,1:T(8,128)} %get-tuple-element.45), kind=kLoop, calls=%fused_computation.98 | loop fusion | bytes 33538048 | tf_op jit(solution)/shard_map/slice | solution.py:43
  133.8 19.5 %fusion.17 = f32[32,32,2048]{2,0,1:T(8,128)} fusion(f32[32,32,2048]{2,0,1:T(8,128)} %get-tuple-element.43, f32[32,34,2048]{2,0,1:T(8,128)} %maximum_convert_fusion.2, f32[32,32,2047]{2,0,1:T(8,128)} %get-tuple-element.15, f32[32,32,2047]{2,0,1:T(8,128)} %get-tuple-element.14, f32[32,2048]{1,0:T(8,128)S(1)} %get-tuple-element.35, ...), kind=kOutput, calls=%fused_computation.24 | convolution fusion | flops 88080384 | bytes 53473280 | tf_op jit(solution)/shard_map/io,orn->irn/dot_general | solution.py:81
  153.4 5.0 copy_convert_fusion
  159.7 4.5 collective-permute-start.8
  164.2 7.3 %fusion.65 = (f32[32,32,2047]{2,0,1:T(8,128)}, f32[32,32,2047]{2,0,1:T(8,128)}) fusion(f32[32,32,2048]{2,0,1:T(8,128)S(1)} %get-tuple-element.24), kind=kLoop, calls=%fused_computation.97 | loop fusion | bytes 33538048 | tf_op jit(solution)/shard_map/slice | solution.py:43
  171.5 10.0 %convolution_bitcast_fusion.2 = f32[1,32,16]{1,2,0:T(8,128)S(1)} fusion(bf16[16,32,2048]{2,1,0:T(8,128)(2,1)S(1)} %copy-done, bf16[32,32,2048]{2,1,0:T(8,128)(2,1)S(1)} %copy-done.5), kind=kOutput, calls=%fused_computation.52 | convolution fusion | flops 67108864 | bytes 6293504 | tf_op jit(solution)/shard_map/irn,orn->io/dot_general | solution.py:69
  185.4 18.4 %fusion.61 = (bf16[32,32,2048]{2,0,1:T(8,128)(2,1)}, f32[32,32,2048]{2,0,1:T(8,128)}) fusion(f32[32,34,2048]{2,0,1:T(8,128)} %maximum_convert_fusion.3, f32[32,2048]{1,0:T(8,128)S(1)} %get-tuple-element.35, f32[32,2048]{1,0:T(8,128)S(1)} %get-tuple-element.34, f32[32,32,2047]{2,0,1:T(8,128)} %get-tuple-element.13, f32[32,2048]{1,0:T(8,128)S(1)} %concatenate.65, ...), kind=kLoop, calls=%fused_computation.94 | loop fusion | flops 18874368 | bytes 47177728 | tf_op jit(solution)/shard_map/convert_element_type | solution.py:67
  206.1 5.9 %collective-permute-start.10 = (bf16[32,1,2048]{2,0,1:T(8,128)(2,1)S(1)}, bf16[32,1,2048]{2,0,1:T(8,128)(2,1)S(1)}, u32[]{:S(2)}, u32[]{:S(2)}) collective-permute-start(bf16[32,1,2048]{2,0,1:T(8,128)(2,1)S(1)} %get-tuple-element.22), channel_id=1, source_target_pairs={{0,2},{2,4},{4,6},{6,8},{8,10},{10,12},{12,14},{14,16},{16,18},{18... | collective-permute-start | bytes 393224 | tf_op jit(solution)/shard_map/ppermute | solution.py:14
  212.0 13.4 %fusion.64 = (f32[32,32,2047]{2,0,1:T(8,128)}, f32[32,32,2047]{2,0,1:T(8,128)}) fusion(f32[32,32,2048]{2,0,1:T(8,128)} %get-tuple-element.7), kind=kLoop, calls=%fused_computation.96 | loop fusion | bytes 33538048 | tf_op jit(solution)/shard_map/slice | solution.py:43
  228.5 4.0 maximum_convert_fusion.4
  232.5 20.4 %fusion.59 = (bf16[32,32,2048]{2,0,1:T(8,128)(2,1)}, f32[32,32,2048]{2,0,1:T(8,128)}) fusion(bf16[32,32,2048]{2,1,0:T(8,128)(2,1)} %param.6, f32[32,34,2048]{2,0,1:T(8,128)} %maximum_convert_fusion.4, f32[32,2048]{1,0:T(8,128)S(1)} %get-tuple-element.35, f32[32,2048]{1,0:T(8,128)S(1)} %get-tuple-element.34, f32[32,32,2047]{2,0,1:T(8,128)} %get-tuple-element.11, ...), kind=kLoop, calls=%fused_computation.93 | loop fusion | flops 25165824 | bytes 51372032 | tf_op jit(solution)/shard_map/convert_element_type | solution.py:67
  255.2 5.2 collective-permute-start.12
  260.4 13.5 %fusion.63 = (f32[32,32,2047]{2,0,1:T(8,128)}, f32[32,32,2047]{2,0,1:T(8,128)}) fusion(f32[32,32,2048]{2,0,1:T(8,128)} %get-tuple-element.5), kind=kLoop, calls=%fused_computation.95 | loop fusion | bytes 33538048 | tf_op jit(solution)/shard_map/slice | solution.py:43
  277.0 3.9 maximum_convert_fusion.5
  280.9 15.9 %fusion.32 = f32[1,32,16]{1,2,0:T(8,128)S(1)} fusion(f32[32,32,2048]{2,0,1:T(8,128)} %get-tuple-element.7, f32[32,34,2048]{2,0,1:T(8,128)} %maximum_convert_fusion.5, f32[32,32,2047]{2,0,1:T(8,128)} %get-tuple-element.9, f32[32,32,2047]{2,0,1:T(8,128)} %get-tuple-element.8, f32[32,2048]{1,0:T(8,128)S(1)} %get-tuple-element.35, ...), kind=kOutput, calls=%fused_computation.49 | convolution fusion | flops 90177536 | bytes 45090816 | tf_op jit(solution)/shard_map/irn,orn->io/dot_general | solution.py:69
  296.8 278.8 %psum.7 = f32[4,32,16]{1,2,0:T(8,128)S(1)} all-reduce(f32[4,32,16]{1,2,0:T(8,128)S(1)} %pad_maximum_fusion), channel_id=1, replica_groups=mesh['pix'=64,'ch'=2] {'pix'}, use_global_device_ids=true, to_apply=%region_1.2 | all-reduce | flops 2048 | bytes 16384 | tf_op jit(solution)/shard_map/psum | solution.py:79
  (72 shorter events, 49.1 us)
Async XLA Ops:
  7.2 15.9 %copy-start.6 = (s32[32,2048]{1,0:T(8,128)S(1)}, s32[32,2048]{1,0:T(8,128)}, u32[]{:S(2)}) copy-start(s32[32,2048]{1,0:T(8,128)} %param.11) | copy-start | bytes 786436
  7.2 16.0 %copy-start.7 = (f32[32,2048]{1,0:T(8,128)S(1)}, f32[32,2048]{1,0:T(8,128)}, u32[]{:S(2)}) copy-start(f32[32,2048]{1,0:T(8,128)} %param.10) | copy-start | bytes 786436
  7.2 569.0 %reduce-scatter.2.cloned.1.call-start = ((), (), s32[]{:S(2)}) async-start(), calls=%async_computation.1 | async-start | bytes 12582912 | tf_op jit(solution)/shard_map/reduce_scatter | solution.py:85
  15.4 2.0 copy-start.3
  18.1 25.5 %collective-permute-start.3 = (bf16[32,1,2048]{2,0,1:T(8,128)(2,1)}, bf16[32,1,2048]{2,0,1:T(8,128)(2,1)S(1)}, u32[]{:S(2)}, u32[]{:S(2)}) collective-permute-start(bf16[32,1,2048]{2,0,1:T(8,128)(2,1)} %get-tuple-element.33), channel_id=1, source_target_pairs={{2,0},{4,2},{6,4},{8,6},{10,8},{12,10},{14,12},{16,14},{18,16},{20... | collective-permute-start | bytes 393224 | tf_op jit(solution)/shard_map/ppermute | solution.py:15
  19.4 24.2 %collective-permute-start.2 = (bf16[32,1,2048]{2,0,1:T(8,128)(2,1)}, bf16[32,1,2048]{2,0,1:T(8,128)(2,1)}, u32[]{:S(2)}, u32[]{:S(2)}) collective-permute-start(bf16[32,1,2048]{2,0,1:T(8,128)(2,1)} %get-tuple-element.32), channel_id=1, source_target_pairs={{0,2},{2,4},{4,6},{6,8},{8,10},{10,12},{12,14},{14,16},{16,18},{18... | collective-permute-start | bytes 393224 | tf_op jit(solution)/shard_map/ppermute | solution.py:14
  23.8 18.8 %collective-permute-start.1 = (bf16[2,1,2048]{2,1,0:T(2,128)(2,1)}, bf16[2,1,2048]{2,1,0:T(2,128)(2,1)}, u32[]{:S(2)}, u32[]{:S(2)}) collective-permute-start(bf16[2,1,2048]{2,1,0:T(2,128)(2,1)} %get-tuple-element.39), channel_id=1, source_target_pairs={{2,0},{4,2},{6,4},{8,6},{10,8},{12,10},{14,12},{16,14},{18,16},{20... | collective-permute-start | bytes 24584 | tf_op jit(solution)/shard_map/ppermute | solution.py:15
  25.1 17.6 %collective-permute-start = (bf16[2,1,2048]{2,1,0:T(2,128)(2,1)}, bf16[2,1,2048]{2,1,0:T(2,128)(2,1)}, u32[]{:S(2)}, u32[]{:S(2)}) collective-permute-start(bf16[2,1,2048]{2,1,0:T(2,128)(2,1)} %get-tuple-element.38), channel_id=1, source_target_pairs={{0,2},{2,4},{4,6},{6,8},{8,10},{10,12},{12,14},{14,16},{16,18},{18... | collective-permute-start | bytes 24584 | tf_op jit(solution)/shard_map/ppermute | solution.py:14
  28.9 13.5 %copy-start.8 = (f32[32,2048]{1,0:T(8,128)S(1)}, f32[32,2048]{1,0:T(8,128)}, u32[]{:S(2)}) copy-start(f32[32,2048]{1,0:T(8,128)} %param.9) | copy-start | bytes 786436
  42.6 6.5 %copy-start.9 = (bf16[4,32,16]{1,2,0:T(8,128)(2,1)S(1)}, bf16[4,32,16]{1,2,0:T(8,128)(2,1)}, u32[]{:S(2)}) copy-start(bf16[4,32,16]{1,2,0:T(8,128)(2,1)} %param.8) | copy-start | bytes 12292
  68.4 18.9 %collective-permute-start.5 = (bf16[32,1,2048]{2,0,1:T(8,128)(2,1)S(1)}, bf16[32,1,2048]{2,0,1:T(8,128)(2,1)S(1)}, u32[]{:S(2)}, u32[]{:S(2)}) collective-permute-start(bf16[32,1,2048]{2,0,1:T(8,128)(2,1)S(1)} %get-tuple-element.31), channel_id=1, source_target_pairs={{2,0},{4,2},{6,4},{8,6},{10,8},{12,10},{14,12},{16,14},{18,16},{20... | collective-permute-start | bytes 393224 | tf_op jit(solution)/shard_map/ppermute | solution.py:15
  69.7 17.6 %collective-permute-start.4 = (bf16[32,1,2048]{2,0,1:T(8,128)(2,1)S(1)}, bf16[32,1,2048]{2,0,1:T(8,128)(2,1)S(1)}, u32[]{:S(2)}, u32[]{:S(2)}) collective-permute-start(bf16[32,1,2048]{2,0,1:T(8,128)(2,1)S(1)} %get-tuple-element.30), channel_id=1, source_target_pairs={{0,2},{2,4},{4,6},{6,8},{8,10},{10,12},{12,14},{14,16},{16,18},{18... | collective-permute-start | bytes 393224 | tf_op jit(solution)/shard_map/ppermute | solution.py:14
  73.9 13.3 %copy-start.4 = (bf16[32,32,2048]{2,0,1:T(8,128)(2,1)S(1)}, bf16[32,32,2048]{2,0,1:T(8,128)(2,1)}, u32[]{:S(2)}) copy-start(bf16[32,32,2048]{2,0,1:T(8,128)(2,1)} %get-tuple-element.42) | copy-start | bytes 12582916
  110.8 19.2 %collective-permute-start.7 = (bf16[32,1,2048]{2,0,1:T(8,128)(2,1)S(1)}, bf16[32,1,2048]{2,0,1:T(8,128)(2,1)S(1)}, u32[]{:S(2)}, u32[]{:S(2)}) collective-permute-start(bf16[32,1,2048]{2,0,1:T(8,128)(2,1)S(1)} %get-tuple-element.29), channel_id=1, source_target_pairs={{2,0},{4,2},{6,4},{8,6},{10,8},{12,10},{14,12},{16,14},{18,16},{20... | collective-permute-start | bytes 393224 | tf_op jit(solution)/shard_map/ppermute | solution.py:15
  112.1 17.9 %collective-permute-start.6 = (bf16[32,1,2048]{2,0,1:T(8,128)(2,1)S(1)}, bf16[32,1,2048]{2,0,1:T(8,128)(2,1)S(1)}, u32[]{:S(2)}, u32[]{:S(2)}) collective-permute-start(bf16[32,1,2048]{2,0,1:T(8,128)(2,1)S(1)} %get-tuple-element.28), channel_id=1, source_target_pairs={{0,2},{2,4},{4,6},{6,8},{8,10},{10,12},{12,14},{14,16},{16,18},{18... | collective-permute-start | bytes 393224 | tf_op jit(solution)/shard_map/ppermute | solution.py:14
  158.4 23.1 %collective-permute-start.9 = (bf16[32,1,2048]{2,0,1:T(8,128)(2,1)S(1)}, bf16[32,1,2048]{2,0,1:T(8,128)(2,1)S(1)}, u32[]{:S(2)}, u32[]{:S(2)}) collective-permute-start(bf16[32,1,2048]{2,0,1:T(8,128)(2,1)S(1)} %get-tuple-element.27), channel_id=1, source_target_pairs={{2,0},{4,2},{6,4},{8,6},{10,8},{12,10},{14,12},{16,14},{18,16},{20... | collective-permute-start | bytes 393224 | tf_op jit(solution)/shard_map/ppermute | solution.py:15
  159.7 21.8 %collective-permute-start.8 = (bf16[32,1,2048]{2,0,1:T(8,128)(2,1)S(1)}, bf16[32,1,2048]{2,0,1:T(8,128)(2,1)S(1)}, u32[]{:S(2)}, u32[]{:S(2)}) collective-permute-start(bf16[32,1,2048]{2,0,1:T(8,128)(2,1)S(1)} %get-tuple-element.26), channel_id=1, source_target_pairs={{0,2},{2,4},{4,6},{6,8},{8,10},{10,12},{12,14},{14,16},{16,18},{18... | collective-permute-start | bytes 393224 | tf_op jit(solution)/shard_map/ppermute | solution.py:14
  164.2 7.3 %copy-start.5 = (bf16[32,32,2048]{2,1,0:T(8,128)(2,1)S(1)}, bf16[32,32,2048]{2,1,0:T(8,128)(2,1)}, u32[]{:S(2)}) copy-start(bf16[32,32,2048]{2,1,0:T(8,128)(2,1)} %param.6) | copy-start | bytes 12582916
  204.8 23.7 %collective-permute-start.11 = (bf16[32,1,2048]{2,0,1:T(8,128)(2,1)S(1)}, bf16[32,1,2048]{2,0,1:T(8,128)(2,1)S(1)}, u32[]{:S(2)}, u32[]{:S(2)}) collective-permute-start(bf16[32,1,2048]{2,0,1:T(8,128)(2,1)S(1)} %get-tuple-element.23), channel_id=1, source_target_pairs={{2,0},{4,2},{6,4},{8,6},{10,8},{12,10},{14,12},{16,14},{18,16},{20... | collective-permute-start | bytes 393224 | tf_op jit(solution)/shard_map/ppermute | solution.py:15
  206.1 22.4 %collective-permute-start.10 = (bf16[32,1,2048]{2,0,1:T(8,128)(2,1)S(1)}, bf16[32,1,2048]{2,0,1:T(8,128)(2,1)S(1)}, u32[]{:S(2)}, u32[]{:S(2)}) collective-permute-start(bf16[32,1,2048]{2,0,1:T(8,128)(2,1)S(1)} %get-tuple-element.22), channel_id=1, source_target_pairs={{0,2},{2,4},{4,6},{6,8},{8,10},{10,12},{12,14},{14,16},{16,18},{18... | collective-permute-start | bytes 393224 | tf_op jit(solution)/shard_map/ppermute | solution.py:14
  212.0 13.4 %copy-start.1 = (bf16[32,32,2048]{2,0,1:T(8,128)(2,1)S(1)}, bf16[32,32,2048]{2,0,1:T(8,128)(2,1)}, u32[]{:S(2)}) copy-start(bf16[32,32,2048]{2,0,1:T(8,128)(2,1)} %get-tuple-element.6) | copy-start | bytes 12582916
  253.9 23.1 %collective-permute-start.13 = (bf16[32,1,2048]{2,0,1:T(8,128)(2,1)S(1)}, bf16[32,1,2048]{2,0,1:T(8,128)(2,1)S(1)}, u32[]{:S(2)}, u32[]{:S(2)}) collective-permute-start(bf16[32,1,2048]{2,0,1:T(8,128)(2,1)S(1)} %get-tuple-element.21), channel_id=1, source_target_pairs={{2,0},{4,2},{6,4},{8,6},{10,8},{12,10},{14,12},{16,14},{18,16},{20... | collective-permute-start | bytes 393224 | tf_op jit(solution)/shard_map/ppermute | solution.py:15
  255.2 21.9 %collective-permute-start.12 = (bf16[32,1,2048]{2,0,1:T(8,128)(2,1)S(1)}, bf16[32,1,2048]{2,0,1:T(8,128)(2,1)S(1)}, u32[]{:S(2)}, u32[]{:S(2)}) collective-permute-start(bf16[32,1,2048]{2,0,1:T(8,128)(2,1)S(1)} %get-tuple-element.20), channel_id=1, source_target_pairs={{0,2},{2,4},{4,6},{6,8},{8,10},{10,12},{12,14},{14,16},{16,18},{18... | collective-permute-start | bytes 393224 | tf_op jit(solution)/shard_map/ppermute | solution.py:14
  260.4 13.5 %copy-start.2 = (bf16[32,32,2048]{2,0,1:T(8,128)(2,1)S(1)}, bf16[32,32,2048]{2,0,1:T(8,128)(2,1)}, u32[]{:S(2)}) copy-start(bf16[32,32,2048]{2,0,1:T(8,128)(2,1)} %get-tuple-element.4) | copy-start | bytes 12582916
  (1 other events, 1.6 us)
Sparse Core Ops, SparseCore 0:
  153.5 124.3 reduce-scatter.1
where the time goes:
time: 595 us; the launch traced here: 588 us
  blocking collectives  279 us (47%)
  matrix products  96.2 us (16%)
  local copies, waits for them, and re-layouts  84.3 us (14%)
  other arithmetic  73.4 us (12%)
  starting transfers between devices  40.9 us (7%)
  between operations  14.6 us (2%)
    psum x1, blocking collectives, per_device(): lax.psum(local_grad, 'pix') / jnp.sqrt(jnp.float32(total_pixels))  279 us
    slice x6, local copies, waits for them, and re-layouts, operate(): right = jnp.concatenate([field[:, :, 1:], zcol], axis=2)  74.3 us
    dot_general x4, matrix products, per_device(): jnp.einsum('io,orn->irn', cheb_weight[order], grad_out, preferred_element...  64.1 us
    convert_element_type x2, other arithmetic, forward_grads(): term_b = term_now.astype(jnp.bfloat16)  38.8 us
    dot_general x4, matrix products, forward_grads(): jnp.einsum('irn,orn->io', term_b, cotangent, preferred_element_type=jnp.f...  32 us
    ppermute x7, starting transfers between devices, padded_2(): before = lax.ppermute(last, axis, up)  31.8 us
    convert_element_type x6, other arithmetic, operate(): padded_2(field.astype(jnp.bfloat16), (('pix', 1),), 1).astype(field.dtype)  24.9 us
  transfers between devices with their start and end apart: 15, of which 0 were waited for; matrix products, arithmetic and copies ran while one was open for 28% of the time, Pallas kernels for 0%

commit v1 on v0

v1 whole, which is shorter than its diff:
```python
import functools

import jax
import jax.numpy as jnp
from jax import lax
from jax.experimental import pallas as pl
from jax.experimental.pallas import tpu as pltpu
from jax.sharding import PartitionSpec as P

HALO = 4
SIDE = 128
SUB = 16
TILE = 8
INNER = (512, 1536)
OUTER = (1024, 1024)
UNIT = 256
ANY = pl.BlockSpec(memory_space=pl.ANY)
HBM = pl.BlockSpec(memory_space=pltpu.HBM)
VMEM = pl.BlockSpec(memory_space=pltpu.VMEM)
F32, BF16 = jnp.float32, jnp.bfloat16


def params(mib):
    return pltpu.CompilerParams(vmem_limit_bytes=mib * 1024 * 1024)


COST = pl.CostEstimate(flops=1, bytes_accessed=1, transcendentals=0)
LONG = pl.CostEstimate(flops=10**10, bytes_accessed=10**8, transcendentals=0)


def iota(shape, dim):
    return lax.broadcasted_iota(jnp.int32, shape, dim)


def prepare_kernel(
    sides, w_hbm, g_ref, east_ref, south_ref, mask_ref,
    mix_ref, g_out, maps_out, top_ref, bottom_ref, mask_buf, w_ref, sems,
):
    copies = [
        pltpu.make_async_copy(src, dst, sems.at[n])
        for n, (src, dst) in enumerate((
            (w_hbm, w_ref), (mask_ref, mask_buf), (east_ref, maps_out.at[0]),
            (south_ref, maps_out.at[1]), (g_ref, g_out),
        ))
    ]
    for c in copies:
        c.start()
    copies[0].wait()
    nterms, nout, nin = w_ref.shape
    rows, cols = nin * SUB, nout * SUB
    part = nin // sides
    first = (lax.axis_index("ch") + 1) * part
    source = lax.rem(iota((rows, nin), 0) // SUB + first, nin)
    left = (source == iota((rows, nin), 1)).astype(BF16)
    right = (iota((nout, cols), 0) == iota((nout, cols), 1) // SUB).astype(BF16)
    keep = iota((rows, cols), 0) % SUB == iota((rows, cols), 1) % SUB
    for k in range(nterms):
        tall = lax.dot_general(
            left, w_ref[k], (((1,), (1,)), ((), ())), preferred_element_type=F32
        ).astype(BF16)
        full = jnp.dot(tall, right, preferred_element_type=F32)
        mix_ref[:, k * cols : (k + 1) * cols] = jnp.where(keep, full, 0.0).astype(BF16)
    for c in copies[1:4]:
        c.wait()
    mask = mask_buf[...].astype(F32)
    height, total = mask.shape
    east = -2.0 * maps_out[0] * mask * pltpu.roll(mask, total - 1, 1)
    maps_out[0] = jnp.where(iota(mask.shape, 1) == total - 1, 0.0, east)
    maps_out[2] = mask
    copies[4].wait()
    nch = g_out.shape[0]
    for o in range(nch + 3):
        x = g_out[o].astype(F32) if o < nch else maps_out[o - nch]
        top_ref[o] = x[:HALO].astype(BF16)
        bottom_ref[o] = x[height - TILE :][TILE - HALO :].astype(BF16)


def prepare(w, g, east, south, mask, sides):
    nterms, nin, nout = w.shape
    nch, rows, total = g.shape
    edge = jax.ShapeDtypeStruct((nch + 3, HALO, total), BF16)
    args = (w.transpose(0, 2, 1), g, east, south, mask)
    return pl.pallas_call(
        functools.partial(prepare_kernel, sides),
        out_shape=(
            jax.ShapeDtypeStruct((nin * SUB, nterms * nout * SUB), BF16),
            jax.ShapeDtypeStruct(g.shape, g.dtype),
            jax.ShapeDtypeStruct((3, rows, total), F32),
            edge,
            edge,
        ),
        in_specs=[HBM] * 5,
        out_specs=[VMEM] * 5,
        scratch_shapes=[
            pltpu.VMEM((rows, total), jnp.int32),
            pltpu.VMEM((nterms, nout, nin), BF16),
            pltpu.SemaphoreType.DMA((5,)),
        ],
        compiler_params=params(12),
        cost_estimate=COST,
    )(*(pltpu.with_memory_space_constraint(x, pltpu.HBM) for x in args))


def inner_rows(x):
    rows = x.shape[0]
    low = iota((TILE, x.shape[1]), 0) < HALO
    return jnp.concatenate(
        [x[TILE : rows - TILE], jnp.where(low, x[rows - TILE :], x[:TILE])], axis=0
    )


def outer_rows(x, below, above):
    rows = x.shape[0]
    low = iota((TILE, x.shape[1]), 0) < HALO
    return jnp.concatenate(
        [
            x[rows - TILE :], below, above, x[:TILE],
            jnp.where(low, x[TILE : 2 * TILE], x[rows - 2 * TILE : rows - TILE]),
        ],
        axis=0,
    )


def terms_kernel(outer, off, lo, hi, nterms, waits, *refs):
    g_ref, maps_ref, mix_ref = refs[waits : waits + 3]
    below_ref, above_ref = refs[waits + 3 : waits + 5] if outer else (None, None)
    terms_ref, send_ref, w_buf = refs[-3:]
    nch = g_ref.shape[0]
    ext, span = w_buf.shape[1:]
    width = terms_ref.shape[2]
    cols = slice(lo, hi)

    def arrange(x, n):
        x = x.astype(F32)
        if outer:
            below, above = below_ref[n, :, cols], above_ref[n, :, cols]
            return outer_rows(x, below.astype(F32), above.astype(F32))
        return inner_rows(x)

    ew = arrange(maps_ref[0, :, cols], nch)
    south = arrange(maps_ref[1, :, cols], nch + 1)
    mask = arrange(maps_ref[2, :, cols], nch + 2)
    row, col = iota((ext, span), 0), iota((ext, span), 1)
    ww = pltpu.roll(ew, 1, 1)
    if lo == 0:
        ww = jnp.where(col == 0, 0.0, ww)
    sw = -2.0 * south * mask * pltpu.roll(mask, ext - 1, 0)
    for gap in (TILE + HALO - 1, 3 * TILE + HALO - 1) if outer else (ext - HALO - 1,):
        sw = jnp.where(row == gap, 0.0, sw)
    w_buf[0] = ew
    w_buf[1] = ww
    w_buf[2] = sw
    w_buf[3] = pltpu.roll(sw, 1, 0)

    def twice(fields, rounded):
        east, west, south, north = (w_buf[n] for n in range(4))
        out = []
        for v, b in zip(fields, rounded):
            right = pltpu.roll(b, span - 1, 1).astype(F32)
            left = pltpu.roll(b, 1, 1).astype(F32)
            out.append(
                (east * right + west * left)
                + (south * pltpu.roll(v, ext - 1, 0) + north * pltpu.roll(v, 1, 0))
            )
        return out

    def keep(v):
        v = v[:, off : off + width]
        if outer:
            v = jnp.concatenate([v[:TILE], v[2 * TILE : 3 * TILE]], axis=0)
        return v[:SUB].astype(BF16)

    group = 4

    def channels(step, carry):
        chans = [step * group + n for n in range(group)]
        now = [arrange(g_ref[o, :, cols], o) for o in chans]
        prev = None
        for k in range(nterms):
            if k > 0:
                new = twice(now, rounded)
                new = [0.5 * x for x in new] if k == 1 else [x - p for x, p in zip(new, prev)]
                prev, now = now, new
            rounded = [x.astype(BF16) for x in now]
            for o, x in zip(chans, now):
                terms_ref[k * nch + o] = keep(x)
        return carry

    lax.fori_loop(0, nch // group, channels, 0)
    for c in range(0, width, 256):
        x = terms_ref[:, :, c : c + 256].reshape(nterms * nch * SUB, 256)
        y = jnp.dot(mix_ref[: send_ref.shape[0] * SUB], x, preferred_element_type=F32)
        send_ref[:, :, c : c + 256] = y.astype(BF16).reshape(-1, SUB, 256)


def chunk_terms(outer, start, width, g, maps, mix, sent, nterms, beside, waits, cost):
    nch, rows, total = g.shape
    lo, hi = max(0, start - SIDE), min(total, start + width + SIDE)
    ext = 4 * TILE if outer else 3 * TILE
    return pl.pallas_call(
        functools.partial(terms_kernel, outer, start - lo, lo, hi, nterms, len(waits)),
        out_shape=(
            jax.ShapeDtypeStruct((nterms * nch, SUB, width), BF16),
            jax.ShapeDtypeStruct((sent, SUB, width), BF16),
        ),
        in_specs=[ANY] * len(waits) + [VMEM] * (3 + len(beside)),
        out_specs=(VMEM, VMEM),
        scratch_shapes=[pltpu.VMEM((4, ext, hi - lo), F32)],
        compiler_params=params(20),
        cost_estimate=cost,
    )(*waits, g, maps, mix, *beside)


def weights_kernel(places, f_ref, *refs):
    n = len(places)
    terms, (grad_ref, acc) = refs[:n], refs[n:]
    nt = terms[0].shape[0]
    nin, rows, _ = f_ref.shape
    for m, ((outer, start, width), t_ref) in enumerate(zip(places, terms)):
        x = t_ref[...].reshape(nt * SUB, width)
        f = f_ref[:, :, start : start + width].astype(F32)
        if outer:
            f = jnp.concatenate([f[:, rows - TILE :], f[:, :TILE]], axis=1)
        else:
            f = f[:, TILE : rows - TILE]
        f = f.astype(BF16).reshape(nin * SUB, width)
        y = lax.dot_general(x, f, (((1,), (1,)), ((), ())), preferred_element_type=F32)
        if m == 0:
            acc[...] = y
        else:
            acc[...] += y
    r, c = iota((SUB, nin * SUB), 0), iota((SUB, nin * SUB), 1)
    same = (c % SUB == r).astype(F32)
    kept = jnp.sum(acc[...].reshape(nt, SUB, nin * SUB) * same[None], axis=1)
    pick = (iota((nin * SUB, nin), 0) // SUB == iota((nin * SUB, nin), 1)).astype(F32)
    grad_ref[...] = jnp.dot(
        kept, pick, preferred_element_type=F32, precision=lax.Precision.HIGHEST
    )


def weights(places, terms, f):
    nt = terms[0].shape[0]
    nin = f.shape[0]
    return pl.pallas_call(
        functools.partial(weights_kernel, places),
        out_shape=jax.ShapeDtypeStruct((nt, nin), F32),
        in_specs=[VMEM] * (1 + len(terms)),
        out_specs=VMEM,
        scratch_shapes=[pltpu.VMEM((nt * SUB, nin * SUB), F32)],
        compiler_params=params(36),
        cost_estimate=COST,
    )(f, *terms)


def finish_kernel(mix_ref, terms_i, got_i, terms_o, got_o, *refs):
    out = []
    for terms, got in ((terms_i, got_i), (terms_o, got_o)):
        x = terms[...].reshape(-1, UNIT)
        own = jnp.dot(mix_ref[...], x, preferred_element_type=F32)
        out.append(own.reshape(got.shape) + got[...].astype(F32))
    inner, outer = out
    refs[-1][...] = jnp.concatenate([outer[:, TILE:], inner, outer[:, :TILE]], axis=1).astype(BF16)


def finish(start, width, mix, inner, outer, out, rows, total):
    kept = outer[2].shape[0]
    nt = outer[1].shape[0]
    extra = () if out is None else (out,)
    last = mix.shape[0] // (kept * SUB) - 1

    def blocks(piece):
        def index(j):
            return (0, 0, j + (start - piece[0]) // UNIT)

        return [pl.BlockSpec((n, SUB, UNIT), index) for n in (nt, kept)]

    return pl.pallas_call(
        finish_kernel,
        grid=(width // UNIT,),
        out_shape=jax.ShapeDtypeStruct((kept, rows, total), BF16),
        in_specs=[pl.BlockSpec((kept * SUB, mix.shape[1]), lambda j: (last, 0))]
        + blocks(inner)
        + blocks(outer)
        + [ANY] * len(extra),
        out_specs=pl.BlockSpec((kept, rows, UNIT), lambda j: (0, 0, j + start // UNIT)),
        input_output_aliases={5: 0} if extra else {},
        compiler_params=params(16),
        cost_estimate=COST,
    )(mix, *inner[1:], *outer[1:], *extra)


def add_kernel(count, *refs):
    values = [r[...] for r in refs[:count]]
    while len(values) > 1:
        values = [a + b for a, b in zip(values[::2], values[1::2])]
    refs[-1][...] = values[0]


def add(values, waits):
    return pl.pallas_call(
        functools.partial(add_kernel, len(values)),
        out_shape=jax.ShapeDtypeStruct(values[0].shape, F32),
        in_specs=[VMEM] * len(values) + [ANY] * len(waits),
        out_specs=VMEM,
        compiler_params=params(4),
        cost_estimate=COST,
    )(*values, *waits)


def sum_over_pix(value, size, waits):
    steps, step = [], 1
    while step < size:
        steps.append((step, 4 if step * 2 < size else 2))
        step *= steps[-1][1]
    value = add([value], waits[0])
    for n, (step, count) in enumerate(steps[1:] + steps[:1]):
        moved = [
            lax.ppermute(value, "pix", [(i, i ^ (x * step)) for i in range(size)])
            for x in range(1, count)
        ]
        value = add([value, *moved], waits[n + 1] if n + 1 < len(waits) else ())
    return value


def per_device(features, grad_out, cheb_weight, east_weight, south_weight, pixel_mask):
    nch, rows, total = grad_out.shape
    nterms, nin, _ = cheb_weight.shape
    size, sides = lax.axis_size("pix"), lax.axis_size("ch")
    part = nin // sides
    mix, g, maps, top, bottom = prepare(
        cheb_weight, grad_out, east_weight, south_weight, pixel_mask, sides
    )
    pieces = []

    def chunks(outer, widths, beside):
        start = 0
        for width in widths:
            waits = [pieces[-1][1]] if pieces else []
            waits += [pieces[0][2]] if outer and not start else []
            cost = LONG if outer and not start else COST
            terms, send = chunk_terms(
                outer, start, width, g, maps, mix, part, nterms, beside, waits, cost
            )
            got = lax.ppermute(send, "ch", [(i, i ^ 1) for i in range(sides)])
            pieces.append(((outer, start, width), terms, got))
            start += width

    chunks(False, INNER, ())
    down = [(i, i + 1) for i in range(size - 1) if (i + 1) * rows % total]
    up = [(j, i) for i, j in down]
    chunks(True, OUTER, (lax.ppermute(top, "pix", up), lax.ppermute(bottom, "pix", down)))

    grad = weights([p[0] for p in pieces], [p[1] for p in pieces], features)
    pixels = rows * size * total
    arrived = [got for _, _, got in pieces]
    n = len(INNER)
    grad = sum_over_pix(grad, size, (arrived[:n], arrived[n:-1])) / jnp.sqrt(F32(pixels))
    weight_grad = grad.reshape(nterms, nch, nin).transpose(0, 2, 1)
    out = None
    for (_, at, width), outer_terms, outer_got in pieces[n:]:
        for (_, first, span), inner_terms, inner_got in pieces[:n]:
            lo, hi = max(at, first), min(at + width, first + span)
            if lo < hi:
                inner = (first, inner_terms, inner_got)
                outer = (at, outer_terms, outer_got)
                out = finish(lo, hi - lo, mix, inner, outer, out, rows, total)
    return out, weight_grad


def solution(mesh):
    return jax.shard_map(
        per_device,
        mesh=mesh,
        in_specs=(
            P(None, "pix", None),
            P("ch", "pix", None),
            P(None, None, "ch"),
            P("pix", None),
            P("pix", None),
            P("pix", None),
        ),
        out_specs=(P("ch", "pix", None), P(None, None, "ch")),
        check_vma=False,
    )
```

time: 595 us -> 73.9 us (0.12)
  the two profiles are of different devices: /device:TPU:0 before, /device:TPU:1 now
where the time goes in v1:
time: 73.9 us; the launch traced here: 73.7 us
  Pallas kernels  30.1 us (41%)
  starting transfers between devices  25.4 us (34%)
  waiting for transfers between devices  16.7 us (23%)
  between operations  0.77 us (1%)
    pallas_call x4, Pallas kernels, chunk_terms(): pl.pallas_call(functools.partial(terms_kernel, outer, start - lo, lo, hi,...  16.3 us
    ppermute x9, starting transfers between devices, sum_over_pix(): lax.ppermute(value, 'pix', [(i, i ^ x * step) for i in range(size)])  12.7 us
    ppermute x4, waiting for transfers between devices, chunks(): got = lax.ppermute(send, 'ch', [(i, i ^ 1) for i in range(sides)])  12.5 us
    pallas_call x3, Pallas kernels, finish(): pl.pallas_call(finish_kernel, grid=(width // UNIT,), out_shape=jax.ShapeD...  6.93 us
    ppermute x4, starting transfers between devices, chunks(): got = lax.ppermute(send, 'ch', [(i, i ^ 1) for i in range(sides)])  6.24 us
    pallas_call x1, Pallas kernels, weights(): pl.pallas_call(functools.partial(weights_kernel, places), out_shape=jax.S...  4.87 us
    ppermute x9, waiting for transfers between devices, sum_over_pix(): lax.ppermute(value, 'pix', [(i, i ^ x * step) for i in range(size)])  4.24 us
    ppermute x1, starting transfers between devices, per_device(): lax.ppermute(top, 'pix', up)  3.33 us
  transfers between devices with their start and end apart: 15, of which 8 were waited for; matrix products, arithmetic and copies ran while one was open for 0% of the time, Pallas kernels for 38%

profile of v1, /device:TPU:1, one launch (start us, length us, event | category | flops | bytes accessed | tf_op | source)
XLA Modules:
  0.0 73.7 jit_solution(2779876434103432758)
XLA Ops:
  0.6 2.0 %shard_map.77 = (bf16[512,1024]{1,0:T(8,128)(2,1)S(1)}, bf16[16,32,2048]{2,1,0:T(8,128)(2,1)S(1)}, f32[3,32,2048]{2,1,0:T(8,128)S(1)}, bf16[19,4,2048]{2,1,0:T(4,128)(2,1)S(1)}, bf16[19,4,2048]{2,1,0:T(4,128)(2,1)S(1)}) custom-call(bf16[4,16,32]{2,1,0:T(8,128)(2,1)} %bitcast.5, bf16[16,32,2048]{2,1,0:T(8,128)(2,1)} %g_ref.1, f32[32,2048]{1,0:T(8,128)} %east_ref.1, ...), custom_call_target="tpu_custom_call" | custom-call | flops 1 | bytes 1 | tf_op jit(solution)/shard_map/pallas_call | solution.py:83
  2.7 3.3 %collective-permute-start.2 = (bf16[19,4,2048]{2,1,0:T(4,128)(2,1)S(1)}, bf16[19,4,2048]{2,1,0:T(4,128)(2,1)S(1)}, u32[]{:S(2)}, u32[]{:S(2)}) collective-permute-start(bf16[19,4,2048]{2,1,0:T(4,128)(2,1)S(1)} %get-tuple-element.22), channel_id=1, source_target_pairs={{2,0},{4,2},{6,4},{8,6},{10,8},{12,10},{14,12},{16,14},{18,16},{20... | collective-permute-start | bytes 933896 | tf_op jit(solution)/shard_map/ppermute | solution.py:351
  6.0 3.2 %collective-permute-start.3 = (bf16[19,4,2048]{2,1,0:T(4,128)(2,1)S(1)}, bf16[19,4,2048]{2,1,0:T(4,128)(2,1)S(1)}, u32[]{:S(2)}, u32[]{:S(2)}) collective-permute-start(bf16[19,4,2048]{2,1,0:T(4,128)(2,1)S(1)} %get-tuple-element.23), channel_id=1, source_target_pairs={{0,2},{2,4},{4,6},{6,8},{8,10},{10,12},{12,14},{14,16},{16,18},{18... | collective-permute-start | bytes 933896 | tf_op jit(solution)/shard_map/ppermute | solution.py:351
  9.2 2.1 %shard_map.78 = (bf16[64,16,512]{2,1,0:T(8,128)(2,1)S(1)}, bf16[16,16,512]{2,1,0:T(8,128)(2,1)S(1)}) custom-call(bf16[16,32,2048]{2,1,0:T(8,128)(2,1)S(1)} %get-tuple-element.16.refs_0_.refs_1_.refs_2_, f32[3,32,2048]{2,1,0:T(8,128)S(1)} %get-tuple-element.17.refs_1_.refs_2_.refs_3_, bf16[512,1024]{1,0:T(8,128)(2,1)S(1)} %get-tuple-element.15.refs_2_.refs_3_.refs_4_.mix_ref), custom_call_target="tpu_custom_call" | custom-call | flops 1 | bytes 1 | tf_op jit(solution)/shard_map/pallas_call | solution.py:200
  11.3 2.9 %collective-permute-start.1 = (bf16[16,16,512]{2,1,0:T(8,128)(2,1)S(1)}, bf16[16,16,512]{2,1,0:T(8,128)(2,1)S(1)}, u32[]{:S(2)}, u32[]{:S(2)}) collective-permute-start(bf16[16,16,512]{2,1,0:T(8,128)(2,1)S(1)} %get-tuple-element.21), channel_id=1, source_target_pairs={{0,1},{1,0},{2,3},{3,2},{4,5},{5,4},{6,7},{7,6},{8,9},{9,8},{10,11... | collective-permute-start | bytes 786440 | tf_op jit(solution)/shard_map/ppermute | solution.py:344
  14.1 5.3 %shard_map.79 = (bf16[64,16,1536]{2,1,0:T(8,128)(2,1)S(1)}, bf16[16,16,1536]{2,1,0:T(8,128)(2,1)S(1)}) custom-call(bf16[64,16,512]{2,1,0:T(8,128)(2,1)S(1)} %get-tuple-element.18.refs_0_.terms_i, bf16[16,32,2048]{2,1,0:T(8,128)(2,1)S(1)} %get-tuple-element.16.refs_0_.refs_1_.refs_2_, f32[3,32,2048]{2,1,0:T(8,128)S(1)} %get-tuple-element.17.refs_1_.refs_2_.refs_3_, ...), custom_call_target="tpu_custom_call" | custom-call | flops 1 | bytes 1 | tf_op jit(solution)/shard_map/pallas_call | solution.py:200
  19.7 7.0 %collective-permute-done.1.refs_1_.got_i = bf16[16,16,512]{2,1,0:T(8,128)(2,1)S(1)} collective-permute-done((bf16[16,16,512]{2,1,0:T(8,128)(2,1)S(1)}, bf16[16,16,512]{2,1,0:T(8,128)(2,1)S(1)}, u32[]{:S(2)}, u32[]{:S(2)}) %collective-permute-start.1) | collective-permute-done | bytes 262176 | tf_op jit(solution)/shard_map/ppermute | solution.py:344
  26.7 4.5 %shard_map.80 = (bf16[64,16,1024]{2,1,0:T(8,128)(2,1)S(1)}, bf16[16,16,1024]{2,1,0:T(8,128)(2,1)S(1)}) custom-call(bf16[64,16,1536]{2,1,0:T(8,128)(2,1)S(1)} %get-tuple-element.19.refs_0_.terms_i.refs_1_, bf16[16,16,512]{2,1,0:T(8,128)(2,1)S(1)} %collective-permute-done.1.refs_1_.got_i, bf16[16,32,2048]{2,1,0:T(8,128)(2,1)S(1)} %get-tuple-element.16.refs_0_.refs_1_.refs_2_, ...), custom_call_target="tpu_custom_call" | custom-call | flops 10000000000 | bytes 100000000 | tf_op jit(solution)/shard_map/pallas_call | solution.py:200
  31.3 4.5 %shard_map.81 = (bf16[64,16,1024]{2,1,0:T(8,128)(2,1)S(1)}, bf16[16,16,1024]{2,1,0:T(8,128)(2,1)S(1)}) custom-call(bf16[64,16,1024]{2,1,0:T(8,128)(2,1)S(1)} %get-tuple-element.24.refs_0_.terms_o.refs_2_, bf16[16,32,2048]{2,1,0:T(8,128)(2,1)S(1)} %get-tuple-element.16.refs_0_.refs_1_.refs_2_, f32[3,32,2048]{2,1,0:T(8,128)S(1)} %get-tuple-element.17.refs_1_.refs_2_.refs_3_, ...), custom_call_target="tpu_custom_call" | custom-call | flops 1 | bytes 1 | tf_op jit(solution)/shard_map/pallas_call | solution.py:200
  35.8 3.0 %collective-permute-start.4 = (bf16[16,16,1024]{2,1,0:T(8,128)(2,1)S(1)}, bf16[16,16,1024]{2,1,0:T(8,128)(2,1)S(1)}, u32[]{:S(2)}, u32[]{:S(2)}) collective-permute-start(bf16[16,16,1024]{2,1,0:T(8,128)(2,1)S(1)} %get-tuple-element.26), channel_id=1, source_target_pairs={{0,1},{1,0},{2,3},{3,2},{4,5},{5,4},{6,7},{7,6},{8,9},{9,8},{10,11... | collective-permute-start | bytes 1572872 | tf_op jit(solution)/shard_map/ppermute | solution.py:344
  38.8 4.9 %shard_map.85.refs_0_ = f32[64,32]{1,0:T(8,128)S(1)} custom-call(bf16[32,32,2048]{2,1,0:T(8,128)(2,1)S(1)} %copy-done, bf16[64,16,512]{2,1,0:T(8,128)(2,1)S(1)} %get-tuple-element.18.refs_0_.terms_i, bf16[64,16,1536]{2,1,0:T(8,128)(2,1)S(1)} %get-tuple-element.19.refs_0_.terms_i.refs_1_, bf16[64,16,1024]{2,1,0:T(8,128)(2,1)S(1)} %get-tuple-element.24.refs_0_.terms_o.refs_2_, ...), custom_call_target="tpu_custom_call" | custom-call | flops 1 | bytes 1 | tf_op jit(solution)/shard_map/pallas_call | solution.py:244
  44.1 3.0 %collective-permute-start.6 = (f32[64,32]{1,0:T(8,128)S(1)}, f32[64,32]{1,0:T(8,128)S(1)}, u32[]{:S(2)}, u32[]{:S(2)}) collective-permute-start(f32[64,32]{1,0:T(8,128)S(1)} %shard_map.86.refs_0_), channel_id=1, source_target_pairs={{0,8},{2,10},{4,12},{6,14},{8,0},{10,2},{12,4},{14,6},{16,24},{18,... | collective-permute-start | bytes 24584 | tf_op jit(solution)/shard_map/ppermute | solution.py:318
  47.1 1.0 %collective-permute-done.8.refs_3_ = f32[64,32]{1,0:T(8,128)S(1)} collective-permute-done((f32[64,32]{1,0:T(8,128)S(1)}, f32[64,32]{1,0:T(8,128)S(1)}, u32[]{:S(2)}, u32[]{:S(2)}) %collective-permute-start.8) | collective-permute-done | bytes 8224 | tf_op jit(solution)/shard_map/ppermute | solution.py:318
  48.1 0.6 collective-permute-done.7.refs_2_
  48.6 0.7 collective-permute-done.6.refs_1_
  49.3 5.4 %collective-permute-done.5.got_o.refs_4_ = bf16[16,16,1024]{2,1,0:T(8,128)(2,1)S(1)} collective-permute-done((bf16[16,16,1024]{2,1,0:T(8,128)(2,1)S(1)}, bf16[16,16,1024]{2,1,0:T(8,128)(2,1)S(1)}, u32[]{:S(2)}, u32[]{:S(2)}) %collective-permute-start.5) | collective-permute-done | bytes 524320 | tf_op jit(solution)/shard_map/ppermute | solution.py:344
  55.0 3.1 %collective-permute-start.9 = (f32[64,32]{1,0:T(8,128)S(1)}, f32[64,32]{1,0:T(8,128)S(1)}, u32[]{:S(2)}, u32[]{:S(2)}) collective-permute-start(f32[64,32]{1,0:T(8,128)S(1)} %shard_map.87.refs_0_), channel_id=1, source_target_pairs={{0,32},{2,34},{4,36},{6,38},{8,40},{10,42},{12,44},{14,46},{16,48}... | collective-permute-start | bytes 24584 | tf_op jit(solution)/shard_map/ppermute | solution.py:318
  58.1 1.0 %collective-permute-done.11.refs_3_ = f32[64,32]{1,0:T(8,128)S(1)} collective-permute-done((f32[64,32]{1,0:T(8,128)S(1)}, f32[64,32]{1,0:T(8,128)S(1)}, u32[]{:S(2)}, u32[]{:S(2)}) %collective-permute-start.11) | collective-permute-done | bytes 8224 | tf_op jit(solution)/shard_map/ppermute | solution.py:318
  60.1 1.3 %collective-permute-start.14 = (f32[64,32]{1,0:T(8,128)S(1)}, f32[64,32]{1,0:T(8,128)S(1)}, u32[]{:S(2)}, u32[]{:S(2)}) collective-permute-start(f32[64,32]{1,0:T(8,128)S(1)} %shard_map.88.refs_0_), channel_id=1, source_target_pairs={{0,6},{2,4},{4,2},{6,0},{8,14},{10,12},{12,10},{14,8},{16,22},{18,... | collective-permute-start | bytes 24584 | tf_op jit(solution)/shard_map/ppermute | solution.py:318
  61.4 4.7 %collective-permute-start.13 = (f32[64,32]{1,0:T(8,128)S(1)}, f32[64,32]{1,0:T(8,128)S(1)}, u32[]{:S(2)}, u32[]{:S(2)}) collective-permute-start(f32[64,32]{1,0:T(8,128)S(1)} %shard_map.88.refs_0_), channel_id=1, source_target_pairs={{0,4},{2,6},{4,0},{6,2},{8,12},{10,14},{12,8},{14,10},{16,20},{18,... | collective-permute-start | bytes 24584 | tf_op jit(solution)/shard_map/ppermute | solution.py:318
  66.1 1.9 %shard_map.82.refs_0_ = bf16[16,32,2048]{2,1,0:T(8,128)(2,1)} custom-call(bf16[512,1024]{1,0:T(8,128)(2,1)S(1)} %get-tuple-element.15.refs_2_.refs_3_.refs_4_.mix_ref, bf16[64,16,512]{2,1,0:T(8,128)(2,1)S(1)} %get-tuple-element.18.refs_0_.terms_i, bf16[16,16,512]{2,1,0:T(8,128)(2,1)S(1)} %collective-permute-done.1.refs_1_.got_i, ...), custom_call_target="tpu_custom_call" | custom-call | flops 1 | bytes 1 | tf_op jit(solution)/shard_map/pallas_call | solution.py:277
  68.0 1.9 %shard_map.83.refs_0_ = bf16[16,32,2048]{2,1,0:T(8,128)(2,1)} custom-call(bf16[512,1024]{1,0:T(8,128)(2,1)S(1)} %get-tuple-element.15.refs_2_.refs_3_.refs_4_.mix_ref, bf16[64,16,1536]{2,1,0:T(8,128)(2,1)S(1)} %get-tuple-element.19.refs_0_.terms_i.refs_1_, ...), custom_call_target="tpu_custom_call", output_to_operand_aliasing={{}: (5, {})} | custom-call | flops 1 | bytes 1 | tf_op jit(solution)/shard_map/pallas_call | solution.py:277
  69.9 3.2 %shard_map.84 = bf16[16,32,2048]{2,1,0:T(8,128)(2,1)} custom-call(bf16[512,1024]{1,0:T(8,128)(2,1)S(1)} %get-tuple-element.15.refs_2_.refs_3_.refs_4_.mix_ref, bf16[64,16,1536]{2,1,0:T(8,128)(2,1)S(1)} %get-tuple-element.19.refs_0_.terms_i.refs_1_, bf16[16,16,1536]{2,1,0:T(8,128)(2,1)S(1)} %collective-permute-done.got_i.refs_2_, ...), custom_call_target="tpu_custom_call", output_to_operand_aliasing={{}: (5, {})} | custom-call | flops 1 | bytes 1 | tf_op jit(solution)/shard_map/pallas_call | solution.py:277
  73.1 0.6 broadcast_multiply_fusion
  (22 shorter events, 1.9 us)
Async XLA Ops:
  2.7 24.0 %collective-permute-start.2 = (bf16[19,4,2048]{2,1,0:T(4,128)(2,1)S(1)}, bf16[19,4,2048]{2,1,0:T(4,128)(2,1)S(1)}, u32[]{:S(2)}, u32[]{:S(2)}) collective-permute-start(bf16[19,4,2048]{2,1,0:T(4,128)(2,1)S(1)} %get-tuple-element.22), channel_id=1, source_target_pairs={{2,0},{4,2},{6,4},{8,6},{10,8},{12,10},{14,12},{16,14},{18,16},{20... | collective-permute-start | bytes 933896 | tf_op jit(solution)/shard_map/ppermute | solution.py:351
  6.0 20.7 %collective-permute-start.3 = (bf16[19,4,2048]{2,1,0:T(4,128)(2,1)S(1)}, bf16[19,4,2048]{2,1,0:T(4,128)(2,1)S(1)}, u32[]{:S(2)}, u32[]{:S(2)}) collective-permute-start(bf16[19,4,2048]{2,1,0:T(4,128)(2,1)S(1)} %get-tuple-element.23), channel_id=1, source_target_pairs={{0,2},{2,4},{4,6},{6,8},{8,10},{10,12},{12,14},{14,16},{16,18},{18... | collective-permute-start | bytes 933896 | tf_op jit(solution)/shard_map/ppermute | solution.py:351
  11.3 15.4 %collective-permute-start.1 = (bf16[16,16,512]{2,1,0:T(8,128)(2,1)S(1)}, bf16[16,16,512]{2,1,0:T(8,128)(2,1)S(1)}, u32[]{:S(2)}, u32[]{:S(2)}) collective-permute-start(bf16[16,16,512]{2,1,0:T(8,128)(2,1)S(1)} %get-tuple-element.21), channel_id=1, source_target_pairs={{0,1},{1,0},{2,3},{3,2},{4,5},{5,4},{6,7},{7,6},{8,9},{9,8},{10,11... | collective-permute-start | bytes 786440 | tf_op jit(solution)/shard_map/ppermute | solution.py:344
  19.4 24.3 %collective-permute-start = (bf16[16,16,1536]{2,1,0:T(8,128)(2,1)S(1)}, bf16[16,16,1536]{2,1,0:T(8,128)(2,1)S(1)}, u32[]{:S(2)}, u32[]{:S(2)}) collective-permute-start(bf16[16,16,1536]{2,1,0:T(8,128)(2,1)S(1)} %get-tuple-element.20), channel_id=1, source_target_pairs={{0,1},{1,0},{2,3},{3,2},{4,5},{5,4},{6,7},{7,6},{8,9},{9,8},{10,11... | collective-permute-start | bytes 2359304 | tf_op jit(solution)/shard_map/ppermute | solution.py:344
  31.2 23.6 %collective-permute-start.5 = (bf16[16,16,1024]{2,1,0:T(8,128)(2,1)S(1)}, bf16[16,16,1024]{2,1,0:T(8,128)(2,1)S(1)}, u32[]{:S(2)}, u32[]{:S(2)}) collective-permute-start(bf16[16,16,1024]{2,1,0:T(8,128)(2,1)S(1)} %get-tuple-element.27), channel_id=1, source_target_pairs={{0,1},{1,0},{2,3},{3,2},{4,5},{5,4},{6,7},{7,6},{8,9},{9,8},{10,11... | collective-permute-start | bytes 1572872 | tf_op jit(solution)/shard_map/ppermute | solution.py:344
  31.3 7.5 %copy-start = (bf16[32,32,2048]{2,1,0:T(8,128)(2,1)S(1)}, bf16[32,32,2048]{2,1,0:T(8,128)(2,1)}, u32[]{:S(2)}) copy-start(bf16[32,32,2048]{2,1,0:T(8,128)(2,1)} %f_ref.1) | copy-start | bytes 12582916
  35.8 34.1 %collective-permute-start.4 = (bf16[16,16,1024]{2,1,0:T(8,128)(2,1)S(1)}, bf16[16,16,1024]{2,1,0:T(8,128)(2,1)S(1)}, u32[]{:S(2)}, u32[]{:S(2)}) collective-permute-start(bf16[16,16,1024]{2,1,0:T(8,128)(2,1)S(1)} %get-tuple-element.26), channel_id=1, source_target_pairs={{0,1},{1,0},{2,3},{3,2},{4,5},{5,4},{6,7},{7,6},{8,9},{9,8},{10,11... | collective-permute-start | bytes 1572872 | tf_op jit(solution)/shard_map/ppermute | solution.py:344
  43.7 4.4 %collective-permute-start.8 = (f32[64,32]{1,0:T(8,128)S(1)}, f32[64,32]{1,0:T(8,128)S(1)}, u32[]{:S(2)}, u32[]{:S(2)}) collective-permute-start(f32[64,32]{1,0:T(8,128)S(1)} %shard_map.86.refs_0_), channel_id=1, source_target_pairs={{0,24},{2,26},{4,28},{6,30},{8,16},{10,18},{12,20},{14,22},{16,8},... | collective-permute-start | bytes 24584 | tf_op jit(solution)/shard_map/ppermute | solution.py:318
  44.1 4.6 %collective-permute-start.7 = (f32[64,32]{1,0:T(8,128)S(1)}, f32[64,32]{1,0:T(8,128)S(1)}, u32[]{:S(2)}, u32[]{:S(2)}) collective-permute-start(f32[64,32]{1,0:T(8,128)S(1)} %shard_map.86.refs_0_), channel_id=1, source_target_pairs={{0,16},{2,18},{4,20},{6,22},{8,24},{10,26},{12,28},{14,30},{16,0},... | collective-permute-start | bytes 24584 | tf_op jit(solution)/shard_map/ppermute | solution.py:318
  44.1 5.3 %collective-permute-start.6 = (f32[64,32]{1,0:T(8,128)S(1)}, f32[64,32]{1,0:T(8,128)S(1)}, u32[]{:S(2)}, u32[]{:S(2)}) collective-permute-start(f32[64,32]{1,0:T(8,128)S(1)} %shard_map.86.refs_0_), channel_id=1, source_target_pairs={{0,8},{2,10},{4,12},{6,14},{8,0},{10,2},{12,4},{14,6},{16,24},{18,... | collective-permute-start | bytes 24584 | tf_op jit(solution)/shard_map/ppermute | solution.py:318
  54.8 4.3 %collective-permute-start.11 = (f32[64,32]{1,0:T(8,128)S(1)}, f32[64,32]{1,0:T(8,128)S(1)}, u32[]{:S(2)}, u32[]{:S(2)}) collective-permute-start(f32[64,32]{1,0:T(8,128)S(1)} %shard_map.87.refs_0_), channel_id=1, source_target_pairs={{0,96},{2,98},{4,100},{6,102},{8,104},{10,106},{12,108},{14,110},{... | collective-permute-start | bytes 24584 | tf_op jit(solution)/shard_map/ppermute | solution.py:318
  54.9 4.6 %collective-permute-start.10 = (f32[64,32]{1,0:T(8,128)S(1)}, f32[64,32]{1,0:T(8,128)S(1)}, u32[]{:S(2)}, u32[]{:S(2)}) collective-permute-start(f32[64,32]{1,0:T(8,128)S(1)} %shard_map.87.refs_0_), channel_id=1, source_target_pairs={{0,64},{2,66},{4,68},{6,70},{8,72},{10,74},{12,76},{14,78},{16,80}... | collective-permute-start | bytes 24584 | tf_op jit(solution)/shard_map/ppermute | solution.py:318
  55.0 5.1 %collective-permute-start.9 = (f32[64,32]{1,0:T(8,128)S(1)}, f32[64,32]{1,0:T(8,128)S(1)}, u32[]{:S(2)}, u32[]{:S(2)}) collective-permute-start(f32[64,32]{1,0:T(8,128)S(1)} %shard_map.87.refs_0_), channel_id=1, source_target_pairs={{0,32},{2,34},{4,36},{6,38},{8,40},{10,42},{12,44},{14,46},{16,48}... | collective-permute-start | bytes 24584 | tf_op jit(solution)/shard_map/ppermute | solution.py:318
  60.1 12.9 %collective-permute-start.14 = (f32[64,32]{1,0:T(8,128)S(1)}, f32[64,32]{1,0:T(8,128)S(1)}, u32[]{:S(2)}, u32[]{:S(2)}) collective-permute-start(f32[64,32]{1,0:T(8,128)S(1)} %shard_map.88.refs_0_), channel_id=1, source_target_pairs={{0,6},{2,4},{4,2},{6,0},{8,14},{10,12},{12,10},{14,8},{16,22},{18,... | collective-permute-start | bytes 24584 | tf_op jit(solution)/shard_map/ppermute | solution.py:318
  61.4 11.6 %collective-permute-start.13 = (f32[64,32]{1,0:T(8,128)S(1)}, f32[64,32]{1,0:T(8,128)S(1)}, u32[]{:S(2)}, u32[]{:S(2)}) collective-permute-start(f32[64,32]{1,0:T(8,128)S(1)} %shard_map.88.refs_0_), channel_id=1, source_target_pairs={{0,4},{2,6},{4,0},{6,2},{8,12},{10,14},{12,8},{14,10},{16,20},{18,... | collective-permute-start | bytes 24584 | tf_op jit(solution)/shard_map/ppermute | solution.py:318
  66.1 6.9 %collective-permute-start.12 = (f32[64,32]{1,0:T(8,128)S(1)}, f32[64,32]{1,0:T(8,128)S(1)}, u32[]{:S(2)}, u32[]{:S(2)}) collective-permute-start(f32[64,32]{1,0:T(8,128)S(1)} %shard_map.88.refs_0_), channel_id=1, source_target_pairs={{0,2},{2,0},{4,6},{6,4},{8,10},{10,8},{12,14},{14,12},{16,18},{18,... | collective-permute-start | bytes 24584 | tf_op jit(solution)/shard_map/ppermute | solution.py:318

commit v2 on v1

--- a/solution.py
+++ b/solution.py
@@ -11,7 +11,7 @@
 SIDE = 128
 SUB = 16
 TILE = 8
-INNER = (512, 1536)
+INNER = (768, 1280)
 OUTER = (1024, 1024)
 UNIT = 256
 ANY = pl.BlockSpec(memory_space=pl.ANY)
@@ -247,58 +247,87 @@
         in_specs=[VMEM] * (1 + len(terms)),
         out_specs=VMEM,
         scratch_shapes=[pltpu.VMEM((nt * SUB, nin * SUB), F32)],
-        compiler_params=params(36),
+        compiler_params=params(24),
         cost_estimate=COST,
     )(f, *terms)
 
 
-def finish_kernel(mix_ref, terms_i, got_i, terms_o, got_o, *refs):
-    out = []
-    for terms, got in ((terms_i, got_i), (terms_o, got_o)):
-        x = terms[...].reshape(-1, UNIT)
-        own = jnp.dot(mix_ref[...], x, preferred_element_type=F32)
-        out.append(own.reshape(got.shape) + got[...].astype(F32))
-    inner, outer = out
-    refs[-1][...] = jnp.concatenate([outer[:, TILE:], inner, outer[:, :TILE]], axis=1).astype(BF16)
-
-
-def finish(start, width, mix, inner, outer, out, rows, total):
+def own_kernel(mix_ref, *refs):
+    n = len(refs) // 2
+    for t_ref, own_ref in zip(refs[:n], refs[n:]):
+        kept = own_ref.shape[0]
+        for c in range(0, t_ref.shape[2], UNIT):
+            x = t_ref[:, :, c : c + UNIT].reshape(-1, UNIT)
+            y = jnp.dot(mix_ref[-kept * SUB :], x, preferred_element_type=F32)
+            own_ref[:, :, c : c + UNIT] = y.reshape(kept, SUB, UNIT)
+
+
+def own_parts(mix, terms, kept):
+    return pl.pallas_call(
+        own_kernel,
+        out_shape=[jax.ShapeDtypeStruct((kept, *t.shape[1:]), F32) for t in terms],
+        in_specs=[VMEM] * (1 + len(terms)),
+        out_specs=[VMEM] * len(terms),
+        compiler_params=params(20),
+        cost_estimate=COST,
+    )(mix, *terms)
+
+
+def finish_kernel(start, width, from_i, from_o, own_i, got_i, own_o, got_o, *refs):
+    out_ref, mark_ref, buf, sems = refs[-4:]
+    mark_ref[...] = jnp.zeros_like(mark_ref)
+    copies = []
+    for n in range(width // UNIT):
+        part = slice(n * UNIT, (n + 1) * UNIT)
+        i = slice(from_i + n * UNIT, from_i + (n + 1) * UNIT)
+        o = slice(from_o + n * UNIT, from_o + (n + 1) * UNIT)
+        inner = own_i[:, :, i] + got_i[:, :, i].astype(F32)
+        outer = own_o[:, :, o] + got_o[:, :, o].astype(F32)
+        rows = jnp.concatenate([outer[:, TILE:], inner, outer[:, :TILE]], axis=1)
+        buf[:, :, part] = rows.astype(BF16)
+        copies.append(
+            pltpu.make_async_copy(
+                buf.at[:, :, pl.ds(n * UNIT, UNIT)],
+                out_ref.at[:, :, pl.ds(start + n * UNIT, UNIT)],
+                sems.at[n],
+            )
+        )
+        copies[-1].start()
+    for c in copies:
+        c.wait()
+
+
+def finish(start, width, inner, outer, out, rows, total):
     kept = outer[2].shape[0]
-    nt = outer[1].shape[0]
     extra = () if out is None else (out,)
-    last = mix.shape[0] // (kept * SUB) - 1
-
-    def blocks(piece):
-        def index(j):
-            return (0, 0, j + (start - piece[0]) // UNIT)
-
-        return [pl.BlockSpec((n, SUB, UNIT), index) for n in (nt, kept)]
-
-    return pl.pallas_call(
-        finish_kernel,
-        grid=(width // UNIT,),
-        out_shape=jax.ShapeDtypeStruct((kept, rows, total), BF16),
-        in_specs=[pl.BlockSpec((kept * SUB, mix.shape[1]), lambda j: (last, 0))]
-        + blocks(inner)
-        + blocks(outer)
-        + [ANY] * len(extra),
-        out_specs=pl.BlockSpec((kept, rows, UNIT), lambda j: (0, 0, j + start // UNIT)),
-        input_output_aliases={5: 0} if extra else {},
-        compiler_params=params(16),
+    return pl.pallas_call(
+        functools.partial(finish_kernel, start, width, start - inner[0], start - outer[0]),
+        out_shape=(
+            jax.ShapeDtypeStruct((kept, rows, total), BF16),
+            jax.ShapeDtypeStruct((8, 128), F32),
+        ),
+        in_specs=[VMEM] * 4 + [ANY] * len(extra),
+        out_specs=(ANY, VMEM),
+        scratch_shapes=[
+            pltpu.VMEM((kept, rows, width), BF16),
+            pltpu.SemaphoreType.DMA((width // UNIT,)),
+        ],
+        input_output_aliases={4: 0} if extra else {},
+        compiler_params=params(12),
         cost_estimate=COST,
-    )(mix, *inner[1:], *outer[1:], *extra)
-
-
-def add_kernel(count, *refs):
+    )(*inner[1:], *outer[1:], *extra)
+
+
+def add_kernel(count, scale, *refs):
     values = [r[...] for r in refs[:count]]
     while len(values) > 1:
         values = [a + b for a, b in zip(values[::2], values[1::2])]
-    refs[-1][...] = values[0]
-
-
-def add(values, waits):
-    return pl.pallas_call(
-        functools.partial(add_kernel, len(values)),
+    refs[-1][...] = values[0] if scale is None else values[0] / jnp.sqrt(F32(scale))
+
+
+def add(values, waits, scale=None):
+    return pl.pallas_call(
+        functools.partial(add_kernel, len(values), scale),
         out_shape=jax.ShapeDtypeStruct(values[0].shape, F32),
         in_specs=[VMEM] * len(values) + [ANY] * len(waits),
         out_specs=VMEM,
@@ -307,18 +336,20 @@
     )(*values, *waits)
 
 
-def sum_over_pix(value, size, waits):
+def sum_over_pix(values, size, waits, scale):
     steps, step = [], 1
     while step < size:
         steps.append((step, 4 if step * 2 < size else 2))
         step *= steps[-1][1]
-    value = add([value], waits[0])
+    value = add(values, waits[0])
     for n, (step, count) in enumerate(steps[1:] + steps[:1]):
+        last = n + 1 == len(steps)
         moved = [
             lax.ppermute(value, "pix", [(i, i ^ (x * step)) for i in range(size)])
             for x in range(1, count)
         ]
-        value = add([value, *moved], waits[n + 1] if n + 1 < len(waits) else ())
+        wait = waits[n + 1] if n + 1 < len(waits) else ()
+        value = add([value, *moved], wait, scale if last else None)
     return value
 
 
@@ -332,38 +363,48 @@
     )
     pieces = []
 
-    def chunks(outer, widths, beside):
+    def chunks(outer, widths, beside, first):
         start = 0
         for width in widths:
-            waits = [pieces[-1][1]] if pieces else []
-            waits += [pieces[0][2]] if outer and not start else []
-            cost = LONG if outer and not start else COST
+            waits = [pieces[-1][1], *first] if pieces else []
+            late = outer and start
+            waits += [pieces[0][2]] if late else []
             terms, send = chunk_terms(
-                outer, start, width, g, maps, mix, part, nterms, beside, waits, cost
+                outer, start, width, g, maps, mix, part, nterms, beside, waits,
+                LONG if late else COST,
             )
             got = lax.ppermute(send, "ch", [(i, i ^ 1) for i in range(sides)])
             pieces.append(((outer, start, width), terms, got))
             start += width
-
-    chunks(False, INNER, ())
+            first = ()
+
+    def local(some):
+        places, terms, _ = zip(*some)
+        return own_parts(mix, terms, part), weights(places, terms, features)
+
+    n = len(INNER)
+    chunks(False, INNER, (), ())
+    own_inner, grad_inner = local(pieces)
     down = [(i, i + 1) for i in range(size - 1) if (i + 1) * rows % total]
     up = [(j, i) for i, j in down]
-    chunks(True, OUTER, (lax.ppermute(top, "pix", up), lax.ppermute(bottom, "pix", down)))
-
-    grad = weights([p[0] for p in pieces], [p[1] for p in pieces], features)
-    pixels = rows * size * total
-    arrived = [got for _, _, got in pieces]
-    n = len(INNER)
-    grad = sum_over_pix(grad, size, (arrived[:n], arrived[n:-1])) / jnp.sqrt(F32(pixels))
-    weight_grad = grad.reshape(nterms, nch, nin).transpose(0, 2, 1)
-    out = None
-    for (_, at, width), outer_terms, outer_got in pieces[n:]:
-        for (_, first, span), inner_terms, inner_got in pieces[:n]:
+    beside = (lax.ppermute(top, "pix", up), lax.ppermute(bottom, "pix", down))
+    chunks(True, OUTER, beside, (own_inner[0], grad_inner))
+    own_outer, grad_outer = local(pieces[n:])
+    pieces = [
+        (place, own, got) for (place, _, got), own in zip(pieces, (*own_inner, *own_outer))
+    ]
+    out, marks = None, []
+    for (_, at, width), outer_own, outer_got in pieces[n:]:
+        for (_, first, span), inner_own, inner_got in pieces[:n]:
             lo, hi = max(at, first), min(at + width, first + span)
             if lo < hi:
-                inner = (first, inner_terms, inner_got)
-                outer = (at, outer_terms, outer_got)
-                out = finish(lo, hi - lo, mix, inner, outer, out, rows, total)
+                inner = (first, inner_own, inner_got)
+                outer = (at, outer_own, outer_got)
+                out, mark = finish(lo, hi - lo, inner, outer, out, rows, total)
+                marks.append(mark)
+    waits = ([got for _, _, got in pieces[:n]], own_outer[:1], marks[-2:-1])
+    grad = sum_over_pix([grad_inner, grad_outer], size, waits, rows * size * total)
+    weight_grad = grad.reshape(nterms, nch, nin).transpose(0, 2, 1)
     return out, weight_grad
 
 

time: 73.9 us -> 67.4 us (0.912)
  waiting for transfers between devices: 16.7 us -> 7.76 us
  starting transfers between devices: 25.4 us -> 26.8 us
  local copies, waits for them, and re-layouts: 0.01 us -> 0.94 us
    ppermute x4, waiting for transfers between devices: 12.5 us -> 0.01 us  [chunks(): got = lax.ppermute(send, 'ch', [(i, i ^ 1) for i in range(sides)])]
    ppermute x4, starting transfers between devices: 6.24 us -> 8.27 us  [chunks(): got = lax.ppermute(send, 'ch', [(i, i ^ 1) for i in range(sides)])]
    ppermute x2, waiting for transfers between devices: 0.01 us -> 1.82 us  [per_device(): beside = (lax.ppermute(top, 'pix', up), lax.ppermute(bottom, 'pix', down))]
    ppermute x9, waiting for transfers between devices: 4.24 us -> 5.93 us  [sum_over_pix(): lax.ppermute(value, 'pix', [(i, i ^ x * step) for i in range(size)])]
    ppermute x2, starting transfers between devices: 6.52 us -> 5.55 us  [per_device(): beside = (lax.ppermute(top, 'pix', up), lax.ppermute(bottom, 'pix', down))]
    unnamed x2, local copies, waits for them, and re-layouts: 0.01 us -> 0.94 us
    pallas_call x1 -> x2, Pallas kernels: 4.87 us -> 5.43 us  [weights(): pl.pallas_call(functools.partial(weights_kernel, places), out_shape=jax.S...]
    pallas_call x7 -> x9, Pallas kernels: 6.96 us -> 7.08 us  [the longest x3 3.95 us: finish(): pl.pallas_call(functools.partial(finish_kernel, start, width, start - inn...]
  transfers between devices with their start and end apart: 15 -> 15, of which waited for: 8 -> 6; matrix products, arithmetic and copies ran while one was open for 0% -> 0% of each run, Pallas kernels for 38% -> 36%
where the time goes in v2:
time: 67.4 us; the launch traced here: 67.2 us
  Pallas kernels  30.8 us (46%)
  starting transfers between devices  26.8 us (40%)
  waiting for transfers between devices  7.76 us (12%)
  local copies, waits for them, and re-layouts  0.94 us (1%)
  between operations  0.94 us (1%)
    pallas_call x4, Pallas kernels, chunk_terms(): pl.pallas_call(functools.partial(terms_kernel, outer, start - lo, lo, hi,...  16.2 us
    ppermute x9, starting transfers between devices, sum_over_pix(): lax.ppermute(value, 'pix', [(i, i ^ x * step) for i in range(size)])  12.9 us
    ppermute x4, starting transfers between devices, chunks(): got = lax.ppermute(send, 'ch', [(i, i ^ 1) for i in range(sides)])  8.27 us
    ppermute x9, waiting for transfers between devices, sum_over_pix(): lax.ppermute(value, 'pix', [(i, i ^ x * step) for i in range(size)])  5.93 us
    ppermute x2, starting transfers between devices, per_device(): beside = (lax.ppermute(top, 'pix', up), lax.ppermute(bottom, 'pix', down))  5.55 us
    pallas_call x2, Pallas kernels, weights(): pl.pallas_call(functools.partial(weights_kernel, places), out_shape=jax.S...  5.43 us
    pallas_call x3, Pallas kernels, finish(): pl.pallas_call(functools.partial(finish_kernel, start, width, start - inn...  3.95 us
    pallas_call x2, Pallas kernels, own_parts(): pl.pallas_call(own_kernel, out_shape=[jax.ShapeDtypeStruct((kept, *t.shap...  2.49 us
  transfers between devices with their start and end apart: 15, of which 6 were waited for; matrix products, arithmetic and copies ran while one was open for 0% of the time, Pallas kernels for 36%

profile of v2, /device:TPU:1, one launch (start us, length us, event | category | flops | bytes accessed | tf_op | source)
XLA Modules:
  0.0 67.2 jit_solution(16257888376749235057)
XLA Ops:
  0.6 2.0 %shard_map.77 = (bf16[512,1024]{1,0:T(8,128)(2,1)S(1)}, bf16[16,32,2048]{2,1,0:T(8,128)(2,1)S(1)}, f32[3,32,2048]{2,1,0:T(8,128)S(1)}, bf16[19,4,2048]{2,1,0:T(4,128)(2,1)S(1)}, bf16[19,4,2048]{2,1,0:T(4,128)(2,1)S(1)}) custom-call(bf16[4,16,32]{2,1,0:T(8,128)(2,1)} %bitcast.5, bf16[16,32,2048]{2,1,0:T(8,128)(2,1)} %g_ref.1, f32[32,2048]{1,0:T(8,128)} %east_ref.1, ...), custom_call_target="tpu_custom_call" | custom-call | flops 1 | bytes 1 | tf_op jit(solution)/shard_map/pallas_call | solution.py:83
  2.7 2.9 %shard_map.78 = (bf16[64,16,768]{2,1,0:T(8,128)(2,1)S(1)}, bf16[16,16,768]{2,1,0:T(8,128)(2,1)S(1)}) custom-call(bf16[16,32,2048]{2,1,0:T(8,128)(2,1)S(1)} %get-tuple-element.24.refs_0_.refs_1_.refs_3_.refs_2_, f32[3,32,2048]{2,1,0:T(8,128)S(1)} %get-tuple-element.25.refs_1_.refs_2_.refs_4_.refs_3_, ...), custom_call_target="tpu_custom_call" | custom-call | flops 1 | bytes 1 | tf_op jit(solution)/shard_map/pallas_call | solution.py:200
  5.5 3.8 %collective-permute-start.3 = (bf16[16,16,768]{2,1,0:T(8,128)(2,1)S(1)}, bf16[16,16,768]{2,1,0:T(8,128)(2,1)S(1)}, u32[]{:S(2)}, u32[]{:S(2)}) collective-permute-start(bf16[16,16,768]{2,1,0:T(8,128)(2,1)S(1)} %get-tuple-element.34), channel_id=1, source_target_pairs={{0,1},{1,0},{2,3},{3,2},{4,5},{5,4},{6,7},{7,6},{8,9},{9,8},{10,11... | collective-permute-start | bytes 1179656 | tf_op jit(solution)/shard_map/ppermute | solution.py:376
  9.3 2.9 %collective-permute-start.1 = (bf16[19,4,2048]{2,1,0:T(4,128)(2,1)S(1)}, bf16[19,4,2048]{2,1,0:T(4,128)(2,1)S(1)}, u32[]{:S(2)}, u32[]{:S(2)}) collective-permute-start(bf16[19,4,2048]{2,1,0:T(4,128)(2,1)S(1)} %get-tuple-element.31), channel_id=1, source_target_pairs={{2,0},{4,2},{6,4},{8,6},{10,8},{12,10},{14,12},{16,14},{18,16},{20... | collective-permute-start | bytes 933896 | tf_op jit(solution)/shard_map/ppermute | solution.py:390
  12.2 2.7 %collective-permute-start.2 = (bf16[19,4,2048]{2,1,0:T(4,128)(2,1)S(1)}, bf16[19,4,2048]{2,1,0:T(4,128)(2,1)S(1)}, u32[]{:S(2)}, u32[]{:S(2)}) collective-permute-start(bf16[19,4,2048]{2,1,0:T(4,128)(2,1)S(1)} %get-tuple-element.32), channel_id=1, source_target_pairs={{0,2},{2,4},{4,6},{6,8},{8,10},{10,12},{12,14},{14,16},{16,18},{18... | collective-permute-start | bytes 933896 | tf_op jit(solution)/shard_map/ppermute | solution.py:390
  14.9 4.4 %shard_map.79 = (bf16[64,16,1280]{2,1,0:T(8,128)(2,1)S(1)}, bf16[16,16,1280]{2,1,0:T(8,128)(2,1)S(1)}) custom-call(bf16[64,16,768]{2,1,0:T(8,128)(2,1)S(1)} %get-tuple-element.26.refs_0_, bf16[16,32,2048]{2,1,0:T(8,128)(2,1)S(1)} %get-tuple-element.24.refs_0_.refs_1_.refs_3_.refs_2_, f32[3,32,2048]{2,1,0:T(8,128)S(1)} %get-tuple-element.25.refs_1_.refs_2_.refs_4_.refs_3_, ...), custom_call_target="tpu_custom_call" | custom-call | flops 1 | bytes 1 | tf_op jit(solution)/shard_map/pallas_call | solution.py:200
  20.5 1.2 %shard_map.80 = (f32[16,16,768]{2,1,0:T(8,128)S(1)}, f32[16,16,1280]{2,1,0:T(8,128)S(1)}) custom-call(bf16[512,1024]{1,0:T(8,128)(2,1)S(1)} %get-tuple-element.23.refs_2_.refs_3_.mix_ref.refs_5_.refs_4_, bf16[64,16,768]{2,1,0:T(8,128)(2,1)S(1)} %get-tuple-element.26.refs_0_, bf16[64,16,1280]{2,1,0:T(8,128)(2,1)S(1)} %get-tuple-element.27.refs_1_.refs_0_), custom_call_target="tpu_custom_call" | custom-call | flops 1 | bytes 1 | tf_op jit(solution)/shard_map/pallas_call | solution.py:266
  22.7 2.7 %shard_map.81.refs_2_.refs_0_ = f32[64,32]{1,0:T(8,128)S(1)} custom-call(bf16[32,32,2048]{2,1,0:T(8,128)(2,1)S(1)} %copy-done, bf16[64,16,768]{2,1,0:T(8,128)(2,1)S(1)} %get-tuple-element.26.refs_0_, bf16[64,16,1280]{2,1,0:T(8,128)(2,1)S(1)} %get-tuple-element.27.refs_1_.refs_0_), custom_call_target="tpu_custom_call" | custom-call | flops 1 | bytes 1 | tf_op jit(solution)/shard_map/pallas_call | solution.py:244
  25.4 1.8 %collective-permute-done.1.refs_6_.refs_5_ = bf16[19,4,2048]{2,1,0:T(4,128)(2,1)S(1)} collective-permute-done((bf16[19,4,2048]{2,1,0:T(4,128)(2,1)S(1)}, bf16[19,4,2048]{2,1,0:T(4,128)(2,1)S(1)}, u32[]{:S(2)}, u32[]{:S(2)}) %collective-permute-start.1) | collective-permute-done | bytes 311328 | tf_op jit(solution)/shard_map/ppermute | solution.py:390
  27.2 4.5 %shard_map.82 = (bf16[64,16,1024]{2,1,0:T(8,128)(2,1)S(1)}, bf16[16,16,1024]{2,1,0:T(8,128)(2,1)S(1)}) custom-call(bf16[64,16,1280]{2,1,0:T(8,128)(2,1)S(1)} %get-tuple-element.27.refs_1_.refs_0_, f32[16,16,768]{2,1,0:T(8,128)S(1)} %get-tuple-element.30.refs_1_.own_i, f32[64,32]{1,0:T(8,128)S(1)} %shard_map.81.refs_2_.refs_0_, ...), custom_call_target="tpu_custom_call" | custom-call | flops 1 | bytes 1 | tf_op jit(solution)/shard_map/pallas_call | solution.py:200
  31.7 1.6 %collective-permute-start.5 = (bf16[16,16,1024]{2,1,0:T(8,128)(2,1)S(1)}, bf16[16,16,1024]{2,1,0:T(8,128)(2,1)S(1)}, u32[]{:S(2)}, u32[]{:S(2)}) collective-permute-start(bf16[16,16,1024]{2,1,0:T(8,128)(2,1)S(1)} %get-tuple-element.39), channel_id=1, source_target_pairs={{0,1},{1,0},{2,3},{3,2},{4,5},{5,4},{6,7},{7,6},{8,9},{9,8},{10,11... | collective-permute-start | bytes 1572872 | tf_op jit(solution)/shard_map/ppermute | solution.py:376
  33.3 4.5 %shard_map.83 = (bf16[64,16,1024]{2,1,0:T(8,128)(2,1)S(1)}, bf16[16,16,1024]{2,1,0:T(8,128)(2,1)S(1)}) custom-call(bf16[64,16,1024]{2,1,0:T(8,128)(2,1)S(1)} %get-tuple-element.33.refs_0_, bf16[16,16,768]{2,1,0:T(8,128)(2,1)S(1)} %collective-permute-done.3.refs_1_.got_i.refs_2_, bf16[16,32,2048]{2,1,0:T(8,128)(2,1)S(1)} %get-tuple-element.24.refs_0_.refs_1_.refs_3_.refs_2_, ...), custom_call_target="tpu_custom_call" | custom-call | flops 10000000000 | bytes 100000000 | tf_op jit(solution)/shard_map/pallas_call | solution.py:200
  37.8 1.7 %collective-permute-start.4 = (bf16[16,16,1024]{2,1,0:T(8,128)(2,1)S(1)}, bf16[16,16,1024]{2,1,0:T(8,128)(2,1)S(1)}, u32[]{:S(2)}, u32[]{:S(2)}) collective-permute-start(bf16[16,16,1024]{2,1,0:T(8,128)(2,1)S(1)} %get-tuple-element.37), channel_id=1, source_target_pairs={{0,1},{1,0},{2,3},{3,2},{4,5},{5,4},{6,7},{7,6},{8,9},{9,8},{10,11... | collective-permute-start | bytes 1572872 | tf_op jit(solution)/shard_map/ppermute | solution.py:376
  39.5 2.7 %shard_map.88.refs_1_ = f32[64,32]{1,0:T(8,128)S(1)} custom-call(bf16[32,32,2048]{2,1,0:T(8,128)(2,1)S(1)} %copy-done, bf16[64,16,1024]{2,1,0:T(8,128)(2,1)S(1)} %get-tuple-element.33.refs_0_, bf16[64,16,1024]{2,1,0:T(8,128)(2,1)S(1)} %get-tuple-element.35.refs_1_), custom_call_target="tpu_custom_call" | custom-call | flops 1 | bytes 1 | tf_op jit(solution)/shard_map/pallas_call | solution.py:244
  42.3 2.0 %collective-permute-start.8 = (f32[64,32]{1,0:T(8,128)S(1)}, f32[64,32]{1,0:T(8,128)S(1)}, u32[]{:S(2)}, u32[]{:S(2)}) collective-permute-start(f32[64,32]{1,0:T(8,128)S(1)} %shard_map.89.refs_0_), channel_id=1, source_target_pairs={{0,24},{2,26},{4,28},{6,30},{8,16},{10,18},{12,20},{14,22},{16,8},... | collective-permute-start | bytes 24584 | tf_op jit(solution)/shard_map/ppermute | solution.py:348
  44.3 1.7 %collective-permute-start.7 = (f32[64,32]{1,0:T(8,128)S(1)}, f32[64,32]{1,0:T(8,128)S(1)}, u32[]{:S(2)}, u32[]{:S(2)}) collective-permute-start(f32[64,32]{1,0:T(8,128)S(1)} %shard_map.89.refs_0_), channel_id=1, source_target_pairs={{0,16},{2,18},{4,20},{6,22},{8,24},{10,26},{12,28},{14,30},{16,0},... | collective-permute-start | bytes 24584 | tf_op jit(solution)/shard_map/ppermute | solution.py:348
  46.0 1.2 %shard_map.84 = (f32[16,16,1024]{2,1,0:T(8,128)S(1)}, f32[16,16,1024]{2,1,0:T(8,128)S(1)}) custom-call(bf16[512,1024]{1,0:T(8,128)(2,1)S(1)} %get-tuple-element.23.refs_2_.refs_3_.mix_ref.refs_5_.refs_4_, bf16[64,16,1024]{2,1,0:T(8,128)(2,1)S(1)} %get-tuple-element.33.refs_0_, bf16[64,16,1024]{2,1,0:T(8,128)(2,1)S(1)} %get-tuple-element.35.refs_1_), custom_call_target="tpu_custom_call" | custom-call | flops 1 | bytes 1 | tf_op jit(solution)/shard_map/pallas_call | solution.py:266
  47.3 1.6 %collective-permute-done.7.refs_2_ = f32[64,32]{1,0:T(8,128)S(1)} collective-permute-done((f32[64,32]{1,0:T(8,128)S(1)}, f32[64,32]{1,0:T(8,128)S(1)}, u32[]{:S(2)}, u32[]{:S(2)}) %collective-permute-start.7) | collective-permute-done | bytes 8224 | tf_op jit(solution)/shard_map/ppermute | solution.py:348
  49.1 5.8 %collective-permute-start.11 = (f32[64,32]{1,0:T(8,128)S(1)}, f32[64,32]{1,0:T(8,128)S(1)}, u32[]{:S(2)}, u32[]{:S(2)}) collective-permute-start(f32[64,32]{1,0:T(8,128)S(1)} %shard_map.90.refs_0_), channel_id=1, source_target_pairs={{0,96},{2,98},{4,100},{6,102},{8,104},{10,106},{12,108},{14,110},{... | collective-permute-start | bytes 24584 | tf_op jit(solution)/shard_map/ppermute | solution.py:348
  55.6 1.5 %shard_map.85 = (bf16[16,32,2048]{2,1,0:T(8,128)(2,1)}, f32[8,128]{1,0:T(8,128)}) custom-call(f32[16,16,768]{2,1,0:T(8,128)S(1)} %get-tuple-element.30.refs_1_.own_i, bf16[16,16,768]{2,1,0:T(8,128)(2,1)S(1)} %collective-permute-done.3.refs_1_.got_i.refs_2_, f32[16,16,1024]{2,1,0:T(8,128)S(1)} %get-tuple-element.38.own_o.refs_4_, ...), custom_call_target="tpu_custom_call" | custom-call | flops 1 | bytes 1 | tf_op jit(solution)/shard_map/pallas_call | solution.py:303
  57.9 1.8 %collective-permute-done.10.refs_2_ = f32[64,32]{1,0:T(8,128)S(1)} collective-permute-done((f32[64,32]{1,0:T(8,128)S(1)}, f32[64,32]{1,0:T(8,128)S(1)}, u32[]{:S(2)}, u32[]{:S(2)}) %collective-permute-start.10) | collective-permute-done | bytes 8224 | tf_op jit(solution)/shard_map/ppermute | solution.py:348
  59.7 2.2 %collective-permute-start.14 = (f32[64,32]{1,0:T(8,128)S(1)}, f32[64,32]{1,0:T(8,128)S(1)}, u32[]{:S(2)}, u32[]{:S(2)}) collective-permute-start(f32[64,32]{1,0:T(8,128)S(1)} %shard_map.91.refs_0_), channel_id=1, source_target_pairs={{0,6},{2,4},{4,2},{6,0},{8,14},{10,12},{12,10},{14,8},{16,22},{18,... | collective-permute-start | bytes 24584 | tf_op jit(solution)/shard_map/ppermute | solution.py:348
  63.6 1.2 %collective-permute-done.13.refs_2_ = f32[64,32]{1,0:T(8,128)S(1)} collective-permute-done((f32[64,32]{1,0:T(8,128)S(1)}, f32[64,32]{1,0:T(8,128)S(1)}, u32[]{:S(2)}, u32[]{:S(2)}) %collective-permute-start.13) | collective-permute-done | bytes 8224 | tf_op jit(solution)/shard_map/ppermute | solution.py:348
  65.4 1.6 %shard_map.87 = (bf16[16,32,2048]{2,1,0:T(8,128)(2,1)}, f32[8,128]{1,0:T(8,128)}) custom-call(f32[16,16,1280]{2,1,0:T(8,128)S(1)} %get-tuple-element.28.own_i, bf16[16,16,1280]{2,1,0:T(8,128)(2,1)S(1)} %collective-permute-done.got_i.refs_3_, f32[16,16,1024]{2,1,0:T(8,128)S(1)} %get-tuple-element.36.own_o, ...), custom_call_target="tpu_custom_call", output_to_operand_aliasing={{0}: (4, {})} | custom-call | flops 1 | bytes 1 | tf_op jit(solution)/shard_map/pallas_call | solution.py:303
  (24 shorter events, 6.0 us)
Async XLA Ops:
  5.5 27.8 %collective-permute-start.3 = (bf16[16,16,768]{2,1,0:T(8,128)(2,1)S(1)}, bf16[16,16,768]{2,1,0:T(8,128)(2,1)S(1)}, u32[]{:S(2)}, u32[]{:S(2)}) collective-permute-start(bf16[16,16,768]{2,1,0:T(8,128)(2,1)S(1)} %get-tuple-element.34), channel_id=1, source_target_pairs={{0,1},{1,0},{2,3},{3,2},{4,5},{5,4},{6,7},{7,6},{8,9},{9,8},{10,11... | collective-permute-start | bytes 1179656 | tf_op jit(solution)/shard_map/ppermute | solution.py:376
  9.3 17.9 %collective-permute-start.1 = (bf16[19,4,2048]{2,1,0:T(4,128)(2,1)S(1)}, bf16[19,4,2048]{2,1,0:T(4,128)(2,1)S(1)}, u32[]{:S(2)}, u32[]{:S(2)}) collective-permute-start(bf16[19,4,2048]{2,1,0:T(4,128)(2,1)S(1)} %get-tuple-element.31), channel_id=1, source_target_pairs={{2,0},{4,2},{6,4},{8,6},{10,8},{12,10},{14,12},{16,14},{18,16},{20... | collective-permute-start | bytes 933896 | tf_op jit(solution)/shard_map/ppermute | solution.py:390
  12.2 15.0 %collective-permute-start.2 = (bf16[19,4,2048]{2,1,0:T(4,128)(2,1)S(1)}, bf16[19,4,2048]{2,1,0:T(4,128)(2,1)S(1)}, u32[]{:S(2)}, u32[]{:S(2)}) collective-permute-start(bf16[19,4,2048]{2,1,0:T(4,128)(2,1)S(1)} %get-tuple-element.32), channel_id=1, source_target_pairs={{0,2},{2,4},{4,6},{6,8},{8,10},{10,12},{12,14},{14,16},{16,18},{18... | collective-permute-start | bytes 933896 | tf_op jit(solution)/shard_map/ppermute | solution.py:390
  19.4 22.9 %collective-permute-start = (bf16[16,16,1280]{2,1,0:T(8,128)(2,1)S(1)}, bf16[16,16,1280]{2,1,0:T(8,128)(2,1)S(1)}, u32[]{:S(2)}, u32[]{:S(2)}) collective-permute-start(bf16[16,16,1280]{2,1,0:T(8,128)(2,1)S(1)} %get-tuple-element.29), channel_id=1, source_target_pairs={{0,1},{1,0},{2,3},{3,2},{4,5},{5,4},{6,7},{7,6},{8,9},{9,8},{10,11... | collective-permute-start | bytes 1966088 | tf_op jit(solution)/shard_map/ppermute | solution.py:376
  20.5 2.2 %copy-start = (bf16[32,32,2048]{2,1,0:T(8,128)(2,1)S(1)}, bf16[32,32,2048]{2,1,0:T(8,128)(2,1)}, u32[]{:S(2)}) copy-start(bf16[32,32,2048]{2,1,0:T(8,128)(2,1)} %f_ref.3) | copy-start | bytes 12582916
  31.7 23.9 %collective-permute-start.5 = (bf16[16,16,1024]{2,1,0:T(8,128)(2,1)S(1)}, bf16[16,16,1024]{2,1,0:T(8,128)(2,1)S(1)}, u32[]{:S(2)}, u32[]{:S(2)}) collective-permute-start(bf16[16,16,1024]{2,1,0:T(8,128)(2,1)S(1)} %get-tuple-element.39), channel_id=1, source_target_pairs={{0,1},{1,0},{2,3},{3,2},{4,5},{5,4},{6,7},{7,6},{8,9},{9,8},{10,11... | collective-permute-start | bytes 1572872 | tf_op jit(solution)/shard_map/ppermute | solution.py:376
  37.8 27.5 %collective-permute-start.4 = (bf16[16,16,1024]{2,1,0:T(8,128)(2,1)S(1)}, bf16[16,16,1024]{2,1,0:T(8,128)(2,1)S(1)}, u32[]{:S(2)}, u32[]{:S(2)}) collective-permute-start(bf16[16,16,1024]{2,1,0:T(8,128)(2,1)S(1)} %get-tuple-element.37), channel_id=1, source_target_pairs={{0,1},{1,0},{2,3},{3,2},{4,5},{5,4},{6,7},{7,6},{8,9},{9,8},{10,11... | collective-permute-start | bytes 1572872 | tf_op jit(solution)/shard_map/ppermute | solution.py:376
  42.3 5.0 %collective-permute-start.8 = (f32[64,32]{1,0:T(8,128)S(1)}, f32[64,32]{1,0:T(8,128)S(1)}, u32[]{:S(2)}, u32[]{:S(2)}) collective-permute-start(f32[64,32]{1,0:T(8,128)S(1)} %shard_map.89.refs_0_), channel_id=1, source_target_pairs={{0,24},{2,26},{4,28},{6,30},{8,16},{10,18},{12,20},{14,22},{16,8},... | collective-permute-start | bytes 24584 | tf_op jit(solution)/shard_map/ppermute | solution.py:348
  44.3 4.6 %collective-permute-start.7 = (f32[64,32]{1,0:T(8,128)S(1)}, f32[64,32]{1,0:T(8,128)S(1)}, u32[]{:S(2)}, u32[]{:S(2)}) collective-permute-start(f32[64,32]{1,0:T(8,128)S(1)} %shard_map.89.refs_0_), channel_id=1, source_target_pairs={{0,16},{2,18},{4,20},{6,22},{8,24},{10,26},{12,28},{14,30},{16,0},... | collective-permute-start | bytes 24584 | tf_op jit(solution)/shard_map/ppermute | solution.py:348
  46.0 3.1 %collective-permute-start.6 = (f32[64,32]{1,0:T(8,128)S(1)}, f32[64,32]{1,0:T(8,128)S(1)}, u32[]{:S(2)}, u32[]{:S(2)}) collective-permute-start(f32[64,32]{1,0:T(8,128)S(1)} %shard_map.89.refs_0_), channel_id=1, source_target_pairs={{0,8},{2,10},{4,12},{6,14},{8,0},{10,2},{12,4},{14,6},{16,24},{18,... | collective-permute-start | bytes 24584 | tf_op jit(solution)/shard_map/ppermute | solution.py:348
  49.1 8.8 %collective-permute-start.11 = (f32[64,32]{1,0:T(8,128)S(1)}, f32[64,32]{1,0:T(8,128)S(1)}, u32[]{:S(2)}, u32[]{:S(2)}) collective-permute-start(f32[64,32]{1,0:T(8,128)S(1)} %shard_map.90.refs_0_), channel_id=1, source_target_pairs={{0,96},{2,98},{4,100},{6,102},{8,104},{10,106},{12,108},{14,110},{... | collective-permute-start | bytes 24584 | tf_op jit(solution)/shard_map/ppermute | solution.py:348
  54.9 4.9 %collective-permute-start.10 = (f32[64,32]{1,0:T(8,128)S(1)}, f32[64,32]{1,0:T(8,128)S(1)}, u32[]{:S(2)}, u32[]{:S(2)}) collective-permute-start(f32[64,32]{1,0:T(8,128)S(1)} %shard_map.90.refs_0_), channel_id=1, source_target_pairs={{0,64},{2,66},{4,68},{6,70},{8,72},{10,74},{12,76},{14,78},{16,80}... | collective-permute-start | bytes 24584 | tf_op jit(solution)/shard_map/ppermute | solution.py:348
  54.9 4.9 %collective-permute-start.9 = (f32[64,32]{1,0:T(8,128)S(1)}, f32[64,32]{1,0:T(8,128)S(1)}, u32[]{:S(2)}, u32[]{:S(2)}) collective-permute-start(f32[64,32]{1,0:T(8,128)S(1)} %shard_map.90.refs_0_), channel_id=1, source_target_pairs={{0,32},{2,34},{4,36},{6,38},{8,40},{10,42},{12,44},{14,46},{16,48}... | collective-permute-start | bytes 24584 | tf_op jit(solution)/shard_map/ppermute | solution.py:348
  59.7 3.8 %collective-permute-start.14 = (f32[64,32]{1,0:T(8,128)S(1)}, f32[64,32]{1,0:T(8,128)S(1)}, u32[]{:S(2)}, u32[]{:S(2)}) collective-permute-start(f32[64,32]{1,0:T(8,128)S(1)} %shard_map.91.refs_0_), channel_id=1, source_target_pairs={{0,6},{2,4},{4,2},{6,0},{8,14},{10,12},{12,10},{14,8},{16,22},{18,... | collective-permute-start | bytes 24584 | tf_op jit(solution)/shard_map/ppermute | solution.py:348
  62.0 2.8 %collective-permute-start.13 = (f32[64,32]{1,0:T(8,128)S(1)}, f32[64,32]{1,0:T(8,128)S(1)}, u32[]{:S(2)}, u32[]{:S(2)}) collective-permute-start(f32[64,32]{1,0:T(8,128)S(1)} %shard_map.91.refs_0_), channel_id=1, source_target_pairs={{0,4},{2,6},{4,0},{6,2},{8,12},{10,14},{12,8},{14,10},{16,20},{18,... | collective-permute-start | bytes 24584 | tf_op jit(solution)/shard_map/ppermute | solution.py:348
  62.0 2.8 %collective-permute-start.12 = (f32[64,32]{1,0:T(8,128)S(1)}, f32[64,32]{1,0:T(8,128)S(1)}, u32[]{:S(2)}, u32[]{:S(2)}) collective-permute-start(f32[64,32]{1,0:T(8,128)S(1)} %shard_map.91.refs_0_), channel_id=1, source_target_pairs={{0,2},{2,0},{4,6},{6,4},{8,10},{10,8},{12,14},{14,12},{16,18},{18,... | collective-permute-start | bytes 24584 | tf_op jit(solution)/shard_map/ppermute | solution.py:348

commit v3 on v2

--- a/solution.py
+++ b/solution.py
@@ -11,7 +11,7 @@
 SIDE = 128
 SUB = 16
 TILE = 8
-INNER = (768, 1280)
+INNER = (512, 1536)
 OUTER = (1024, 1024)
 UNIT = 256
 ANY = pl.BlockSpec(memory_space=pl.ANY)
@@ -34,7 +34,7 @@
 
 def prepare_kernel(
     sides, w_hbm, g_ref, east_ref, south_ref, mask_ref,
-    mix_ref, g_out, maps_out, top_ref, bottom_ref, mask_buf, w_ref, sems,
+    mix_ref, g_out, maps_out, partner_ref, other_ref, mask_buf, w_ref, sems,
 ):
     copies = [
         pltpu.make_async_copy(src, dst, sems.at[n])
@@ -69,10 +69,12 @@
     maps_out[2] = mask
     copies[4].wait()
     nch = g_out.shape[0]
+    even = lax.axis_index("pix") % 2 == 0
     for o in range(nch + 3):
         x = g_out[o].astype(F32) if o < nch else maps_out[o - nch]
-        top_ref[o] = x[:HALO].astype(BF16)
-        bottom_ref[o] = x[height - TILE :][TILE - HALO :].astype(BF16)
+        top, bottom = x[:HALO].astype(BF16), x[height - TILE :][TILE - HALO :].astype(BF16)
+        partner_ref[o] = jnp.where(even, bottom, top)
+        other_ref[o] = jnp.where(even, top, bottom)
 
 
 def prepare(w, g, east, south, mask, sides):
@@ -123,7 +125,8 @@
 
 def terms_kernel(outer, off, lo, hi, nterms, waits, *refs):
     g_ref, maps_ref, mix_ref = refs[waits : waits + 3]
-    below_ref, above_ref = refs[waits + 3 : waits + 5] if outer else (None, None)
+    partner_ref, other_ref = refs[waits + 3 : waits + 5] if outer else (None, None)
+    even = lax.axis_index("pix") % 2 == 0
     terms_ref, send_ref, w_buf = refs[-3:]
     nch = g_ref.shape[0]
     ext, span = w_buf.shape[1:]
@@ -133,8 +136,10 @@
     def arrange(x, n):
         x = x.astype(F32)
         if outer:
-            below, above = below_ref[n, :, cols], above_ref[n, :, cols]
-            return outer_rows(x, below.astype(F32), above.astype(F32))
+            partner = partner_ref[n, :, cols].astype(F32)
+            other = other_ref[n, :, cols].astype(F32)
+            below, above = jnp.where(even, partner, other), jnp.where(even, other, partner)
+            return outer_rows(x, below, above)
         return inner_rows(x)
 
     ew = arrange(maps_ref[0, :, cols], nch)
@@ -358,7 +363,7 @@
     nterms, nin, _ = cheb_weight.shape
     size, sides = lax.axis_size("pix"), lax.axis_size("ch")
     part = nin // sides
-    mix, g, maps, top, bottom = prepare(
+    mix, g, maps, to_partner, to_other = prepare(
         cheb_weight, grad_out, east_weight, south_weight, pixel_mask, sides
     )
     pieces = []
@@ -385,9 +390,11 @@
     n = len(INNER)
     chunks(False, INNER, (), ())
     own_inner, grad_inner = local(pieces)
-    down = [(i, i + 1) for i in range(size - 1) if (i + 1) * rows % total]
-    up = [(j, i) for i, j in down]
-    beside = (lax.ppermute(top, "pix", up), lax.ppermute(bottom, "pix", down))
+    def swap(x, first):
+        pairs = [(i, i + 1) for i in range(first, size - 1, 2) if (i + 1) * rows % total]
+        return lax.ppermute(x, "pix", pairs + [(j, i) for i, j in pairs])
+
+    beside = (swap(to_partner, 0), swap(to_other, 1))
     chunks(True, OUTER, beside, (own_inner[0], grad_inner))
     own_outer, grad_outer = local(pieces[n:])
     pieces = [
@@ -402,7 +409,7 @@
                 outer = (at, outer_own, outer_got)
                 out, mark = finish(lo, hi - lo, inner, outer, out, rows, total)
                 marks.append(mark)
-    waits = ([got for _, _, got in pieces[:n]], own_outer[:1], marks[-2:-1])
+    waits = ([got for _, _, got in pieces[:n]], own_outer[:1], marks[-2:-1], marks[-1:])
     grad = sum_over_pix([grad_inner, grad_outer], size, waits, rows * size * total)
     weight_grad = grad.reshape(nterms, nch, nin).transpose(0, 2, 1)
     return out, weight_grad

time: 67.4 us -> 65.3 us (0.969)
  starting transfers between devices: 26.8 us -> 22.8 us
  waiting for transfers between devices: 7.76 us -> 10 us
    ppermute x4, waiting for transfers between devices: 0.01 us -> 8.89 us  [chunks(): got = lax.ppermute(send, 'ch', [(i, i ^ 1) for i in range(sides)])]
    ppermute x9, waiting for transfers between devices: 5.93 us -> 1.14 us  [sum_over_pix(): lax.ppermute(value, 'pix', [(i, i ^ x * step) for i in range(size)])]
    ppermute x4, starting transfers between devices: 8.27 us -> 6.44 us  [chunks(): got = lax.ppermute(send, 'ch', [(i, i ^ 1) for i in range(sides)])]
    ppermute x2, waiting for transfers between devices: 1.82 us -> 0.01 us  [swap(): return lax.ppermute(x, 'pix', pairs + [(j, i) for i, j in pairs])]
    ppermute x9, starting transfers between devices: 12.9 us -> 11.7 us  [sum_over_pix(): lax.ppermute(value, 'pix', [(i, i ^ x * step) for i in range(size)])]
    ppermute x2, starting transfers between devices: 5.55 us -> 4.69 us  [swap(): return lax.ppermute(x, 'pix', pairs + [(j, i) for i, j in pairs])]
  transfers between devices with their start and end apart: 15 -> 15, of which waited for: 6 -> 6; matrix products, arithmetic and copies ran while one was open for 0% -> 0% of each run, Pallas kernels for 36% -> 42%
where the time goes in v3:
time: 65.3 us; the launch traced here: 65.1 us
  Pallas kernels  30.5 us (47%)
  starting transfers between devices  22.8 us (35%)
  waiting for transfers between devices  10 us (15%)
  local copies, waits for them, and re-layouts  0.94 us (1%)
  between operations  0.81 us (1%)
    pallas_call x4, Pallas kernels, chunk_terms(): pl.pallas_call(functools.partial(terms_kernel, outer, start - lo, lo, hi,...  16.3 us
    ppermute x9, starting transfers between devices, sum_over_pix(): lax.ppermute(value, 'pix', [(i, i ^ x * step) for i in range(size)])  11.7 us
    ppermute x4, waiting for transfers between devices, chunks(): got = lax.ppermute(send, 'ch', [(i, i ^ 1) for i in range(sides)])  8.89 us
    ppermute x4, starting transfers between devices, chunks(): got = lax.ppermute(send, 'ch', [(i, i ^ 1) for i in range(sides)])  6.44 us
    pallas_call x2, Pallas kernels, weights(): pl.pallas_call(functools.partial(weights_kernel, places), out_shape=jax.S...  5.43 us
    ppermute x2, starting transfers between devices, swap(): return lax.ppermute(x, 'pix', pairs + [(j, i) for i, j in pairs])  4.69 us
    pallas_call x3, Pallas kernels, finish(): pl.pallas_call(functools.partial(finish_kernel, start, width, start - inn...  3.37 us
    pallas_call x2, Pallas kernels, own_parts(): pl.pallas_call(own_kernel, out_shape=[jax.ShapeDtypeStruct((kept, *t.shap...  2.48 us
  transfers between devices with their start and end apart: 15, of which 6 were waited for; matrix products, arithmetic and copies ran while one was open for 0% of the time, Pallas kernels for 42%

profile of v3, /device:TPU:1, one launch (start us, length us, event | category | flops | bytes accessed | tf_op | source)
XLA Modules:
  0.0 65.1 jit_solution(12855503244422651819)
XLA Ops:
  0.6 2.3 %shard_map.77 = (bf16[512,1024]{1,0:T(8,128)(2,1)S(1)}, bf16[16,32,2048]{2,1,0:T(8,128)(2,1)S(1)}, f32[3,32,2048]{2,1,0:T(8,128)S(1)}, bf16[19,4,2048]{2,1,0:T(4,128)(2,1)S(1)}, bf16[19,4,2048]{2,1,0:T(4,128)(2,1)S(1)}) custom-call(bf16[4,16,32]{2,1,0:T(8,128)(2,1)} %bitcast.5, bf16[16,32,2048]{2,1,0:T(8,128)(2,1)} %g_ref.1, f32[32,2048]{1,0:T(8,128)} %east_ref.1, ...), custom_call_target="tpu_custom_call" | custom-call | flops 1 | bytes 1 | tf_op jit(solution)/shard_map/pallas_call | solution.py:85
  2.9 1.5 %collective-permute-start.1 = (bf16[19,4,2048]{2,1,0:T(4,128)(2,1)S(1)}, bf16[19,4,2048]{2,1,0:T(4,128)(2,1)S(1)}, u32[]{:S(2)}, u32[]{:S(2)}) collective-permute-start(bf16[19,4,2048]{2,1,0:T(4,128)(2,1)S(1)} %get-tuple-element.32), channel_id=1, source_target_pairs={{0,2},{4,6},{8,10},{12,14},{16,18},{20,22},{24,26},{28,30},{32,34}... | collective-permute-start | bytes 933896 | tf_op jit(solution)/shard_map/ppermute | solution.py:395
  4.4 3.2 %collective-permute-start.2 = (bf16[19,4,2048]{2,1,0:T(4,128)(2,1)S(1)}, bf16[19,4,2048]{2,1,0:T(4,128)(2,1)S(1)}, u32[]{:S(2)}, u32[]{:S(2)}) collective-permute-start(bf16[19,4,2048]{2,1,0:T(4,128)(2,1)S(1)} %get-tuple-element.33), channel_id=1, source_target_pairs={{2,4},{6,8},{10,12},{14,16},{18,20},{22,24},{26,28},{30,32},{34,36... | collective-permute-start | bytes 933896 | tf_op jit(solution)/shard_map/ppermute | solution.py:395
  7.6 2.1 %shard_map.78 = (bf16[64,16,512]{2,1,0:T(8,128)(2,1)S(1)}, bf16[16,16,512]{2,1,0:T(8,128)(2,1)S(1)}) custom-call(bf16[16,32,2048]{2,1,0:T(8,128)(2,1)S(1)} %get-tuple-element.25.refs_0_.refs_1_.refs_3_.refs_2_, f32[3,32,2048]{2,1,0:T(8,128)S(1)} %get-tuple-element.26.refs_1_.refs_2_.refs_4_.refs_3_, ...), custom_call_target="tpu_custom_call" | custom-call | flops 1 | bytes 1 | tf_op jit(solution)/shard_map/pallas_call | solution.py:205
  9.7 2.7 %collective-permute-start.3 = (bf16[16,16,512]{2,1,0:T(8,128)(2,1)S(1)}, bf16[16,16,512]{2,1,0:T(8,128)(2,1)S(1)}, u32[]{:S(2)}, u32[]{:S(2)}) collective-permute-start(bf16[16,16,512]{2,1,0:T(8,128)(2,1)S(1)} %get-tuple-element.35), channel_id=1, source_target_pairs={{0,1},{1,0},{2,3},{3,2},{4,5},{5,4},{6,7},{7,6},{8,9},{9,8},{10,11... | collective-permute-start | bytes 786440 | tf_op jit(solution)/shard_map/ppermute | solution.py:381
  12.4 5.3 %shard_map.79 = (bf16[64,16,1536]{2,1,0:T(8,128)(2,1)S(1)}, bf16[16,16,1536]{2,1,0:T(8,128)(2,1)S(1)}) custom-call(bf16[64,16,512]{2,1,0:T(8,128)(2,1)S(1)} %get-tuple-element.27.refs_0_, bf16[16,32,2048]{2,1,0:T(8,128)(2,1)S(1)} %get-tuple-element.25.refs_0_.refs_1_.refs_3_.refs_2_, f32[3,32,2048]{2,1,0:T(8,128)S(1)} %get-tuple-element.26.refs_1_.refs_2_.refs_4_.refs_3_, ...), custom_call_target="tpu_custom_call" | custom-call | flops 1 | bytes 1 | tf_op jit(solution)/shard_map/pallas_call | solution.py:205
  18.1 1.2 %shard_map.80 = (f32[16,16,512]{2,1,0:T(8,128)S(1)}, f32[16,16,1536]{2,1,0:T(8,128)S(1)}) custom-call(bf16[512,1024]{1,0:T(8,128)(2,1)S(1)} %get-tuple-element.24.refs_2_.refs_3_.mix_ref.refs_5_.refs_4_, bf16[64,16,512]{2,1,0:T(8,128)(2,1)S(1)} %get-tuple-element.27.refs_0_, bf16[64,16,1536]{2,1,0:T(8,128)(2,1)S(1)} %get-tuple-element.28.refs_1_.refs_0_), custom_call_target="tpu_custom_call" | custom-call | flops 1 | bytes 1 | tf_op jit(solution)/shard_map/pallas_call | solution.py:271
  19.3 0.9 %copy-done = bf16[32,32,2048]{2,1,0:T(8,128)(2,1)S(1)} copy-done((bf16[32,32,2048]{2,1,0:T(8,128)(2,1)S(1)}, bf16[32,32,2048]{2,1,0:T(8,128)(2,1)}, u32[]{:S(2)}) %copy-start) | copy-done | bytes 4194328
  20.2 2.7 %shard_map.81.refs_2_.refs_0_ = f32[64,32]{1,0:T(8,128)S(1)} custom-call(bf16[32,32,2048]{2,1,0:T(8,128)(2,1)S(1)} %copy-done, bf16[64,16,512]{2,1,0:T(8,128)(2,1)S(1)} %get-tuple-element.27.refs_0_, bf16[64,16,1536]{2,1,0:T(8,128)(2,1)S(1)} %get-tuple-element.28.refs_1_.refs_0_), custom_call_target="tpu_custom_call" | custom-call | flops 1 | bytes 1 | tf_op jit(solution)/shard_map/pallas_call | solution.py:249
  23.0 4.5 %shard_map.82 = (bf16[64,16,1024]{2,1,0:T(8,128)(2,1)S(1)}, bf16[16,16,1024]{2,1,0:T(8,128)(2,1)S(1)}) custom-call(bf16[64,16,1536]{2,1,0:T(8,128)(2,1)S(1)} %get-tuple-element.28.refs_1_.refs_0_, f32[16,16,512]{2,1,0:T(8,128)S(1)} %get-tuple-element.31.refs_1_.own_i, f32[64,32]{1,0:T(8,128)S(1)} %shard_map.81.refs_2_.refs_0_, ...), custom_call_target="tpu_custom_call" | custom-call | flops 1 | bytes 1 | tf_op jit(solution)/shard_map/pallas_call | solution.py:205
  27.5 2.7 %collective-permute-start.5 = (bf16[16,16,1024]{2,1,0:T(8,128)(2,1)S(1)}, bf16[16,16,1024]{2,1,0:T(8,128)(2,1)S(1)}, u32[]{:S(2)}, u32[]{:S(2)}) collective-permute-start(bf16[16,16,1024]{2,1,0:T(8,128)(2,1)S(1)} %get-tuple-element.40), channel_id=1, source_target_pairs={{0,1},{1,0},{2,3},{3,2},{4,5},{5,4},{6,7},{7,6},{8,9},{9,8},{10,11... | collective-permute-start | bytes 1572872 | tf_op jit(solution)/shard_map/ppermute | solution.py:381
  30.2 4.5 %shard_map.83 = (bf16[64,16,1024]{2,1,0:T(8,128)(2,1)S(1)}, bf16[16,16,1024]{2,1,0:T(8,128)(2,1)S(1)}) custom-call(bf16[64,16,1024]{2,1,0:T(8,128)(2,1)S(1)} %get-tuple-element.34.refs_0_, bf16[16,16,512]{2,1,0:T(8,128)(2,1)S(1)} %collective-permute-done.3.refs_1_.got_i.refs_2_, bf16[16,32,2048]{2,1,0:T(8,128)(2,1)S(1)} %get-tuple-element.25.refs_0_.refs_1_.refs_3_.refs_2_, ...), custom_call_target="tpu_custom_call" | custom-call | flops 10000000000 | bytes 100000000 | tf_op jit(solution)/shard_map/pallas_call | solution.py:205
  35.3 2.7 %shard_map.88.refs_1_ = f32[64,32]{1,0:T(8,128)S(1)} custom-call(bf16[32,32,2048]{2,1,0:T(8,128)(2,1)S(1)} %copy-done, bf16[64,16,1024]{2,1,0:T(8,128)(2,1)S(1)} %get-tuple-element.34.refs_0_, bf16[64,16,1024]{2,1,0:T(8,128)(2,1)S(1)} %get-tuple-element.36.refs_1_), custom_call_target="tpu_custom_call" | custom-call | flops 1 | bytes 1 | tf_op jit(solution)/shard_map/pallas_call | solution.py:249
  38.1 5.4 %collective-permute-done.got_i.refs_3_ = bf16[16,16,1536]{2,1,0:T(8,128)(2,1)S(1)} collective-permute-done((bf16[16,16,1536]{2,1,0:T(8,128)(2,1)S(1)}, bf16[16,16,1536]{2,1,0:T(8,128)(2,1)S(1)}, u32[]{:S(2)}, u32[]{:S(2)}) %collective-permute-start) | collective-permute-done | bytes 786464 | tf_op jit(solution)/shard_map/ppermute | solution.py:381
  44.1 2.7 %collective-permute-start.6 = (f32[64,32]{1,0:T(8,128)S(1)}, f32[64,32]{1,0:T(8,128)S(1)}, u32[]{:S(2)}, u32[]{:S(2)}) collective-permute-start(f32[64,32]{1,0:T(8,128)S(1)} %shard_map.89.refs_0_), channel_id=1, source_target_pairs={{0,8},{2,10},{4,12},{6,14},{8,0},{10,2},{12,4},{14,6},{16,24},{18,... | collective-permute-start | bytes 24584 | tf_op jit(solution)/shard_map/ppermute | solution.py:353
  46.8 1.2 %shard_map.84 = (f32[16,16,1024]{2,1,0:T(8,128)S(1)}, f32[16,16,1024]{2,1,0:T(8,128)S(1)}) custom-call(bf16[512,1024]{1,0:T(8,128)(2,1)S(1)} %get-tuple-element.24.refs_2_.refs_3_.mix_ref.refs_5_.refs_4_, bf16[64,16,1024]{2,1,0:T(8,128)(2,1)S(1)} %get-tuple-element.34.refs_0_, bf16[64,16,1024]{2,1,0:T(8,128)(2,1)S(1)} %get-tuple-element.36.refs_1_), custom_call_target="tpu_custom_call" | custom-call | flops 1 | bytes 1 | tf_op jit(solution)/shard_map/pallas_call | solution.py:271
  48.9 2.2 %collective-permute-start.11 = (f32[64,32]{1,0:T(8,128)S(1)}, f32[64,32]{1,0:T(8,128)S(1)}, u32[]{:S(2)}, u32[]{:S(2)}) collective-permute-start(f32[64,32]{1,0:T(8,128)S(1)} %shard_map.90.refs_0_), channel_id=1, source_target_pairs={{0,96},{2,98},{4,100},{6,102},{8,104},{10,106},{12,108},{14,110},{... | collective-permute-start | bytes 24584 | tf_op jit(solution)/shard_map/ppermute | solution.py:353
  51.6 0.6 collective-permute-start.9
  52.2 2.5 %collective-permute-done.5.got_o = bf16[16,16,1024]{2,1,0:T(8,128)(2,1)S(1)} collective-permute-done((bf16[16,16,1024]{2,1,0:T(8,128)(2,1)S(1)}, bf16[16,16,1024]{2,1,0:T(8,128)(2,1)S(1)}, u32[]{:S(2)}, u32[]{:S(2)}) %collective-permute-start.5) | collective-permute-done | bytes 524320 | tf_op jit(solution)/shard_map/ppermute | solution.py:381
  54.7 1.5 %shard_map.85 = (bf16[16,32,2048]{2,1,0:T(8,128)(2,1)}, f32[8,128]{1,0:T(8,128)}) custom-call(f32[16,16,512]{2,1,0:T(8,128)S(1)} %get-tuple-element.31.refs_1_.own_i, bf16[16,16,512]{2,1,0:T(8,128)(2,1)S(1)} %collective-permute-done.3.refs_1_.got_i.refs_2_, f32[16,16,1024]{2,1,0:T(8,128)S(1)} %get-tuple-element.39.own_o.refs_4_, ...), custom_call_target="tpu_custom_call" | custom-call | flops 1 | bytes 1 | tf_op jit(solution)/shard_map/pallas_call | solution.py:308
  56.2 0.9 %shard_map.86 = (bf16[16,32,2048]{2,1,0:T(8,128)(2,1)}, f32[8,128]{1,0:T(8,128)S(1)}) custom-call(f32[16,16,1536]{2,1,0:T(8,128)S(1)} %get-tuple-element.29.own_i, bf16[16,16,1536]{2,1,0:T(8,128)(2,1)S(1)} %collective-permute-done.got_i.refs_3_, f32[16,16,1024]{2,1,0:T(8,128)S(1)} %get-tuple-element.39.own_o.refs_4_, ...), custom_call_target="tpu_custom_call", output_to_operand_aliasing={{0}: (4, {})} | custom-call | flops 1 | bytes 1 | tf_op jit(solution)/shard_map/pallas_call | solution.py:308
  57.1 4.6 %collective-permute-start.14 = (f32[64,32]{1,0:T(8,128)S(1)}, f32[64,32]{1,0:T(8,128)S(1)}, u32[]{:S(2)}, u32[]{:S(2)}) collective-permute-start(f32[64,32]{1,0:T(8,128)S(1)} %shard_map.91.refs_0_), channel_id=1, source_target_pairs={{0,6},{2,4},{4,2},{6,0},{8,14},{10,12},{12,10},{14,8},{16,22},{18,... | collective-permute-start | bytes 24584 | tf_op jit(solution)/shard_map/ppermute | solution.py:353
  62.2 0.9 %collective-permute-done.4.got_o = bf16[16,16,1024]{2,1,0:T(8,128)(2,1)S(1)} collective-permute-done((bf16[16,16,1024]{2,1,0:T(8,128)(2,1)S(1)}, bf16[16,16,1024]{2,1,0:T(8,128)(2,1)S(1)}, u32[]{:S(2)}, u32[]{:S(2)}) %collective-permute-start.4) | collective-permute-done | bytes 524320 | tf_op jit(solution)/shard_map/ppermute | solution.py:381
  63.1 1.1 %shard_map.87 = (bf16[16,32,2048]{2,1,0:T(8,128)(2,1)}, f32[8,128]{1,0:T(8,128)S(1)}) custom-call(f32[16,16,1536]{2,1,0:T(8,128)S(1)} %get-tuple-element.29.own_i, bf16[16,16,1536]{2,1,0:T(8,128)(2,1)S(1)} %collective-permute-done.got_i.refs_3_, f32[16,16,1024]{2,1,0:T(8,128)S(1)} %get-tuple-element.37.own_o, ...), custom_call_target="tpu_custom_call", output_to_operand_aliasing={{0}: (4, {})} | custom-call | flops 1 | bytes 1 | tf_op jit(solution)/shard_map/pallas_call | solution.py:308
  (24 shorter events, 4.4 us)
Async XLA Ops:
  2.9 20.1 %collective-permute-start.1 = (bf16[19,4,2048]{2,1,0:T(4,128)(2,1)S(1)}, bf16[19,4,2048]{2,1,0:T(4,128)(2,1)S(1)}, u32[]{:S(2)}, u32[]{:S(2)}) collective-permute-start(bf16[19,4,2048]{2,1,0:T(4,128)(2,1)S(1)} %get-tuple-element.32), channel_id=1, source_target_pairs={{0,2},{4,6},{8,10},{12,14},{16,18},{20,22},{24,26},{28,30},{32,34}... | collective-permute-start | bytes 933896 | tf_op jit(solution)/shard_map/ppermute | solution.py:395
  4.4 18.6 %collective-permute-start.2 = (bf16[19,4,2048]{2,1,0:T(4,128)(2,1)S(1)}, bf16[19,4,2048]{2,1,0:T(4,128)(2,1)S(1)}, u32[]{:S(2)}, u32[]{:S(2)}) collective-permute-start(bf16[19,4,2048]{2,1,0:T(4,128)(2,1)S(1)} %get-tuple-element.33), channel_id=1, source_target_pairs={{2,4},{6,8},{10,12},{14,16},{18,20},{22,24},{26,28},{30,32},{34,36... | collective-permute-start | bytes 933896 | tf_op jit(solution)/shard_map/ppermute | solution.py:395
  9.7 20.5 %collective-permute-start.3 = (bf16[16,16,512]{2,1,0:T(8,128)(2,1)S(1)}, bf16[16,16,512]{2,1,0:T(8,128)(2,1)S(1)}, u32[]{:S(2)}, u32[]{:S(2)}) collective-permute-start(bf16[16,16,512]{2,1,0:T(8,128)(2,1)S(1)} %get-tuple-element.35), channel_id=1, source_target_pairs={{0,1},{1,0},{2,3},{3,2},{4,5},{5,4},{6,7},{7,6},{8,9},{9,8},{10,11... | collective-permute-start | bytes 786440 | tf_op jit(solution)/shard_map/ppermute | solution.py:381
  17.6 25.9 %collective-permute-start = (bf16[16,16,1536]{2,1,0:T(8,128)(2,1)S(1)}, bf16[16,16,1536]{2,1,0:T(8,128)(2,1)S(1)}, u32[]{:S(2)}, u32[]{:S(2)}) collective-permute-start(bf16[16,16,1536]{2,1,0:T(8,128)(2,1)S(1)} %get-tuple-element.30), channel_id=1, source_target_pairs={{0,1},{1,0},{2,3},{3,2},{4,5},{5,4},{6,7},{7,6},{8,9},{9,8},{10,11... | collective-permute-start | bytes 2359304 | tf_op jit(solution)/shard_map/ppermute | solution.py:381
  18.1 2.2 %copy-start = (bf16[32,32,2048]{2,1,0:T(8,128)(2,1)S(1)}, bf16[32,32,2048]{2,1,0:T(8,128)(2,1)}, u32[]{:S(2)}) copy-start(bf16[32,32,2048]{2,1,0:T(8,128)(2,1)} %f_ref.3) | copy-start | bytes 12582916
  27.5 27.2 %collective-permute-start.5 = (bf16[16,16,1024]{2,1,0:T(8,128)(2,1)S(1)}, bf16[16,16,1024]{2,1,0:T(8,128)(2,1)S(1)}, u32[]{:S(2)}, u32[]{:S(2)}) collective-permute-start(bf16[16,16,1024]{2,1,0:T(8,128)(2,1)S(1)} %get-tuple-element.40), channel_id=1, source_target_pairs={{0,1},{1,0},{2,3},{3,2},{4,5},{5,4},{6,7},{7,6},{8,9},{9,8},{10,11... | collective-permute-start | bytes 1572872 | tf_op jit(solution)/shard_map/ppermute | solution.py:381
  34.7 28.4 %collective-permute-start.4 = (bf16[16,16,1024]{2,1,0:T(8,128)(2,1)S(1)}, bf16[16,16,1024]{2,1,0:T(8,128)(2,1)S(1)}, u32[]{:S(2)}, u32[]{:S(2)}) collective-permute-start(bf16[16,16,1024]{2,1,0:T(8,128)(2,1)S(1)} %get-tuple-element.38), channel_id=1, source_target_pairs={{0,1},{1,0},{2,3},{3,2},{4,5},{5,4},{6,7},{7,6},{8,9},{9,8},{10,11... | collective-permute-start | bytes 1572872 | tf_op jit(solution)/shard_map/ppermute | solution.py:381
  43.5 4.5 %collective-permute-start.8 = (f32[64,32]{1,0:T(8,128)S(1)}, f32[64,32]{1,0:T(8,128)S(1)}, u32[]{:S(2)}, u32[]{:S(2)}) collective-permute-start(f32[64,32]{1,0:T(8,128)S(1)} %shard_map.89.refs_0_), channel_id=1, source_target_pairs={{0,24},{2,26},{4,28},{6,30},{8,16},{10,18},{12,20},{14,22},{16,8},... | collective-permute-start | bytes 24584 | tf_op jit(solution)/shard_map/ppermute | solution.py:353
  43.9 4.6 %collective-permute-start.7 = (f32[64,32]{1,0:T(8,128)S(1)}, f32[64,32]{1,0:T(8,128)S(1)}, u32[]{:S(2)}, u32[]{:S(2)}) collective-permute-start(f32[64,32]{1,0:T(8,128)S(1)} %shard_map.89.refs_0_), channel_id=1, source_target_pairs={{0,16},{2,18},{4,20},{6,22},{8,24},{10,26},{12,28},{14,30},{16,0},... | collective-permute-start | bytes 24584 | tf_op jit(solution)/shard_map/ppermute | solution.py:353
  44.1 4.8 %collective-permute-start.6 = (f32[64,32]{1,0:T(8,128)S(1)}, f32[64,32]{1,0:T(8,128)S(1)}, u32[]{:S(2)}, u32[]{:S(2)}) collective-permute-start(f32[64,32]{1,0:T(8,128)S(1)} %shard_map.89.refs_0_), channel_id=1, source_target_pairs={{0,8},{2,10},{4,12},{6,14},{8,0},{10,2},{12,4},{14,6},{16,24},{18,... | collective-permute-start | bytes 24584 | tf_op jit(solution)/shard_map/ppermute | solution.py:353
  48.9 8.2 %collective-permute-start.11 = (f32[64,32]{1,0:T(8,128)S(1)}, f32[64,32]{1,0:T(8,128)S(1)}, u32[]{:S(2)}, u32[]{:S(2)}) collective-permute-start(f32[64,32]{1,0:T(8,128)S(1)} %shard_map.90.refs_0_), channel_id=1, source_target_pairs={{0,96},{2,98},{4,100},{6,102},{8,104},{10,106},{12,108},{14,110},{... | collective-permute-start | bytes 24584 | tf_op jit(solution)/shard_map/ppermute | solution.py:353
  51.0 6.0 %collective-permute-start.10 = (f32[64,32]{1,0:T(8,128)S(1)}, f32[64,32]{1,0:T(8,128)S(1)}, u32[]{:S(2)}, u32[]{:S(2)}) collective-permute-start(f32[64,32]{1,0:T(8,128)S(1)} %shard_map.90.refs_0_), channel_id=1, source_target_pairs={{0,64},{2,66},{4,68},{6,70},{8,72},{10,74},{12,76},{14,78},{16,80}... | collective-permute-start | bytes 24584 | tf_op jit(solution)/shard_map/ppermute | solution.py:353
  51.6 5.5 %collective-permute-start.9 = (f32[64,32]{1,0:T(8,128)S(1)}, f32[64,32]{1,0:T(8,128)S(1)}, u32[]{:S(2)}, u32[]{:S(2)}) collective-permute-start(f32[64,32]{1,0:T(8,128)S(1)} %shard_map.90.refs_0_), channel_id=1, source_target_pairs={{0,32},{2,34},{4,36},{6,38},{8,40},{10,42},{12,44},{14,46},{16,48}... | collective-permute-start | bytes 24584 | tf_op jit(solution)/shard_map/ppermute | solution.py:353
  57.1 7.1 %collective-permute-start.14 = (f32[64,32]{1,0:T(8,128)S(1)}, f32[64,32]{1,0:T(8,128)S(1)}, u32[]{:S(2)}, u32[]{:S(2)}) collective-permute-start(f32[64,32]{1,0:T(8,128)S(1)} %shard_map.91.refs_0_), channel_id=1, source_target_pairs={{0,6},{2,4},{4,2},{6,0},{8,14},{10,12},{12,10},{14,8},{16,22},{18,... | collective-permute-start | bytes 24584 | tf_op jit(solution)/shard_map/ppermute | solution.py:353
  61.7 2.8 %collective-permute-start.13 = (f32[64,32]{1,0:T(8,128)S(1)}, f32[64,32]{1,0:T(8,128)S(1)}, u32[]{:S(2)}, u32[]{:S(2)}) collective-permute-start(f32[64,32]{1,0:T(8,128)S(1)} %shard_map.91.refs_0_), channel_id=1, source_target_pairs={{0,4},{2,6},{4,0},{6,2},{8,12},{10,14},{12,8},{14,10},{16,20},{18,... | collective-permute-start | bytes 24584 | tf_op jit(solution)/shard_map/ppermute | solution.py:353
  61.7 2.8 %collective-permute-start.12 = (f32[64,32]{1,0:T(8,128)S(1)}, f32[64,32]{1,0:T(8,128)S(1)}, u32[]{:S(2)}, u32[]{:S(2)}) collective-permute-start(f32[64,32]{1,0:T(8,128)S(1)} %shard_map.91.refs_0_), channel_id=1, source_target_pairs={{0,2},{2,0},{4,6},{6,4},{8,10},{10,8},{12,14},{14,12},{16,18},{18,... | collective-permute-start | bytes 24584 | tf_op jit(solution)/shard_map/ppermute | solution.py:353

commit v4 on v3

--- a/solution.py
+++ b/solution.py
@@ -14,6 +14,7 @@
 INNER = (512, 1536)
 OUTER = (1024, 1024)
 UNIT = 256
+NEED = 3
 ANY = pl.BlockSpec(memory_space=pl.ANY)
 HBM = pl.BlockSpec(memory_space=pltpu.HBM)
 VMEM = pl.BlockSpec(memory_space=pltpu.VMEM)
@@ -32,9 +33,16 @@
     return lax.broadcasted_iota(jnp.int32, shape, dim)
 
 
+def dense_rows(n, nch):
+    if n < nch:
+        return n * NEED, NEED
+    before = nch * NEED
+    return (before, NEED - 1) if n == nch else (before + (n - nch) * NEED - 1, NEED)
+
+
 def prepare_kernel(
     sides, w_hbm, g_ref, east_ref, south_ref, mask_ref,
-    mix_ref, g_out, maps_out, partner_ref, other_ref, mask_buf, w_ref, sems,
+    mix_ref, g_out, maps_out, partner_ref, other_ref, mask_buf, w_ref, dense, sems,
 ):
     copies = [
         pltpu.make_async_copy(src, dst, sems.at[n])
@@ -72,15 +80,19 @@
     even = lax.axis_index("pix") % 2 == 0
     for o in range(nch + 3):
         x = g_out[o].astype(F32) if o < nch else maps_out[o - nch]
-        top, bottom = x[:HALO].astype(BF16), x[height - TILE :][TILE - HALO :].astype(BF16)
-        partner_ref[o] = jnp.where(even, bottom, top)
-        other_ref[o] = jnp.where(even, top, bottom)
+        head, tail = x[:TILE], x[height - TILE :]
+        partner = jnp.where(even, tail[TILE - HALO :], head[:HALO])
+        partner_ref[o] = partner.astype(BF16)
+        at, count = dense_rows(o, nch)
+        other = jnp.where(even, head, pltpu.roll(tail, count, 0))
+        dense[at : at + count] = other[:count]
+    other_ref[...] = dense[...].astype(BF16)
 
 
 def prepare(w, g, east, south, mask, sides):
     nterms, nin, nout = w.shape
     nch, rows, total = g.shape
-    edge = jax.ShapeDtypeStruct((nch + 3, HALO, total), BF16)
+    dense = (nch + 3) * NEED - 1
     args = (w.transpose(0, 2, 1), g, east, south, mask)
     return pl.pallas_call(
         functools.partial(prepare_kernel, sides),
@@ -88,14 +100,15 @@
             jax.ShapeDtypeStruct((nin * SUB, nterms * nout * SUB), BF16),
             jax.ShapeDtypeStruct(g.shape, g.dtype),
             jax.ShapeDtypeStruct((3, rows, total), F32),
-            edge,
-            edge,
+            jax.ShapeDtypeStruct((nch + 3, HALO, total), BF16),
+            jax.ShapeDtypeStruct((dense, total), BF16),
         ),
         in_specs=[HBM] * 5,
         out_specs=[VMEM] * 5,
         scratch_shapes=[
             pltpu.VMEM((rows, total), jnp.int32),
             pltpu.VMEM((nterms, nout, nin), BF16),
+            pltpu.VMEM((dense, total), F32),
             pltpu.SemaphoreType.DMA((5,)),
         ],
         compiler_params=params(12),
@@ -111,12 +124,12 @@
     )
 
 
-def outer_rows(x, below, above):
+def outer_rows(x, beside):
     rows = x.shape[0]
     low = iota((TILE, x.shape[1]), 0) < HALO
     return jnp.concatenate(
         [
-            x[rows - TILE :], below, above, x[:TILE],
+            x[rows - TILE :], beside, x[:TILE],
             jnp.where(low, x[TILE : 2 * TILE], x[rows - 2 * TILE : rows - TILE]),
         ],
         axis=0,
@@ -126,20 +139,30 @@
 def terms_kernel(outer, off, lo, hi, nterms, waits, *refs):
     g_ref, maps_ref, mix_ref = refs[waits : waits + 3]
     partner_ref, other_ref = refs[waits + 3 : waits + 5] if outer else (None, None)
-    even = lax.axis_index("pix") % 2 == 0
-    terms_ref, send_ref, w_buf = refs[-3:]
+    (terms_ref, send_ref, w_buf), tiles = refs[-5:-2] if outer else refs[-3:], refs[-1]
     nch = g_ref.shape[0]
     ext, span = w_buf.shape[1:]
     width = terms_ref.shape[2]
     cols = slice(lo, hi)
+    if outer:
+        below = 1 - lax.axis_index("pix") % 2
+        side = (iota((TILE, span), 0) < HALO).astype(jnp.int32)
+        dense = refs[-2]
+        count = dense.shape[0] - 2 * TILE
+        dense[:TILE] = jnp.zeros((TILE, span), F32)
+        dense[TILE : TILE + count] = other_ref[:, cols].astype(F32)
+        dense[TILE + count :] = jnp.zeros((TILE, span), F32)
+        for n in range(nch + 3):
+            at, many = dense_rows(n, nch)
+            last, first = dense[at + many : at + many + TILE], dense[TILE + at : 2 * TILE + at]
+            tiles[n] = jnp.where(below == 1, last, first)
 
     def arrange(x, n):
         x = x.astype(F32)
         if outer:
             partner = partner_ref[n, :, cols].astype(F32)
-            other = other_ref[n, :, cols].astype(F32)
-            below, above = jnp.where(even, partner, other), jnp.where(even, other, partner)
-            return outer_rows(x, below, above)
+            partner = jnp.concatenate([partner, partner], axis=0)
+            return outer_rows(x, jnp.where(side == below, partner, tiles[n]))
         return inner_rows(x)
 
     ew = arrange(maps_ref[0, :, cols], nch)
@@ -202,6 +225,12 @@
     nch, rows, total = g.shape
     lo, hi = max(0, start - SIDE), min(total, start + width + SIDE)
     ext = 4 * TILE if outer else 3 * TILE
+    halo = []
+    if outer:
+        halo = [
+            pltpu.VMEM((beside[1].shape[0] + 2 * TILE, hi - lo), F32),
+            pltpu.VMEM((nch + 3, TILE, hi - lo), F32),
+        ]
     return pl.pallas_call(
         functools.partial(terms_kernel, outer, start - lo, lo, hi, nterms, len(waits)),
         out_shape=(
@@ -210,7 +239,7 @@
         ),
         in_specs=[ANY] * len(waits) + [VMEM] * (3 + len(beside)),
         out_specs=(VMEM, VMEM),
-        scratch_shapes=[pltpu.VMEM((4, ext, hi - lo), F32)],
+        scratch_shapes=[pltpu.VMEM((4, ext, hi - lo), F32)] + halo,
         compiler_params=params(20),
         cost_estimate=cost,
     )(*waits, g, maps, mix, *beside)

time: 65.3 us -> 63.7 us (0.975)
  waiting for transfers between devices: 10 us -> 5.41 us
  starting transfers between devices: 22.8 us -> 25.4 us
    ppermute x4, waiting for transfers between devices: 8.89 us -> 0.71 us  [chunks(): got = lax.ppermute(send, 'ch', [(i, i ^ 1) for i in range(sides)])]
    ppermute x9, waiting for transfers between devices: 1.14 us -> 4.7 us  [sum_over_pix(): lax.ppermute(value, 'pix', [(i, i ^ x * step) for i in range(size)])]
    ppermute x9, starting transfers between devices: 11.7 us -> 13.4 us  [sum_over_pix(): lax.ppermute(value, 'pix', [(i, i ^ x * step) for i in range(size)])]
    ppermute x4, starting transfers between devices: 6.44 us -> 8.03 us  [chunks(): got = lax.ppermute(send, 'ch', [(i, i ^ 1) for i in range(sides)])]
    ppermute x2, starting transfers between devices: 4.69 us -> 3.98 us  [swap(): return lax.ppermute(x, 'pix', pairs + [(j, i) for i, j in pairs])]
  transfers between devices with their start and end apart: 15 -> 15, of which waited for: 6 -> 4; matrix products, arithmetic and copies ran while one was open for 0% -> 0% of each run, Pallas kernels for 42% -> 44%
where the time goes in v4:
time: 63.7 us; the launch traced here: 63.5 us
  Pallas kernels  30.9 us (49%)
  starting transfers between devices  25.4 us (40%)
  waiting for transfers between devices  5.41 us (8%)
  local copies, waits for them, and re-layouts  0.94 us (1%)
  between operations  0.81 us (1%)
    pallas_call x4, Pallas kernels, chunk_terms(): pl.pallas_call(functools.partial(terms_kernel, outer, start - lo, lo, hi,...  16.7 us
    ppermute x9, starting transfers between devices, sum_over_pix(): lax.ppermute(value, 'pix', [(i, i ^ x * step) for i in range(size)])  13.4 us
    ppermute x4, starting transfers between devices, chunks(): got = lax.ppermute(send, 'ch', [(i, i ^ 1) for i in range(sides)])  8.03 us
    pallas_call x2, Pallas kernels, weights(): pl.pallas_call(functools.partial(weights_kernel, places), out_shape=jax.S...  5.43 us
    ppermute x9, waiting for transfers between devices, sum_over_pix(): lax.ppermute(value, 'pix', [(i, i ^ x * step) for i in range(size)])  4.7 us
    ppermute x2, starting transfers between devices, swap(): return lax.ppermute(x, 'pix', pairs + [(j, i) for i, j in pairs])  3.98 us
    pallas_call x3, Pallas kernels, finish(): pl.pallas_call(functools.partial(finish_kernel, start, width, start - inn...  3.37 us
    pallas_call x2, Pallas kernels, own_parts(): pl.pallas_call(own_kernel, out_shape=[jax.ShapeDtypeStruct((kept, *t.shap...  2.48 us
  transfers between devices with their start and end apart: 15, of which 4 were waited for; matrix products, arithmetic and copies ran while one was open for 0% of the time, Pallas kernels for 44%

profile of v4, /device:TPU:1, one launch (start us, length us, event | category | flops | bytes accessed | tf_op | source)
XLA Modules:
  0.0 63.5 jit_solution(4875186993005183116)
XLA Ops:
  0.6 2.3 %shard_map.77 = (bf16[512,1024]{1,0:T(8,128)(2,1)S(1)}, bf16[16,32,2048]{2,1,0:T(8,128)(2,1)S(1)}, f32[3,32,2048]{2,1,0:T(8,128)S(1)}, bf16[19,4,2048]{2,1,0:T(4,128)(2,1)S(1)}, bf16[56,2048]{1,0:T(8,128)(2,1)S(1)}) custom-call(bf16[4,16,32]{2,1,0:T(8,128)(2,1)} %bitcast.5, bf16[16,32,2048]{2,1,0:T(8,128)(2,1)} %g_ref.1, f32[32,2048]{1,0:T(8,128)} %east_ref.1, ...), custom_call_target="tpu_custom_call" | custom-call | flops 1 | bytes 1 | tf_op jit(solution)/shard_map/pallas_call | solution.py:97
  2.9 1.5 %collective-permute-start.1 = (bf16[19,4,2048]{2,1,0:T(4,128)(2,1)S(1)}, bf16[19,4,2048]{2,1,0:T(4,128)(2,1)S(1)}, u32[]{:S(2)}, u32[]{:S(2)}) collective-permute-start(bf16[19,4,2048]{2,1,0:T(4,128)(2,1)S(1)} %get-tuple-element.32), channel_id=1, source_target_pairs={{0,2},{4,6},{8,10},{12,14},{16,18},{20,22},{24,26},{28,30},{32,34}... | collective-permute-start | bytes 933896 | tf_op jit(solution)/shard_map/ppermute | solution.py:424
  4.4 2.1 %shard_map.78 = (bf16[64,16,512]{2,1,0:T(8,128)(2,1)S(1)}, bf16[16,16,512]{2,1,0:T(8,128)(2,1)S(1)}) custom-call(bf16[16,32,2048]{2,1,0:T(8,128)(2,1)S(1)} %get-tuple-element.25.refs_0_.refs_1_.refs_3_.refs_2_, f32[3,32,2048]{2,1,0:T(8,128)S(1)} %get-tuple-element.26.refs_1_.refs_2_.refs_4_.refs_3_, ...), custom_call_target="tpu_custom_call" | custom-call | flops 1 | bytes 1 | tf_op jit(solution)/shard_map/pallas_call | solution.py:234
  6.5 3.1 %collective-permute-start.3 = (bf16[16,16,512]{2,1,0:T(8,128)(2,1)S(1)}, bf16[16,16,512]{2,1,0:T(8,128)(2,1)S(1)}, u32[]{:S(2)}, u32[]{:S(2)}) collective-permute-start(bf16[16,16,512]{2,1,0:T(8,128)(2,1)S(1)} %get-tuple-element.35), channel_id=1, source_target_pairs={{0,1},{1,0},{2,3},{3,2},{4,5},{5,4},{6,7},{7,6},{8,9},{9,8},{10,11... | collective-permute-start | bytes 786440 | tf_op jit(solution)/shard_map/ppermute | solution.py:410
  9.6 2.5 %collective-permute-start.2 = (bf16[56,2048]{1,0:T(8,128)(2,1)S(1)}, bf16[56,2048]{1,0:T(8,128)(2,1)S(1)}, u32[]{:S(2)}, u32[]{:S(2)}) collective-permute-start(bf16[56,2048]{1,0:T(8,128)(2,1)S(1)} %get-tuple-element.33), channel_id=1, source_target_pairs={{2,4},{6,8},{10,12},{14,16},{18,20},{22,24},{26,28},{30,32},{34,36... | collective-permute-start | bytes 688136 | tf_op jit(solution)/shard_map/ppermute | solution.py:424
  12.0 5.3 %shard_map.79 = (bf16[64,16,1536]{2,1,0:T(8,128)(2,1)S(1)}, bf16[16,16,1536]{2,1,0:T(8,128)(2,1)S(1)}) custom-call(bf16[64,16,512]{2,1,0:T(8,128)(2,1)S(1)} %get-tuple-element.27.refs_0_, bf16[16,32,2048]{2,1,0:T(8,128)(2,1)S(1)} %get-tuple-element.25.refs_0_.refs_1_.refs_3_.refs_2_, f32[3,32,2048]{2,1,0:T(8,128)S(1)} %get-tuple-element.26.refs_1_.refs_2_.refs_4_.refs_3_, ...), custom_call_target="tpu_custom_call" | custom-call | flops 1 | bytes 1 | tf_op jit(solution)/shard_map/pallas_call | solution.py:234
  17.3 1.6 %collective-permute-start = (bf16[16,16,1536]{2,1,0:T(8,128)(2,1)S(1)}, bf16[16,16,1536]{2,1,0:T(8,128)(2,1)S(1)}, u32[]{:S(2)}, u32[]{:S(2)}) collective-permute-start(bf16[16,16,1536]{2,1,0:T(8,128)(2,1)S(1)} %get-tuple-element.30), channel_id=1, source_target_pairs={{0,1},{1,0},{2,3},{3,2},{4,5},{5,4},{6,7},{7,6},{8,9},{9,8},{10,11... | collective-permute-start | bytes 2359304 | tf_op jit(solution)/shard_map/ppermute | solution.py:410
  19.0 1.2 %shard_map.80 = (f32[16,16,512]{2,1,0:T(8,128)S(1)}, f32[16,16,1536]{2,1,0:T(8,128)S(1)}) custom-call(bf16[512,1024]{1,0:T(8,128)(2,1)S(1)} %get-tuple-element.24.refs_2_.refs_3_.mix_ref.refs_5_.refs_4_, bf16[64,16,512]{2,1,0:T(8,128)(2,1)S(1)} %get-tuple-element.27.refs_0_, bf16[64,16,1536]{2,1,0:T(8,128)(2,1)S(1)} %get-tuple-element.28.refs_1_.refs_0_), custom_call_target="tpu_custom_call" | custom-call | flops 1 | bytes 1 | tf_op jit(solution)/shard_map/pallas_call | solution.py:300
  20.2 0.9 %copy-done = bf16[32,32,2048]{2,1,0:T(8,128)(2,1)S(1)} copy-done((bf16[32,32,2048]{2,1,0:T(8,128)(2,1)S(1)}, bf16[32,32,2048]{2,1,0:T(8,128)(2,1)}, u32[]{:S(2)}) %copy-start) | copy-done | bytes 4194328
  21.1 2.7 %shard_map.81.refs_2_.refs_0_ = f32[64,32]{1,0:T(8,128)S(1)} custom-call(bf16[32,32,2048]{2,1,0:T(8,128)(2,1)S(1)} %copy-done, bf16[64,16,512]{2,1,0:T(8,128)(2,1)S(1)} %get-tuple-element.27.refs_0_, bf16[64,16,1536]{2,1,0:T(8,128)(2,1)S(1)} %get-tuple-element.28.refs_1_.refs_0_), custom_call_target="tpu_custom_call" | custom-call | flops 1 | bytes 1 | tf_op jit(solution)/shard_map/pallas_call | solution.py:278
  23.9 4.7 %shard_map.82 = (bf16[64,16,1024]{2,1,0:T(8,128)(2,1)S(1)}, bf16[16,16,1024]{2,1,0:T(8,128)(2,1)S(1)}) custom-call(bf16[64,16,1536]{2,1,0:T(8,128)(2,1)S(1)} %get-tuple-element.28.refs_1_.refs_0_, f32[16,16,512]{2,1,0:T(8,128)S(1)} %get-tuple-element.31.refs_1_.own_i, f32[64,32]{1,0:T(8,128)S(1)} %shard_map.81.refs_2_.refs_0_, ...), custom_call_target="tpu_custom_call" | custom-call | flops 1 | bytes 1 | tf_op jit(solution)/shard_map/pallas_call | solution.py:234
  28.6 1.5 %collective-permute-start.5 = (bf16[16,16,1024]{2,1,0:T(8,128)(2,1)S(1)}, bf16[16,16,1024]{2,1,0:T(8,128)(2,1)S(1)}, u32[]{:S(2)}, u32[]{:S(2)}) collective-permute-start(bf16[16,16,1024]{2,1,0:T(8,128)(2,1)S(1)} %get-tuple-element.40), channel_id=1, source_target_pairs={{0,1},{1,0},{2,3},{3,2},{4,5},{5,4},{6,7},{7,6},{8,9},{9,8},{10,11... | collective-permute-start | bytes 1572872 | tf_op jit(solution)/shard_map/ppermute | solution.py:410
  30.1 4.7 %shard_map.83 = (bf16[64,16,1024]{2,1,0:T(8,128)(2,1)S(1)}, bf16[16,16,1024]{2,1,0:T(8,128)(2,1)S(1)}) custom-call(bf16[64,16,1024]{2,1,0:T(8,128)(2,1)S(1)} %get-tuple-element.34.refs_0_, bf16[16,16,512]{2,1,0:T(8,128)(2,1)S(1)} %collective-permute-done.3.refs_1_.got_i.refs_2_, bf16[16,32,2048]{2,1,0:T(8,128)(2,1)S(1)} %get-tuple-element.25.refs_0_.refs_1_.refs_3_.refs_2_, ...), custom_call_target="tpu_custom_call" | custom-call | flops 10000000000 | bytes 100000000 | tf_op jit(solution)/shard_map/pallas_call | solution.py:234
  34.7 1.8 %collective-permute-start.4 = (bf16[16,16,1024]{2,1,0:T(8,128)(2,1)S(1)}, bf16[16,16,1024]{2,1,0:T(8,128)(2,1)S(1)}, u32[]{:S(2)}, u32[]{:S(2)}) collective-permute-start(bf16[16,16,1024]{2,1,0:T(8,128)(2,1)S(1)} %get-tuple-element.38), channel_id=1, source_target_pairs={{0,1},{1,0},{2,3},{3,2},{4,5},{5,4},{6,7},{7,6},{8,9},{9,8},{10,11... | collective-permute-start | bytes 1572872 | tf_op jit(solution)/shard_map/ppermute | solution.py:410
  36.6 2.7 %shard_map.88.refs_1_ = f32[64,32]{1,0:T(8,128)S(1)} custom-call(bf16[32,32,2048]{2,1,0:T(8,128)(2,1)S(1)} %copy-done, bf16[64,16,1024]{2,1,0:T(8,128)(2,1)S(1)} %get-tuple-element.34.refs_0_, bf16[64,16,1024]{2,1,0:T(8,128)(2,1)S(1)} %get-tuple-element.36.refs_1_), custom_call_target="tpu_custom_call" | custom-call | flops 1 | bytes 1 | tf_op jit(solution)/shard_map/pallas_call | solution.py:278
  39.3 3.8 %collective-permute-start.8 = (f32[64,32]{1,0:T(8,128)S(1)}, f32[64,32]{1,0:T(8,128)S(1)}, u32[]{:S(2)}, u32[]{:S(2)}) collective-permute-start(f32[64,32]{1,0:T(8,128)S(1)} %shard_map.89.refs_0_), channel_id=1, source_target_pairs={{0,24},{2,26},{4,28},{6,30},{8,16},{10,18},{12,20},{14,22},{16,8},... | collective-permute-start | bytes 24584 | tf_op jit(solution)/shard_map/ppermute | solution.py:382
  43.8 1.2 %shard_map.84 = (f32[16,16,1024]{2,1,0:T(8,128)S(1)}, f32[16,16,1024]{2,1,0:T(8,128)S(1)}) custom-call(bf16[512,1024]{1,0:T(8,128)(2,1)S(1)} %get-tuple-element.24.refs_2_.refs_3_.mix_ref.refs_5_.refs_4_, bf16[64,16,1024]{2,1,0:T(8,128)(2,1)S(1)} %get-tuple-element.34.refs_0_, bf16[64,16,1024]{2,1,0:T(8,128)(2,1)S(1)} %get-tuple-element.36.refs_1_), custom_call_target="tpu_custom_call" | custom-call | flops 1 | bytes 1 | tf_op jit(solution)/shard_map/pallas_call | solution.py:300
  45.1 2.6 %collective-permute-done.7.refs_2_ = f32[64,32]{1,0:T(8,128)S(1)} collective-permute-done((f32[64,32]{1,0:T(8,128)S(1)}, f32[64,32]{1,0:T(8,128)S(1)}, u32[]{:S(2)}, u32[]{:S(2)}) %collective-permute-start.7) | collective-permute-done | bytes 8224 | tf_op jit(solution)/shard_map/ppermute | solution.py:382
  47.7 3.3 %collective-permute-start.11 = (f32[64,32]{1,0:T(8,128)S(1)}, f32[64,32]{1,0:T(8,128)S(1)}, u32[]{:S(2)}, u32[]{:S(2)}) collective-permute-start(f32[64,32]{1,0:T(8,128)S(1)} %shard_map.90.refs_0_), channel_id=1, source_target_pairs={{0,96},{2,98},{4,100},{6,102},{8,104},{10,106},{12,108},{14,110},{... | collective-permute-start | bytes 24584 | tf_op jit(solution)/shard_map/ppermute | solution.py:382
  51.7 1.5 %shard_map.85 = (bf16[16,32,2048]{2,1,0:T(8,128)(2,1)}, f32[8,128]{1,0:T(8,128)}) custom-call(f32[16,16,512]{2,1,0:T(8,128)S(1)} %get-tuple-element.31.refs_1_.own_i, bf16[16,16,512]{2,1,0:T(8,128)(2,1)S(1)} %collective-permute-done.3.refs_1_.got_i.refs_2_, f32[16,16,1024]{2,1,0:T(8,128)S(1)} %get-tuple-element.39.own_o.refs_4_, ...), custom_call_target="tpu_custom_call" | custom-call | flops 1 | bytes 1 | tf_op jit(solution)/shard_map/pallas_call | solution.py:337
  53.1 0.9 %shard_map.86 = (bf16[16,32,2048]{2,1,0:T(8,128)(2,1)}, f32[8,128]{1,0:T(8,128)S(1)}) custom-call(f32[16,16,1536]{2,1,0:T(8,128)S(1)} %get-tuple-element.29.own_i, bf16[16,16,1536]{2,1,0:T(8,128)(2,1)S(1)} %collective-permute-done.got_i.refs_3_, f32[16,16,1024]{2,1,0:T(8,128)S(1)} %get-tuple-element.39.own_o.refs_4_, ...), custom_call_target="tpu_custom_call", output_to_operand_aliasing={{0}: (4, {})} | custom-call | flops 1 | bytes 1 | tf_op jit(solution)/shard_map/pallas_call | solution.py:337
  54.0 1.6 %collective-permute-done.10.refs_2_ = f32[64,32]{1,0:T(8,128)S(1)} collective-permute-done((f32[64,32]{1,0:T(8,128)S(1)}, f32[64,32]{1,0:T(8,128)S(1)}, u32[]{:S(2)}, u32[]{:S(2)}) %collective-permute-start.10) | collective-permute-done | bytes 8224 | tf_op jit(solution)/shard_map/ppermute | solution.py:382
  55.6 4.5 %collective-permute-start.14 = (f32[64,32]{1,0:T(8,128)S(1)}, f32[64,32]{1,0:T(8,128)S(1)}, u32[]{:S(2)}, u32[]{:S(2)}) collective-permute-start(f32[64,32]{1,0:T(8,128)S(1)} %shard_map.91.refs_0_), channel_id=1, source_target_pairs={{0,6},{2,4},{4,2},{6,0},{8,14},{10,12},{12,10},{14,8},{16,22},{18,... | collective-permute-start | bytes 24584 | tf_op jit(solution)/shard_map/ppermute | solution.py:382
  61.3 1.1 %shard_map.87 = (bf16[16,32,2048]{2,1,0:T(8,128)(2,1)}, f32[8,128]{1,0:T(8,128)S(1)}) custom-call(f32[16,16,1536]{2,1,0:T(8,128)S(1)} %get-tuple-element.29.own_i, bf16[16,16,1536]{2,1,0:T(8,128)(2,1)S(1)} %collective-permute-done.got_i.refs_3_, f32[16,16,1024]{2,1,0:T(8,128)S(1)} %get-tuple-element.37.own_o, ...), custom_call_target="tpu_custom_call", output_to_operand_aliasing={{0}: (4, {})} | custom-call | flops 1 | bytes 1 | tf_op jit(solution)/shard_map/pallas_call | solution.py:337
  (24 shorter events, 3.7 us)
Async XLA Ops:
  2.9 21.0 %collective-permute-start.1 = (bf16[19,4,2048]{2,1,0:T(4,128)(2,1)S(1)}, bf16[19,4,2048]{2,1,0:T(4,128)(2,1)S(1)}, u32[]{:S(2)}, u32[]{:S(2)}) collective-permute-start(bf16[19,4,2048]{2,1,0:T(4,128)(2,1)S(1)} %get-tuple-element.32), channel_id=1, source_target_pairs={{0,2},{4,6},{8,10},{12,14},{16,18},{20,22},{24,26},{28,30},{32,34}... | collective-permute-start | bytes 933896 | tf_op jit(solution)/shard_map/ppermute | solution.py:424
  6.5 23.6 %collective-permute-start.3 = (bf16[16,16,512]{2,1,0:T(8,128)(2,1)S(1)}, bf16[16,16,512]{2,1,0:T(8,128)(2,1)S(1)}, u32[]{:S(2)}, u32[]{:S(2)}) collective-permute-start(bf16[16,16,512]{2,1,0:T(8,128)(2,1)S(1)} %get-tuple-element.35), channel_id=1, source_target_pairs={{0,1},{1,0},{2,3},{3,2},{4,5},{5,4},{6,7},{7,6},{8,9},{9,8},{10,11... | collective-permute-start | bytes 786440 | tf_op jit(solution)/shard_map/ppermute | solution.py:410
  9.6 14.3 %collective-permute-start.2 = (bf16[56,2048]{1,0:T(8,128)(2,1)S(1)}, bf16[56,2048]{1,0:T(8,128)(2,1)S(1)}, u32[]{:S(2)}, u32[]{:S(2)}) collective-permute-start(bf16[56,2048]{1,0:T(8,128)(2,1)S(1)} %get-tuple-element.33), channel_id=1, source_target_pairs={{2,4},{6,8},{10,12},{14,16},{18,20},{22,24},{26,28},{30,32},{34,36... | collective-permute-start | bytes 688136 | tf_op jit(solution)/shard_map/ppermute | solution.py:424
  17.3 22.0 %collective-permute-start = (bf16[16,16,1536]{2,1,0:T(8,128)(2,1)S(1)}, bf16[16,16,1536]{2,1,0:T(8,128)(2,1)S(1)}, u32[]{:S(2)}, u32[]{:S(2)}) collective-permute-start(bf16[16,16,1536]{2,1,0:T(8,128)(2,1)S(1)} %get-tuple-element.30), channel_id=1, source_target_pairs={{0,1},{1,0},{2,3},{3,2},{4,5},{5,4},{6,7},{7,6},{8,9},{9,8},{10,11... | collective-permute-start | bytes 2359304 | tf_op jit(solution)/shard_map/ppermute | solution.py:410
  19.0 2.2 %copy-start = (bf16[32,32,2048]{2,1,0:T(8,128)(2,1)S(1)}, bf16[32,32,2048]{2,1,0:T(8,128)(2,1)}, u32[]{:S(2)}) copy-start(bf16[32,32,2048]{2,1,0:T(8,128)(2,1)} %f_ref.3) | copy-start | bytes 12582916
  28.6 23.1 %collective-permute-start.5 = (bf16[16,16,1024]{2,1,0:T(8,128)(2,1)S(1)}, bf16[16,16,1024]{2,1,0:T(8,128)(2,1)S(1)}, u32[]{:S(2)}, u32[]{:S(2)}) collective-permute-start(bf16[16,16,1024]{2,1,0:T(8,128)(2,1)S(1)} %get-tuple-element.40), channel_id=1, source_target_pairs={{0,1},{1,0},{2,3},{3,2},{4,5},{5,4},{6,7},{7,6},{8,9},{9,8},{10,11... | collective-permute-start | bytes 1572872 | tf_op jit(solution)/shard_map/ppermute | solution.py:410
  34.7 26.5 %collective-permute-start.4 = (bf16[16,16,1024]{2,1,0:T(8,128)(2,1)S(1)}, bf16[16,16,1024]{2,1,0:T(8,128)(2,1)S(1)}, u32[]{:S(2)}, u32[]{:S(2)}) collective-permute-start(bf16[16,16,1024]{2,1,0:T(8,128)(2,1)S(1)} %get-tuple-element.38), channel_id=1, source_target_pairs={{0,1},{1,0},{2,3},{3,2},{4,5},{5,4},{6,7},{7,6},{8,9},{9,8},{10,11... | collective-permute-start | bytes 1572872 | tf_op jit(solution)/shard_map/ppermute | solution.py:410
  39.3 5.8 %collective-permute-start.8 = (f32[64,32]{1,0:T(8,128)S(1)}, f32[64,32]{1,0:T(8,128)S(1)}, u32[]{:S(2)}, u32[]{:S(2)}) collective-permute-start(f32[64,32]{1,0:T(8,128)S(1)} %shard_map.89.refs_0_), channel_id=1, source_target_pairs={{0,24},{2,26},{4,28},{6,30},{8,16},{10,18},{12,20},{14,22},{16,8},... | collective-permute-start | bytes 24584 | tf_op jit(solution)/shard_map/ppermute | solution.py:382
  43.2 4.6 %collective-permute-start.7 = (f32[64,32]{1,0:T(8,128)S(1)}, f32[64,32]{1,0:T(8,128)S(1)}, u32[]{:S(2)}, u32[]{:S(2)}) collective-permute-start(f32[64,32]{1,0:T(8,128)S(1)} %shard_map.89.refs_0_), channel_id=1, source_target_pairs={{0,16},{2,18},{4,20},{6,22},{8,24},{10,26},{12,28},{14,30},{16,0},... | collective-permute-start | bytes 24584 | tf_op jit(solution)/shard_map/ppermute | solution.py:382
  43.2 4.6 %collective-permute-start.6 = (f32[64,32]{1,0:T(8,128)S(1)}, f32[64,32]{1,0:T(8,128)S(1)}, u32[]{:S(2)}, u32[]{:S(2)}) collective-permute-start(f32[64,32]{1,0:T(8,128)S(1)} %shard_map.89.refs_0_), channel_id=1, source_target_pairs={{0,8},{2,10},{4,12},{6,14},{8,0},{10,2},{12,4},{14,6},{16,24},{18,... | collective-permute-start | bytes 24584 | tf_op jit(solution)/shard_map/ppermute | solution.py:382
  47.7 6.3 %collective-permute-start.11 = (f32[64,32]{1,0:T(8,128)S(1)}, f32[64,32]{1,0:T(8,128)S(1)}, u32[]{:S(2)}, u32[]{:S(2)}) collective-permute-start(f32[64,32]{1,0:T(8,128)S(1)} %shard_map.90.refs_0_), channel_id=1, source_target_pairs={{0,96},{2,98},{4,100},{6,102},{8,104},{10,106},{12,108},{14,110},{... | collective-permute-start | bytes 24584 | tf_op jit(solution)/shard_map/ppermute | solution.py:382
  51.0 4.6 %collective-permute-start.10 = (f32[64,32]{1,0:T(8,128)S(1)}, f32[64,32]{1,0:T(8,128)S(1)}, u32[]{:S(2)}, u32[]{:S(2)}) collective-permute-start(f32[64,32]{1,0:T(8,128)S(1)} %shard_map.90.refs_0_), channel_id=1, source_target_pairs={{0,64},{2,66},{4,68},{6,70},{8,72},{10,74},{12,76},{14,78},{16,80}... | collective-permute-start | bytes 24584 | tf_op jit(solution)/shard_map/ppermute | solution.py:382
  51.0 4.6 %collective-permute-start.9 = (f32[64,32]{1,0:T(8,128)S(1)}, f32[64,32]{1,0:T(8,128)S(1)}, u32[]{:S(2)}, u32[]{:S(2)}) collective-permute-start(f32[64,32]{1,0:T(8,128)S(1)} %shard_map.90.refs_0_), channel_id=1, source_target_pairs={{0,32},{2,34},{4,36},{6,38},{8,40},{10,42},{12,44},{14,46},{16,48}... | collective-permute-start | bytes 24584 | tf_op jit(solution)/shard_map/ppermute | solution.py:382
  55.6 6.8 %collective-permute-start.14 = (f32[64,32]{1,0:T(8,128)S(1)}, f32[64,32]{1,0:T(8,128)S(1)}, u32[]{:S(2)}, u32[]{:S(2)}) collective-permute-start(f32[64,32]{1,0:T(8,128)S(1)} %shard_map.91.refs_0_), channel_id=1, source_target_pairs={{0,6},{2,4},{4,2},{6,0},{8,14},{10,12},{12,10},{14,8},{16,22},{18,... | collective-permute-start | bytes 24584 | tf_op jit(solution)/shard_map/ppermute | solution.py:382
  60.1 2.8 %collective-permute-start.13 = (f32[64,32]{1,0:T(8,128)S(1)}, f32[64,32]{1,0:T(8,128)S(1)}, u32[]{:S(2)}, u32[]{:S(2)}) collective-permute-start(f32[64,32]{1,0:T(8,128)S(1)} %shard_map.91.refs_0_), channel_id=1, source_target_pairs={{0,4},{2,6},{4,0},{6,2},{8,12},{10,14},{12,8},{14,10},{16,20},{18,... | collective-permute-start | bytes 24584 | tf_op jit(solution)/shard_map/ppermute | solution.py:382
  60.2 2.6 %collective-permute-start.12 = (f32[64,32]{1,0:T(8,128)S(1)}, f32[64,32]{1,0:T(8,128)S(1)}, u32[]{:S(2)}, u32[]{:S(2)}) collective-permute-start(f32[64,32]{1,0:T(8,128)S(1)} %shard_map.91.refs_0_), channel_id=1, source_target_pairs={{0,2},{2,0},{4,6},{6,4},{8,10},{10,8},{12,14},{14,12},{16,18},{18,... | collective-permute-start | bytes 24584 | tf_op jit(solution)/shard_map/ppermute | solution.py:382

commit v5 on v4

--- a/solution.py
+++ b/solution.py
@@ -14,6 +14,7 @@
 INNER = (512, 1536)
 OUTER = (1024, 1024)
 UNIT = 256
+PARTS = 4
 NEED = 3
 ANY = pl.BlockSpec(memory_space=pl.ANY)
 HBM = pl.BlockSpec(memory_space=pltpu.HBM)
@@ -44,12 +45,16 @@
     sides, w_hbm, g_ref, east_ref, south_ref, mask_ref,
     mix_ref, g_out, maps_out, partner_ref, other_ref, mask_buf, w_ref, dense, sems,
 ):
+    nch = g_out.shape[0]
+    some = nch // PARTS
+    pairs = [
+        (w_hbm, w_ref), (mask_ref, mask_buf), (east_ref, maps_out.at[0]), (south_ref, maps_out.at[1]),
+    ]
+    for n in range(PARTS):
+        part = pl.ds(n * some, some)
+        pairs.append((g_ref.at[part], g_out.at[part]))
     copies = [
-        pltpu.make_async_copy(src, dst, sems.at[n])
-        for n, (src, dst) in enumerate((
-            (w_hbm, w_ref), (mask_ref, mask_buf), (east_ref, maps_out.at[0]),
-            (south_ref, maps_out.at[1]), (g_ref, g_out),
-        ))
+        pltpu.make_async_copy(src, dst, sems.at[n]) for n, (src, dst) in enumerate(pairs)
     ]
     for c in copies:
         c.start()
@@ -75,10 +80,10 @@
     east = -2.0 * maps_out[0] * mask * pltpu.roll(mask, total - 1, 1)
     maps_out[0] = jnp.where(iota(mask.shape, 1) == total - 1, 0.0, east)
     maps_out[2] = mask
-    copies[4].wait()
-    nch = g_out.shape[0]
     even = lax.axis_index("pix") % 2 == 0
     for o in range(nch + 3):
+        if o < nch and o % some == 0:
+            copies[4 + o // some].wait()
         x = g_out[o].astype(F32) if o < nch else maps_out[o - nch]
         head, tail = x[:TILE], x[height - TILE :]
         partner = jnp.where(even, tail[TILE - HALO :], head[:HALO])
@@ -109,7 +114,7 @@
             pltpu.VMEM((rows, total), jnp.int32),
             pltpu.VMEM((nterms, nout, nin), BF16),
             pltpu.VMEM((dense, total), F32),
-            pltpu.SemaphoreType.DMA((5,)),
+            pltpu.SemaphoreType.DMA((4 + PARTS,)),
         ],
         compiler_params=params(12),
         cost_estimate=COST,
@@ -405,7 +410,7 @@
             waits += [pieces[0][2]] if late else []
             terms, send = chunk_terms(
                 outer, start, width, g, maps, mix, part, nterms, beside, waits,
-                LONG if late else COST,
+                LONG if outer and not start else COST,
             )
             got = lax.ppermute(send, "ch", [(i, i ^ 1) for i in range(sides)])
             pieces.append(((outer, start, width), terms, got))

time: 63.7 us -> 63 us (0.989)
  starting transfers between devices: 25.4 us -> 24 us
  waiting for transfers between devices: 5.41 us -> 6.32 us
    ppermute x4, waiting for transfers between devices: 0.71 us -> 3.75 us  [chunks(): got = lax.ppermute(send, 'ch', [(i, i ^ 1) for i in range(sides)])]
    ppermute x9, waiting for transfers between devices: 4.7 us -> 2.57 us  [sum_over_pix(): lax.ppermute(value, 'pix', [(i, i ^ x * step) for i in range(size)])]
    ppermute x4, starting transfers between devices: 8.03 us -> 6.44 us  [chunks(): got = lax.ppermute(send, 'ch', [(i, i ^ 1) for i in range(sides)])]
    ppermute x2, starting transfers between devices: 3.98 us -> 4.69 us  [swap(): return lax.ppermute(x, 'pix', pairs + [(j, i) for i, j in pairs])]
  transfers between devices with their start and end apart: 15 -> 15, of which waited for: 4 -> 6; matrix products, arithmetic and copies ran while one was open for 0% -> 0% of each run, Pallas kernels for 44% -> 45%
where the time goes in v5:
time: 63 us; the launch traced here: 62.8 us
  Pallas kernels  30.7 us (49%)
  starting transfers between devices  24 us (38%)
  waiting for transfers between devices  6.32 us (10%)
  local copies, waits for them, and re-layouts  0.94 us (1%)
  between operations  0.79 us (1%)
    pallas_call x4, Pallas kernels, chunk_terms(): pl.pallas_call(functools.partial(terms_kernel, outer, start - lo, lo, hi,...  16.7 us
    ppermute x9, starting transfers between devices, sum_over_pix(): lax.ppermute(value, 'pix', [(i, i ^ x * step) for i in range(size)])  12.9 us
    ppermute x4, starting transfers between devices, chunks(): got = lax.ppermute(send, 'ch', [(i, i ^ 1) for i in range(sides)])  6.44 us
    pallas_call x2, Pallas kernels, weights(): pl.pallas_call(functools.partial(weights_kernel, places), out_shape=jax.S...  5.44 us
    ppermute x2, starting transfers between devices, swap(): return lax.ppermute(x, 'pix', pairs + [(j, i) for i, j in pairs])  4.69 us
    ppermute x4, waiting for transfers between devices, chunks(): got = lax.ppermute(send, 'ch', [(i, i ^ 1) for i in range(sides)])  3.75 us
    pallas_call x3, Pallas kernels, finish(): pl.pallas_call(functools.partial(finish_kernel, start, width, start - inn...  3.37 us
    ppermute x9, waiting for transfers between devices, sum_over_pix(): lax.ppermute(value, 'pix', [(i, i ^ x * step) for i in range(size)])  2.57 us
  transfers between devices with their start and end apart: 15, of which 6 were waited for; matrix products, arithmetic and copies ran while one was open for 0% of the time, Pallas kernels for 45%

profile of v5, /device:TPU:1, one launch (start us, length us, event | category | flops | bytes accessed | tf_op | source)
XLA Modules:
  0.0 62.8 jit_solution(13831600768369729516)
XLA Ops:
  0.6 2.1 %shard_map.77 = (bf16[512,1024]{1,0:T(8,128)(2,1)S(1)}, bf16[16,32,2048]{2,1,0:T(8,128)(2,1)S(1)}, f32[3,32,2048]{2,1,0:T(8,128)S(1)}, bf16[19,4,2048]{2,1,0:T(4,128)(2,1)S(1)}, bf16[56,2048]{1,0:T(8,128)(2,1)S(1)}) custom-call(bf16[4,16,32]{2,1,0:T(8,128)(2,1)} %bitcast.5, bf16[16,32,2048]{2,1,0:T(8,128)(2,1)} %g_ref.1, f32[32,2048]{1,0:T(8,128)} %east_ref.1, ...), custom_call_target="tpu_custom_call" | custom-call | flops 1 | bytes 1 | tf_op jit(solution)/shard_map/pallas_call | solution.py:102
  2.7 1.5 %collective-permute-start.1 = (bf16[19,4,2048]{2,1,0:T(4,128)(2,1)S(1)}, bf16[19,4,2048]{2,1,0:T(4,128)(2,1)S(1)}, u32[]{:S(2)}, u32[]{:S(2)}) collective-permute-start(bf16[19,4,2048]{2,1,0:T(4,128)(2,1)S(1)} %get-tuple-element.32), channel_id=1, source_target_pairs={{0,2},{4,6},{8,10},{12,14},{16,18},{20,22},{24,26},{28,30},{32,34}... | collective-permute-start | bytes 933896 | tf_op jit(solution)/shard_map/ppermute | solution.py:429
  4.2 3.2 %collective-permute-start.2 = (bf16[56,2048]{1,0:T(8,128)(2,1)S(1)}, bf16[56,2048]{1,0:T(8,128)(2,1)S(1)}, u32[]{:S(2)}, u32[]{:S(2)}) collective-permute-start(bf16[56,2048]{1,0:T(8,128)(2,1)S(1)} %get-tuple-element.33), channel_id=1, source_target_pairs={{2,4},{6,8},{10,12},{14,16},{18,20},{22,24},{26,28},{30,32},{34,36... | collective-permute-start | bytes 688136 | tf_op jit(solution)/shard_map/ppermute | solution.py:429
  7.4 2.1 %shard_map.78 = (bf16[64,16,512]{2,1,0:T(8,128)(2,1)S(1)}, bf16[16,16,512]{2,1,0:T(8,128)(2,1)S(1)}) custom-call(bf16[16,32,2048]{2,1,0:T(8,128)(2,1)S(1)} %get-tuple-element.25.refs_0_.refs_1_.refs_3_.refs_2_, f32[3,32,2048]{2,1,0:T(8,128)S(1)} %get-tuple-element.26.refs_1_.refs_2_.refs_4_.refs_3_, ...), custom_call_target="tpu_custom_call" | custom-call | flops 1 | bytes 1 | tf_op jit(solution)/shard_map/pallas_call | solution.py:239
  9.5 2.7 %collective-permute-start.3 = (bf16[16,16,512]{2,1,0:T(8,128)(2,1)S(1)}, bf16[16,16,512]{2,1,0:T(8,128)(2,1)S(1)}, u32[]{:S(2)}, u32[]{:S(2)}) collective-permute-start(bf16[16,16,512]{2,1,0:T(8,128)(2,1)S(1)} %get-tuple-element.35), channel_id=1, source_target_pairs={{0,1},{1,0},{2,3},{3,2},{4,5},{5,4},{6,7},{7,6},{8,9},{9,8},{10,11... | collective-permute-start | bytes 786440 | tf_op jit(solution)/shard_map/ppermute | solution.py:415
  12.2 5.3 %shard_map.79 = (bf16[64,16,1536]{2,1,0:T(8,128)(2,1)S(1)}, bf16[16,16,1536]{2,1,0:T(8,128)(2,1)S(1)}) custom-call(bf16[64,16,512]{2,1,0:T(8,128)(2,1)S(1)} %get-tuple-element.27.refs_0_, bf16[16,32,2048]{2,1,0:T(8,128)(2,1)S(1)} %get-tuple-element.25.refs_0_.refs_1_.refs_3_.refs_2_, f32[3,32,2048]{2,1,0:T(8,128)S(1)} %get-tuple-element.26.refs_1_.refs_2_.refs_4_.refs_3_, ...), custom_call_target="tpu_custom_call" | custom-call | flops 1 | bytes 1 | tf_op jit(solution)/shard_map/pallas_call | solution.py:239
  17.9 1.2 %shard_map.80 = (f32[16,16,512]{2,1,0:T(8,128)S(1)}, f32[16,16,1536]{2,1,0:T(8,128)S(1)}) custom-call(bf16[512,1024]{1,0:T(8,128)(2,1)S(1)} %get-tuple-element.24.refs_2_.refs_3_.mix_ref.refs_5_.refs_4_, bf16[64,16,512]{2,1,0:T(8,128)(2,1)S(1)} %get-tuple-element.27.refs_0_, bf16[64,16,1536]{2,1,0:T(8,128)(2,1)S(1)} %get-tuple-element.28.refs_1_.refs_0_), custom_call_target="tpu_custom_call" | custom-call | flops 1 | bytes 1 | tf_op jit(solution)/shard_map/pallas_call | solution.py:305
  19.1 0.9 %copy-done = bf16[32,32,2048]{2,1,0:T(8,128)(2,1)S(1)} copy-done((bf16[32,32,2048]{2,1,0:T(8,128)(2,1)S(1)}, bf16[32,32,2048]{2,1,0:T(8,128)(2,1)}, u32[]{:S(2)}) %copy-start) | copy-done | bytes 4194328
  20.1 2.7 %shard_map.81.refs_2_.refs_0_ = f32[64,32]{1,0:T(8,128)S(1)} custom-call(bf16[32,32,2048]{2,1,0:T(8,128)(2,1)S(1)} %copy-done, bf16[64,16,512]{2,1,0:T(8,128)(2,1)S(1)} %get-tuple-element.27.refs_0_, bf16[64,16,1536]{2,1,0:T(8,128)(2,1)S(1)} %get-tuple-element.28.refs_1_.refs_0_), custom_call_target="tpu_custom_call" | custom-call | flops 1 | bytes 1 | tf_op jit(solution)/shard_map/pallas_call | solution.py:283
  22.8 4.7 %shard_map.82 = (bf16[64,16,1024]{2,1,0:T(8,128)(2,1)S(1)}, bf16[16,16,1024]{2,1,0:T(8,128)(2,1)S(1)}) custom-call(bf16[64,16,1536]{2,1,0:T(8,128)(2,1)S(1)} %get-tuple-element.28.refs_1_.refs_0_, f32[16,16,512]{2,1,0:T(8,128)S(1)} %get-tuple-element.31.refs_1_.own_i, f32[64,32]{1,0:T(8,128)S(1)} %shard_map.81.refs_2_.refs_0_, ...), custom_call_target="tpu_custom_call" | custom-call | flops 10000000000 | bytes 100000000 | tf_op jit(solution)/shard_map/pallas_call | solution.py:239
  27.5 2.7 %collective-permute-start.5 = (bf16[16,16,1024]{2,1,0:T(8,128)(2,1)S(1)}, bf16[16,16,1024]{2,1,0:T(8,128)(2,1)S(1)}, u32[]{:S(2)}, u32[]{:S(2)}) collective-permute-start(bf16[16,16,1024]{2,1,0:T(8,128)(2,1)S(1)} %get-tuple-element.40), channel_id=1, source_target_pairs={{0,1},{1,0},{2,3},{3,2},{4,5},{5,4},{6,7},{7,6},{8,9},{9,8},{10,11... | collective-permute-start | bytes 1572872 | tf_op jit(solution)/shard_map/ppermute | solution.py:415
  30.2 4.7 %shard_map.83 = (bf16[64,16,1024]{2,1,0:T(8,128)(2,1)S(1)}, bf16[16,16,1024]{2,1,0:T(8,128)(2,1)S(1)}) custom-call(bf16[64,16,1024]{2,1,0:T(8,128)(2,1)S(1)} %get-tuple-element.34.refs_0_, bf16[16,16,512]{2,1,0:T(8,128)(2,1)S(1)} %collective-permute-done.3.refs_1_.got_i.refs_2_, bf16[16,32,2048]{2,1,0:T(8,128)(2,1)S(1)} %get-tuple-element.25.refs_0_.refs_1_.refs_3_.refs_2_, ...), custom_call_target="tpu_custom_call" | custom-call | flops 1 | bytes 1 | tf_op jit(solution)/shard_map/pallas_call | solution.py:239
  35.5 2.7 %shard_map.88.refs_1_ = f32[64,32]{1,0:T(8,128)S(1)} custom-call(bf16[32,32,2048]{2,1,0:T(8,128)(2,1)S(1)} %copy-done, bf16[64,16,1024]{2,1,0:T(8,128)(2,1)S(1)} %get-tuple-element.34.refs_0_, bf16[64,16,1024]{2,1,0:T(8,128)(2,1)S(1)} %get-tuple-element.36.refs_1_), custom_call_target="tpu_custom_call" | custom-call | flops 1 | bytes 1 | tf_op jit(solution)/shard_map/pallas_call | solution.py:283
  38.2 1.8 %collective-permute-done.got_i.refs_3_ = bf16[16,16,1536]{2,1,0:T(8,128)(2,1)S(1)} collective-permute-done((bf16[16,16,1536]{2,1,0:T(8,128)(2,1)S(1)}, bf16[16,16,1536]{2,1,0:T(8,128)(2,1)S(1)}, u32[]{:S(2)}, u32[]{:S(2)}) %collective-permute-start) | collective-permute-done | bytes 786464 | tf_op jit(solution)/shard_map/ppermute | solution.py:415
  40.0 2.1 %collective-permute-start.8 = (f32[64,32]{1,0:T(8,128)S(1)}, f32[64,32]{1,0:T(8,128)S(1)}, u32[]{:S(2)}, u32[]{:S(2)}) collective-permute-start(f32[64,32]{1,0:T(8,128)S(1)} %shard_map.89.refs_0_), channel_id=1, source_target_pairs={{0,24},{2,26},{4,28},{6,30},{8,16},{10,18},{12,20},{14,22},{16,8},... | collective-permute-start | bytes 24584 | tf_op jit(solution)/shard_map/ppermute | solution.py:387
  42.1 1.2 %collective-permute-start.6 = (f32[64,32]{1,0:T(8,128)S(1)}, f32[64,32]{1,0:T(8,128)S(1)}, u32[]{:S(2)}, u32[]{:S(2)}) collective-permute-start(f32[64,32]{1,0:T(8,128)S(1)} %shard_map.89.refs_0_), channel_id=1, source_target_pairs={{0,8},{2,10},{4,12},{6,14},{8,0},{10,2},{12,4},{14,6},{16,24},{18,... | collective-permute-start | bytes 24584 | tf_op jit(solution)/shard_map/ppermute | solution.py:387
  43.3 1.2 %shard_map.84 = (f32[16,16,1024]{2,1,0:T(8,128)S(1)}, f32[16,16,1024]{2,1,0:T(8,128)S(1)}) custom-call(bf16[512,1024]{1,0:T(8,128)(2,1)S(1)} %get-tuple-element.24.refs_2_.refs_3_.mix_ref.refs_5_.refs_4_, bf16[64,16,1024]{2,1,0:T(8,128)(2,1)S(1)} %get-tuple-element.34.refs_0_, bf16[64,16,1024]{2,1,0:T(8,128)(2,1)S(1)} %get-tuple-element.36.refs_1_), custom_call_target="tpu_custom_call" | custom-call | flops 1 | bytes 1 | tf_op jit(solution)/shard_map/pallas_call | solution.py:305
  44.5 2.1 %collective-permute-done.7.refs_2_ = f32[64,32]{1,0:T(8,128)S(1)} collective-permute-done((f32[64,32]{1,0:T(8,128)S(1)}, f32[64,32]{1,0:T(8,128)S(1)}, u32[]{:S(2)}, u32[]{:S(2)}) %collective-permute-start.7) | collective-permute-done | bytes 8224 | tf_op jit(solution)/shard_map/ppermute | solution.py:387
  46.7 2.6 %collective-permute-start.11 = (f32[64,32]{1,0:T(8,128)S(1)}, f32[64,32]{1,0:T(8,128)S(1)}, u32[]{:S(2)}, u32[]{:S(2)}) collective-permute-start(f32[64,32]{1,0:T(8,128)S(1)} %shard_map.90.refs_0_), channel_id=1, source_target_pairs={{0,96},{2,98},{4,100},{6,102},{8,104},{10,106},{12,108},{14,110},{... | collective-permute-start | bytes 24584 | tf_op jit(solution)/shard_map/ppermute | solution.py:387
  50.0 1.2 %collective-permute-done.5.got_o = bf16[16,16,1024]{2,1,0:T(8,128)(2,1)S(1)} collective-permute-done((bf16[16,16,1024]{2,1,0:T(8,128)(2,1)S(1)}, bf16[16,16,1024]{2,1,0:T(8,128)(2,1)S(1)}, u32[]{:S(2)}, u32[]{:S(2)}) %collective-permute-start.5) | collective-permute-done | bytes 524320 | tf_op jit(solution)/shard_map/ppermute | solution.py:415
  51.2 1.5 %shard_map.85 = (bf16[16,32,2048]{2,1,0:T(8,128)(2,1)}, f32[8,128]{1,0:T(8,128)}) custom-call(f32[16,16,512]{2,1,0:T(8,128)S(1)} %get-tuple-element.31.refs_1_.own_i, bf16[16,16,512]{2,1,0:T(8,128)(2,1)S(1)} %collective-permute-done.3.refs_1_.got_i.refs_2_, f32[16,16,1024]{2,1,0:T(8,128)S(1)} %get-tuple-element.39.own_o.refs_4_, ...), custom_call_target="tpu_custom_call" | custom-call | flops 1 | bytes 1 | tf_op jit(solution)/shard_map/pallas_call | solution.py:342
  53.8 4.2 %collective-permute-start.14 = (f32[64,32]{1,0:T(8,128)S(1)}, f32[64,32]{1,0:T(8,128)S(1)}, u32[]{:S(2)}, u32[]{:S(2)}) collective-permute-start(f32[64,32]{1,0:T(8,128)S(1)} %shard_map.91.refs_0_), channel_id=1, source_target_pairs={{0,6},{2,4},{4,2},{6,0},{8,14},{10,12},{12,10},{14,8},{16,22},{18,... | collective-permute-start | bytes 24584 | tf_op jit(solution)/shard_map/ppermute | solution.py:387
  58.0 2.1 %collective-permute-start.13 = (f32[64,32]{1,0:T(8,128)S(1)}, f32[64,32]{1,0:T(8,128)S(1)}, u32[]{:S(2)}, u32[]{:S(2)}) collective-permute-start(f32[64,32]{1,0:T(8,128)S(1)} %shard_map.91.refs_0_), channel_id=1, source_target_pairs={{0,4},{2,6},{4,0},{6,2},{8,12},{10,14},{12,8},{14,10},{16,20},{18,... | collective-permute-start | bytes 24584 | tf_op jit(solution)/shard_map/ppermute | solution.py:387
  60.8 1.1 %shard_map.87 = (bf16[16,32,2048]{2,1,0:T(8,128)(2,1)}, f32[8,128]{1,0:T(8,128)S(1)}) custom-call(f32[16,16,1536]{2,1,0:T(8,128)S(1)} %get-tuple-element.29.own_i, bf16[16,16,1536]{2,1,0:T(8,128)(2,1)S(1)} %collective-permute-done.got_i.refs_3_, f32[16,16,1024]{2,1,0:T(8,128)S(1)} %get-tuple-element.37.own_o, ...), custom_call_target="tpu_custom_call", output_to_operand_aliasing={{0}: (4, {})} | custom-call | flops 1 | bytes 1 | tf_op jit(solution)/shard_map/pallas_call | solution.py:342
  (24 shorter events, 4.5 us)
Async XLA Ops:
  2.7 20.1 %collective-permute-start.1 = (bf16[19,4,2048]{2,1,0:T(4,128)(2,1)S(1)}, bf16[19,4,2048]{2,1,0:T(4,128)(2,1)S(1)}, u32[]{:S(2)}, u32[]{:S(2)}) collective-permute-start(bf16[19,4,2048]{2,1,0:T(4,128)(2,1)S(1)} %get-tuple-element.32), channel_id=1, source_target_pairs={{0,2},{4,6},{8,10},{12,14},{16,18},{20,22},{24,26},{28,30},{32,34}... | collective-permute-start | bytes 933896 | tf_op jit(solution)/shard_map/ppermute | solution.py:429
  4.2 18.6 %collective-permute-start.2 = (bf16[56,2048]{1,0:T(8,128)(2,1)S(1)}, bf16[56,2048]{1,0:T(8,128)(2,1)S(1)}, u32[]{:S(2)}, u32[]{:S(2)}) collective-permute-start(bf16[56,2048]{1,0:T(8,128)(2,1)S(1)} %get-tuple-element.33), channel_id=1, source_target_pairs={{2,4},{6,8},{10,12},{14,16},{18,20},{22,24},{26,28},{30,32},{34,36... | collective-permute-start | bytes 688136 | tf_op jit(solution)/shard_map/ppermute | solution.py:429
  9.5 20.7 %collective-permute-start.3 = (bf16[16,16,512]{2,1,0:T(8,128)(2,1)S(1)}, bf16[16,16,512]{2,1,0:T(8,128)(2,1)S(1)}, u32[]{:S(2)}, u32[]{:S(2)}) collective-permute-start(bf16[16,16,512]{2,1,0:T(8,128)(2,1)S(1)} %get-tuple-element.35), channel_id=1, source_target_pairs={{0,1},{1,0},{2,3},{3,2},{4,5},{5,4},{6,7},{7,6},{8,9},{9,8},{10,11... | collective-permute-start | bytes 786440 | tf_op jit(solution)/shard_map/ppermute | solution.py:415
  17.5 22.5 %collective-permute-start = (bf16[16,16,1536]{2,1,0:T(8,128)(2,1)S(1)}, bf16[16,16,1536]{2,1,0:T(8,128)(2,1)S(1)}, u32[]{:S(2)}, u32[]{:S(2)}) collective-permute-start(bf16[16,16,1536]{2,1,0:T(8,128)(2,1)S(1)} %get-tuple-element.30), channel_id=1, source_target_pairs={{0,1},{1,0},{2,3},{3,2},{4,5},{5,4},{6,7},{7,6},{8,9},{9,8},{10,11... | collective-permute-start | bytes 2359304 | tf_op jit(solution)/shard_map/ppermute | solution.py:415
  17.9 2.2 %copy-start = (bf16[32,32,2048]{2,1,0:T(8,128)(2,1)S(1)}, bf16[32,32,2048]{2,1,0:T(8,128)(2,1)}, u32[]{:S(2)}) copy-start(bf16[32,32,2048]{2,1,0:T(8,128)(2,1)} %f_ref.3) | copy-start | bytes 12582916
  27.5 23.8 %collective-permute-start.5 = (bf16[16,16,1024]{2,1,0:T(8,128)(2,1)S(1)}, bf16[16,16,1024]{2,1,0:T(8,128)(2,1)S(1)}, u32[]{:S(2)}, u32[]{:S(2)}) collective-permute-start(bf16[16,16,1024]{2,1,0:T(8,128)(2,1)S(1)} %get-tuple-element.40), channel_id=1, source_target_pairs={{0,1},{1,0},{2,3},{3,2},{4,5},{5,4},{6,7},{7,6},{8,9},{9,8},{10,11... | collective-permute-start | bytes 1572872 | tf_op jit(solution)/shard_map/ppermute | solution.py:415
  34.9 25.9 %collective-permute-start.4 = (bf16[16,16,1024]{2,1,0:T(8,128)(2,1)S(1)}, bf16[16,16,1024]{2,1,0:T(8,128)(2,1)S(1)}, u32[]{:S(2)}, u32[]{:S(2)}) collective-permute-start(bf16[16,16,1024]{2,1,0:T(8,128)(2,1)S(1)} %get-tuple-element.38), channel_id=1, source_target_pairs={{0,1},{1,0},{2,3},{3,2},{4,5},{5,4},{6,7},{7,6},{8,9},{9,8},{10,11... | collective-permute-start | bytes 1572872 | tf_op jit(solution)/shard_map/ppermute | solution.py:415
  40.0 4.5 %collective-permute-start.8 = (f32[64,32]{1,0:T(8,128)S(1)}, f32[64,32]{1,0:T(8,128)S(1)}, u32[]{:S(2)}, u32[]{:S(2)}) collective-permute-start(f32[64,32]{1,0:T(8,128)S(1)} %shard_map.89.refs_0_), channel_id=1, source_target_pairs={{0,24},{2,26},{4,28},{6,30},{8,16},{10,18},{12,20},{14,22},{16,8},... | collective-permute-start | bytes 24584 | tf_op jit(solution)/shard_map/ppermute | solution.py:387
  42.1 4.6 %collective-permute-start.7 = (f32[64,32]{1,0:T(8,128)S(1)}, f32[64,32]{1,0:T(8,128)S(1)}, u32[]{:S(2)}, u32[]{:S(2)}) collective-permute-start(f32[64,32]{1,0:T(8,128)S(1)} %shard_map.89.refs_0_), channel_id=1, source_target_pairs={{0,16},{2,18},{4,20},{6,22},{8,24},{10,26},{12,28},{14,30},{16,0},... | collective-permute-start | bytes 24584 | tf_op jit(solution)/shard_map/ppermute | solution.py:387
  42.1 4.6 %collective-permute-start.6 = (f32[64,32]{1,0:T(8,128)S(1)}, f32[64,32]{1,0:T(8,128)S(1)}, u32[]{:S(2)}, u32[]{:S(2)}) collective-permute-start(f32[64,32]{1,0:T(8,128)S(1)} %shard_map.89.refs_0_), channel_id=1, source_target_pairs={{0,8},{2,10},{4,12},{6,14},{8,0},{10,2},{12,4},{14,6},{16,24},{18,... | collective-permute-start | bytes 24584 | tf_op jit(solution)/shard_map/ppermute | solution.py:387
  46.7 6.9 %collective-permute-start.11 = (f32[64,32]{1,0:T(8,128)S(1)}, f32[64,32]{1,0:T(8,128)S(1)}, u32[]{:S(2)}, u32[]{:S(2)}) collective-permute-start(f32[64,32]{1,0:T(8,128)S(1)} %shard_map.90.refs_0_), channel_id=1, source_target_pairs={{0,96},{2,98},{4,100},{6,102},{8,104},{10,106},{12,108},{14,110},{... | collective-permute-start | bytes 24584 | tf_op jit(solution)/shard_map/ppermute | solution.py:387
  49.2 4.6 %collective-permute-start.10 = (f32[64,32]{1,0:T(8,128)S(1)}, f32[64,32]{1,0:T(8,128)S(1)}, u32[]{:S(2)}, u32[]{:S(2)}) collective-permute-start(f32[64,32]{1,0:T(8,128)S(1)} %shard_map.90.refs_0_), channel_id=1, source_target_pairs={{0,64},{2,66},{4,68},{6,70},{8,72},{10,74},{12,76},{14,78},{16,80}... | collective-permute-start | bytes 24584 | tf_op jit(solution)/shard_map/ppermute | solution.py:387
  49.8 4.1 %collective-permute-start.9 = (f32[64,32]{1,0:T(8,128)S(1)}, f32[64,32]{1,0:T(8,128)S(1)}, u32[]{:S(2)}, u32[]{:S(2)}) collective-permute-start(f32[64,32]{1,0:T(8,128)S(1)} %shard_map.90.refs_0_), channel_id=1, source_target_pairs={{0,32},{2,34},{4,36},{6,38},{8,40},{10,42},{12,44},{14,46},{16,48}... | collective-permute-start | bytes 24584 | tf_op jit(solution)/shard_map/ppermute | solution.py:387
  53.8 8.1 %collective-permute-start.14 = (f32[64,32]{1,0:T(8,128)S(1)}, f32[64,32]{1,0:T(8,128)S(1)}, u32[]{:S(2)}, u32[]{:S(2)}) collective-permute-start(f32[64,32]{1,0:T(8,128)S(1)} %shard_map.91.refs_0_), channel_id=1, source_target_pairs={{0,6},{2,4},{4,2},{6,0},{8,14},{10,12},{12,10},{14,8},{16,22},{18,... | collective-permute-start | bytes 24584 | tf_op jit(solution)/shard_map/ppermute | solution.py:387
  58.0 4.1 %collective-permute-start.13 = (f32[64,32]{1,0:T(8,128)S(1)}, f32[64,32]{1,0:T(8,128)S(1)}, u32[]{:S(2)}, u32[]{:S(2)}) collective-permute-start(f32[64,32]{1,0:T(8,128)S(1)} %shard_map.91.refs_0_), channel_id=1, source_target_pairs={{0,4},{2,6},{4,0},{6,2},{8,12},{10,14},{12,8},{14,10},{16,20},{18,... | collective-permute-start | bytes 24584 | tf_op jit(solution)/shard_map/ppermute | solution.py:387
  60.1 2.0 %collective-permute-start.12 = (f32[64,32]{1,0:T(8,128)S(1)}, f32[64,32]{1,0:T(8,128)S(1)}, u32[]{:S(2)}, u32[]{:S(2)}) collective-permute-start(f32[64,32]{1,0:T(8,128)S(1)} %shard_map.91.refs_0_), channel_id=1, source_target_pairs={{0,2},{2,0},{4,6},{6,4},{8,10},{10,8},{12,14},{14,12},{16,18},{18,... | collective-permute-start | bytes 24584 | tf_op jit(solution)/shard_map/ppermute | solution.py:387

commit v6 on v5

--- a/solution.py
+++ b/solution.py
@@ -43,7 +43,7 @@
 
 def prepare_kernel(
     sides, w_hbm, g_ref, east_ref, south_ref, mask_ref,
-    mix_ref, g_out, maps_out, partner_ref, other_ref, mask_buf, w_ref, dense, sems,
+    mix_ref, g_out, maps_out, other_ref, mask_buf, w_ref, dense, sems,
 ):
     nch = g_out.shape[0]
     some = nch // PARTS
@@ -86,8 +86,6 @@
             copies[4 + o // some].wait()
         x = g_out[o].astype(F32) if o < nch else maps_out[o - nch]
         head, tail = x[:TILE], x[height - TILE :]
-        partner = jnp.where(even, tail[TILE - HALO :], head[:HALO])
-        partner_ref[o] = partner.astype(BF16)
         at, count = dense_rows(o, nch)
         other = jnp.where(even, head, pltpu.roll(tail, count, 0))
         dense[at : at + count] = other[:count]
@@ -105,11 +103,10 @@
             jax.ShapeDtypeStruct((nin * SUB, nterms * nout * SUB), BF16),
             jax.ShapeDtypeStruct(g.shape, g.dtype),
             jax.ShapeDtypeStruct((3, rows, total), F32),
-            jax.ShapeDtypeStruct((nch + 3, HALO, total), BF16),
             jax.ShapeDtypeStruct((dense, total), BF16),
         ),
         in_specs=[HBM] * 5,
-        out_specs=[VMEM] * 5,
+        out_specs=[VMEM] * 4,
         scratch_shapes=[
             pltpu.VMEM((rows, total), jnp.int32),
             pltpu.VMEM((nterms, nout, nin), BF16),
@@ -141,9 +138,11 @@
     )
 
 
-def terms_kernel(outer, off, lo, hi, nterms, waits, *refs):
+def terms_kernel(outer, off, lo, hi, nterms, waits, pack, *refs):
     g_ref, maps_ref, mix_ref = refs[waits : waits + 3]
     partner_ref, other_ref = refs[waits + 3 : waits + 5] if outer else (None, None)
+    pack_ref = refs[-2] if pack else None
+    refs = refs[:-2] + refs[-1:] if pack else refs
     (terms_ref, send_ref, w_buf), tiles = refs[-5:-2] if outer else refs[-3:], refs[-1]
     nch = g_ref.shape[0]
     ext, span = w_buf.shape[1:]
@@ -219,6 +218,12 @@
                 terms_ref[k * nch + o] = keep(x)
         return carry
 
+    if pack:
+        even = lax.axis_index("pix") % 2 == 0
+        for o in range(nch + 3):
+            x = g_ref[o].astype(F32) if o < nch else maps_ref[o - nch]
+            head, tail = x[:TILE], x[x.shape[0] - TILE :]
+            pack_ref[o] = jnp.where(even, tail[TILE - HALO :], head[:HALO]).astype(BF16)
     lax.fori_loop(0, nch // group, channels, 0)
     for c in range(0, width, 256):
         x = terms_ref[:, :, c : c + 256].reshape(nterms * nch * SUB, 256)
@@ -230,6 +235,8 @@
     nch, rows, total = g.shape
     lo, hi = max(0, start - SIDE), min(total, start + width + SIDE)
     ext = 4 * TILE if outer else 3 * TILE
+    pack = not waits
+    packed = [jax.ShapeDtypeStruct((nch + 3, HALO, total), BF16)] if pack else []
     halo = []
     if outer:
         halo = [
@@ -237,13 +244,14 @@
             pltpu.VMEM((nch + 3, TILE, hi - lo), F32),
         ]
     return pl.pallas_call(
-        functools.partial(terms_kernel, outer, start - lo, lo, hi, nterms, len(waits)),
+        functools.partial(terms_kernel, outer, start - lo, lo, hi, nterms, len(waits), pack),
         out_shape=(
             jax.ShapeDtypeStruct((nterms * nch, SUB, width), BF16),
             jax.ShapeDtypeStruct((sent, SUB, width), BF16),
+            *packed,
         ),
         in_specs=[ANY] * len(waits) + [VMEM] * (3 + len(beside)),
-        out_specs=(VMEM, VMEM),
+        out_specs=(VMEM,) * (2 + pack),
         scratch_shapes=[pltpu.VMEM((4, ext, hi - lo), F32)] + halo,
         compiler_params=params(20),
         cost_estimate=cost,
@@ -397,10 +405,10 @@
     nterms, nin, _ = cheb_weight.shape
     size, sides = lax.axis_size("pix"), lax.axis_size("ch")
     part = nin // sides
-    mix, g, maps, to_partner, to_other = prepare(
+    mix, g, maps, to_other = prepare(
         cheb_weight, grad_out, east_weight, south_weight, pixel_mask, sides
     )
-    pieces = []
+    pieces, to_partner = [], []
 
     def chunks(outer, widths, beside, first):
         start = 0
@@ -408,12 +416,13 @@
             waits = [pieces[-1][1], *first] if pieces else []
             late = outer and start
             waits += [pieces[0][2]] if late else []
-            terms, send = chunk_terms(
+            terms, send, *packed = chunk_terms(
                 outer, start, width, g, maps, mix, part, nterms, beside, waits,
-                LONG if outer and not start else COST,
+                LONG if outer and not start or not outer and start else COST,
             )
             got = lax.ppermute(send, "ch", [(i, i ^ 1) for i in range(sides)])
             pieces.append(((outer, start, width), terms, got))
+            to_partner.extend(packed)
             start += width
             first = ()
 
@@ -428,7 +437,7 @@
         pairs = [(i, i + 1) for i in range(first, size - 1, 2) if (i + 1) * rows % total]
         return lax.ppermute(x, "pix", pairs + [(j, i) for i, j in pairs])
 
-    beside = (swap(to_partner, 0), swap(to_other, 1))
+    beside = (swap(to_partner[0], 0), swap(to_other, 1))
     chunks(True, OUTER, beside, (own_inner[0], grad_inner))
     own_outer, grad_outer = local(pieces[n:])
     pieces = [

time: 63 us -> 66 us (1.048)
  the two profiles are of different devices: /device:TPU:1 before, /device:TPU:6 now
where the time goes in v6:
time: 66 us; the launch traced here: 65.8 us
  Pallas kernels  30.7 us (47%)
  starting transfers between devices  24.4 us (37%)
  waiting for transfers between devices  8.93 us (14%)
  local copies, waits for them, and re-layouts  0.94 us (1%)
  between operations  0.83 us (1%)
    pallas_call x4, Pallas kernels, chunk_terms(): pl.pallas_call(functools.partial(terms_kernel, outer, start - lo, lo, hi,...  16.8 us
    ppermute x9, starting transfers between devices, sum_over_pix(): lax.ppermute(value, 'pix', [(i, i ^ x * step) for i in range(size)])  10.2 us
    ppermute x4, waiting for transfers between devices, chunks(): got = lax.ppermute(send, 'ch', [(i, i ^ 1) for i in range(sides)])  7.93 us
    ppermute x4, starting transfers between devices, chunks(): got = lax.ppermute(send, 'ch', [(i, i ^ 1) for i in range(sides)])  7.56 us
    ppermute x2, starting transfers between devices, swap(): return lax.ppermute(x, 'pix', pairs + [(j, i) for i, j in pairs])  6.67 us
    pallas_call x2, Pallas kernels, weights(): pl.pallas_call(functools.partial(weights_kernel, places), out_shape=jax.S...  5.44 us
    pallas_call x3, Pallas kernels, finish(): pl.pallas_call(functools.partial(finish_kernel, start, width, start - inn...  3.37 us
    pallas_call x2, Pallas kernels, own_parts(): pl.pallas_call(own_kernel, out_shape=[jax.ShapeDtypeStruct((kept, *t.shap...  2.48 us
  transfers between devices with their start and end apart: 15, of which 5 were waited for; matrix products, arithmetic and copies ran while one was open for 0% of the time, Pallas kernels for 43%

profile of v6, /device:TPU:6, one launch (start us, length us, event | category | flops | bytes accessed | tf_op | source)
XLA Modules:
  0.0 65.8 jit_solution(16262540520549185864)
XLA Ops:
  0.6 2.0 %shard_map.77 = (bf16[512,1024]{1,0:T(8,128)(2,1)S(1)}, bf16[16,32,2048]{2,1,0:T(8,128)(2,1)S(1)}, f32[3,32,2048]{2,1,0:T(8,128)S(1)}, bf16[56,2048]{1,0:T(8,128)(2,1)S(1)}) custom-call(bf16[4,16,32]{2,1,0:T(8,128)(2,1)} %bitcast.5, bf16[16,32,2048]{2,1,0:T(8,128)(2,1)} %g_ref.1, f32[32,2048]{1,0:T(8,128)} %east_ref.1, f32[32,2048]{1,0:T(8,128)} %south_ref.1, ...), custom_call_target="tpu_custom_call" | custom-call | flops 1 | bytes 1 | tf_op jit(solution)/shard_map/pallas_call | solution.py:100
  2.6 6.7 %collective-permute-start.2 = (bf16[56,2048]{1,0:T(8,128)(2,1)S(1)}, bf16[56,2048]{1,0:T(8,128)(2,1)S(1)}, u32[]{:S(2)}, u32[]{:S(2)}) collective-permute-start(bf16[56,2048]{1,0:T(8,128)(2,1)S(1)} %get-tuple-element.33), channel_id=1, source_target_pairs={{2,4},{6,8},{10,12},{14,16},{18,20},{22,24},{26,28},{30,32},{34,36... | collective-permute-start | bytes 688136 | tf_op jit(solution)/shard_map/ppermute | solution.py:438
  9.3 2.2 %shard_map.78 = (bf16[64,16,512]{2,1,0:T(8,128)(2,1)S(1)}, bf16[16,16,512]{2,1,0:T(8,128)(2,1)S(1)}, bf16[19,4,2048]{2,1,0:T(4,128)(2,1)S(1)}) custom-call(bf16[16,32,2048]{2,1,0:T(8,128)(2,1)S(1)} %get-tuple-element.25.refs_0_.refs_1_.refs_3_.refs_2_, f32[3,32,2048]{2,1,0:T(8,128)S(1)} %get-tuple-element.26.refs_1_.refs_2_.refs_4_.refs_3_, ...), custom_call_target="tpu_custom_call" | custom-call | flops 1 | bytes 1 | tf_op jit(solution)/shard_map/pallas_call | solution.py:246
  11.5 3.0 %collective-permute-start.3 = (bf16[16,16,512]{2,1,0:T(8,128)(2,1)S(1)}, bf16[16,16,512]{2,1,0:T(8,128)(2,1)S(1)}, u32[]{:S(2)}, u32[]{:S(2)}) collective-permute-start(bf16[16,16,512]{2,1,0:T(8,128)(2,1)S(1)} %get-tuple-element.35), channel_id=1, source_target_pairs={{0,1},{1,0},{2,3},{3,2},{4,5},{5,4},{6,7},{7,6},{8,9},{9,8},{10,11... | collective-permute-start | bytes 786440 | tf_op jit(solution)/shard_map/ppermute | solution.py:423
  14.5 5.3 %shard_map.79 = (bf16[64,16,1536]{2,1,0:T(8,128)(2,1)S(1)}, bf16[16,16,1536]{2,1,0:T(8,128)(2,1)S(1)}) custom-call(bf16[64,16,512]{2,1,0:T(8,128)(2,1)S(1)} %get-tuple-element.27.refs_0_, bf16[16,32,2048]{2,1,0:T(8,128)(2,1)S(1)} %get-tuple-element.25.refs_0_.refs_1_.refs_3_.refs_2_, f32[3,32,2048]{2,1,0:T(8,128)S(1)} %get-tuple-element.26.refs_1_.refs_2_.refs_4_.refs_3_, ...), custom_call_target="tpu_custom_call" | custom-call | flops 10000000000 | bytes 100000000 | tf_op jit(solution)/shard_map/pallas_call | solution.py:246
  20.4 1.2 %shard_map.80 = (f32[16,16,512]{2,1,0:T(8,128)S(1)}, f32[16,16,1536]{2,1,0:T(8,128)S(1)}) custom-call(bf16[512,1024]{1,0:T(8,128)(2,1)S(1)} %get-tuple-element.24.refs_2_.refs_3_.mix_ref.refs_5_.refs_4_, bf16[64,16,512]{2,1,0:T(8,128)(2,1)S(1)} %get-tuple-element.27.refs_0_, bf16[64,16,1536]{2,1,0:T(8,128)(2,1)S(1)} %get-tuple-element.28.refs_1_.refs_0_), custom_call_target="tpu_custom_call" | custom-call | flops 1 | bytes 1 | tf_op jit(solution)/shard_map/pallas_call | solution.py:313
  21.7 0.9 %copy-done = bf16[32,32,2048]{2,1,0:T(8,128)(2,1)S(1)} copy-done((bf16[32,32,2048]{2,1,0:T(8,128)(2,1)S(1)}, bf16[32,32,2048]{2,1,0:T(8,128)(2,1)}, u32[]{:S(2)}) %copy-start) | copy-done | bytes 4194328
  22.6 2.7 %shard_map.81.refs_2_.refs_0_ = f32[64,32]{1,0:T(8,128)S(1)} custom-call(bf16[32,32,2048]{2,1,0:T(8,128)(2,1)S(1)} %copy-done, bf16[64,16,512]{2,1,0:T(8,128)(2,1)S(1)} %get-tuple-element.27.refs_0_, bf16[64,16,1536]{2,1,0:T(8,128)(2,1)S(1)} %get-tuple-element.28.refs_1_.refs_0_), custom_call_target="tpu_custom_call" | custom-call | flops 1 | bytes 1 | tf_op jit(solution)/shard_map/pallas_call | solution.py:291
  25.4 4.7 %shard_map.82 = (bf16[64,16,1024]{2,1,0:T(8,128)(2,1)S(1)}, bf16[16,16,1024]{2,1,0:T(8,128)(2,1)S(1)}) custom-call(bf16[64,16,1536]{2,1,0:T(8,128)(2,1)S(1)} %get-tuple-element.28.refs_1_.refs_0_, f32[16,16,512]{2,1,0:T(8,128)S(1)} %get-tuple-element.31.refs_1_.own_i, f32[64,32]{1,0:T(8,128)S(1)} %shard_map.81.refs_2_.refs_0_, ...), custom_call_target="tpu_custom_call" | custom-call | flops 10000000000 | bytes 100000000 | tf_op jit(solution)/shard_map/pallas_call | solution.py:246
  30.0 3.0 %collective-permute-start.5 = (bf16[16,16,1024]{2,1,0:T(8,128)(2,1)S(1)}, bf16[16,16,1024]{2,1,0:T(8,128)(2,1)S(1)}, u32[]{:S(2)}, u32[]{:S(2)}) collective-permute-start(bf16[16,16,1024]{2,1,0:T(8,128)(2,1)S(1)} %get-tuple-element.40), channel_id=1, source_target_pairs={{0,1},{1,0},{2,3},{3,2},{4,5},{5,4},{6,7},{7,6},{8,9},{9,8},{10,11... | collective-permute-start | bytes 1572872 | tf_op jit(solution)/shard_map/ppermute | solution.py:423
  33.0 4.7 %shard_map.83 = (bf16[64,16,1024]{2,1,0:T(8,128)(2,1)S(1)}, bf16[16,16,1024]{2,1,0:T(8,128)(2,1)S(1)}) custom-call(bf16[64,16,1024]{2,1,0:T(8,128)(2,1)S(1)} %get-tuple-element.34.refs_0_, bf16[16,16,512]{2,1,0:T(8,128)(2,1)S(1)} %collective-permute-done.3.refs_1_.got_i.refs_2_, bf16[16,32,2048]{2,1,0:T(8,128)(2,1)S(1)} %get-tuple-element.25.refs_0_.refs_1_.refs_3_.refs_2_, ...), custom_call_target="tpu_custom_call" | custom-call | flops 1 | bytes 1 | tf_op jit(solution)/shard_map/pallas_call | solution.py:246
  37.7 0.9 %collective-permute-start.4 = (bf16[16,16,1024]{2,1,0:T(8,128)(2,1)S(1)}, bf16[16,16,1024]{2,1,0:T(8,128)(2,1)S(1)}, u32[]{:S(2)}, u32[]{:S(2)}) collective-permute-start(bf16[16,16,1024]{2,1,0:T(8,128)(2,1)S(1)} %get-tuple-element.38), channel_id=1, source_target_pairs={{0,1},{1,0},{2,3},{3,2},{4,5},{5,4},{6,7},{7,6},{8,9},{9,8},{10,11... | collective-permute-start | bytes 1572872 | tf_op jit(solution)/shard_map/ppermute | solution.py:423
  38.6 2.7 %shard_map.88.refs_1_ = f32[64,32]{1,0:T(8,128)S(1)} custom-call(bf16[32,32,2048]{2,1,0:T(8,128)(2,1)S(1)} %copy-done, bf16[64,16,1024]{2,1,0:T(8,128)(2,1)S(1)} %get-tuple-element.34.refs_0_, bf16[64,16,1024]{2,1,0:T(8,128)(2,1)S(1)} %get-tuple-element.36.refs_1_), custom_call_target="tpu_custom_call" | custom-call | flops 1 | bytes 1 | tf_op jit(solution)/shard_map/pallas_call | solution.py:291
  42.4 3.3 %collective-permute-start.6 = (f32[64,32]{1,0:T(8,128)S(1)}, f32[64,32]{1,0:T(8,128)S(1)}, u32[]{:S(2)}, u32[]{:S(2)}) collective-permute-start(f32[64,32]{1,0:T(8,128)S(1)} %shard_map.89.refs_0_), channel_id=1, source_target_pairs={{0,8},{2,10},{4,12},{6,14},{8,0},{10,2},{12,4},{14,6},{16,24},{18,... | collective-permute-start | bytes 24584 | tf_op jit(solution)/shard_map/ppermute | solution.py:395
  45.7 1.2 %shard_map.84 = (f32[16,16,1024]{2,1,0:T(8,128)S(1)}, f32[16,16,1024]{2,1,0:T(8,128)S(1)}) custom-call(bf16[512,1024]{1,0:T(8,128)(2,1)S(1)} %get-tuple-element.24.refs_2_.refs_3_.mix_ref.refs_5_.refs_4_, bf16[64,16,1024]{2,1,0:T(8,128)(2,1)S(1)} %get-tuple-element.34.refs_0_, bf16[64,16,1024]{2,1,0:T(8,128)(2,1)S(1)} %get-tuple-element.36.refs_1_), custom_call_target="tpu_custom_call" | custom-call | flops 1 | bytes 1 | tf_op jit(solution)/shard_map/pallas_call | solution.py:313
  47.0 0.8 %collective-permute-done.7.refs_2_ = f32[64,32]{1,0:T(8,128)S(1)} collective-permute-done((f32[64,32]{1,0:T(8,128)S(1)}, f32[64,32]{1,0:T(8,128)S(1)}, u32[]{:S(2)}, u32[]{:S(2)}) %collective-permute-start.7) | collective-permute-done | bytes 8224 | tf_op jit(solution)/shard_map/ppermute | solution.py:395
  48.4 2.4 %collective-permute-start.10 = (f32[64,32]{1,0:T(8,128)S(1)}, f32[64,32]{1,0:T(8,128)S(1)}, u32[]{:S(2)}, u32[]{:S(2)}) collective-permute-start(f32[64,32]{1,0:T(8,128)S(1)} %shard_map.90.refs_0_), channel_id=1, source_target_pairs={{0,64},{2,66},{4,68},{6,70},{8,72},{10,74},{12,76},{14,78},{16,80}... | collective-permute-start | bytes 24584 | tf_op jit(solution)/shard_map/ppermute | solution.py:395
  50.8 1.3 %collective-permute-start.9 = (f32[64,32]{1,0:T(8,128)S(1)}, f32[64,32]{1,0:T(8,128)S(1)}, u32[]{:S(2)}, u32[]{:S(2)}) collective-permute-start(f32[64,32]{1,0:T(8,128)S(1)} %shard_map.90.refs_0_), channel_id=1, source_target_pairs={{0,32},{2,34},{4,36},{6,38},{8,40},{10,42},{12,44},{14,46},{16,48}... | collective-permute-start | bytes 24584 | tf_op jit(solution)/shard_map/ppermute | solution.py:395
  52.9 1.5 %shard_map.85 = (bf16[16,32,2048]{2,1,0:T(8,128)(2,1)}, f32[8,128]{1,0:T(8,128)}) custom-call(f32[16,16,512]{2,1,0:T(8,128)S(1)} %get-tuple-element.31.refs_1_.own_i, bf16[16,16,512]{2,1,0:T(8,128)(2,1)S(1)} %collective-permute-done.3.refs_1_.got_i.refs_2_, f32[16,16,1024]{2,1,0:T(8,128)S(1)} %get-tuple-element.39.own_o.refs_4_, ...), custom_call_target="tpu_custom_call" | custom-call | flops 1 | bytes 1 | tf_op jit(solution)/shard_map/pallas_call | solution.py:350
  54.3 0.9 %shard_map.86 = (bf16[16,32,2048]{2,1,0:T(8,128)(2,1)}, f32[8,128]{1,0:T(8,128)S(1)}) custom-call(f32[16,16,1536]{2,1,0:T(8,128)S(1)} %get-tuple-element.29.own_i, bf16[16,16,1536]{2,1,0:T(8,128)(2,1)S(1)} %collective-permute-done.got_i.refs_3_, f32[16,16,1024]{2,1,0:T(8,128)S(1)} %get-tuple-element.39.own_o.refs_4_, ...), custom_call_target="tpu_custom_call", output_to_operand_aliasing={{0}: (4, {})} | custom-call | flops 1 | bytes 1 | tf_op jit(solution)/shard_map/pallas_call | solution.py:350
  55.4 1.0 %collective-permute-start.13 = (f32[64,32]{1,0:T(8,128)S(1)}, f32[64,32]{1,0:T(8,128)S(1)}, u32[]{:S(2)}, u32[]{:S(2)}) collective-permute-start(f32[64,32]{1,0:T(8,128)S(1)} %shard_map.91.refs_0_), channel_id=1, source_target_pairs={{0,4},{2,6},{4,0},{6,2},{8,12},{10,14},{12,8},{14,10},{16,20},{18,... | collective-permute-start | bytes 24584 | tf_op jit(solution)/shard_map/ppermute | solution.py:395
  56.3 0.9 %collective-permute-start.12 = (f32[64,32]{1,0:T(8,128)S(1)}, f32[64,32]{1,0:T(8,128)S(1)}, u32[]{:S(2)}, u32[]{:S(2)}) collective-permute-start(f32[64,32]{1,0:T(8,128)S(1)} %shard_map.91.refs_0_), channel_id=1, source_target_pairs={{0,2},{2,0},{4,6},{6,4},{8,10},{10,8},{12,14},{14,12},{16,18},{18,... | collective-permute-start | bytes 24584 | tf_op jit(solution)/shard_map/ppermute | solution.py:395
  57.2 6.9 %collective-permute-done.4.got_o = bf16[16,16,1024]{2,1,0:T(8,128)(2,1)S(1)} collective-permute-done((bf16[16,16,1024]{2,1,0:T(8,128)(2,1)S(1)}, bf16[16,16,1024]{2,1,0:T(8,128)(2,1)S(1)}, u32[]{:S(2)}, u32[]{:S(2)}) %collective-permute-start.4) | collective-permute-done | bytes 524320 | tf_op jit(solution)/shard_map/ppermute | solution.py:423
  64.1 1.1 %shard_map.87 = (bf16[16,32,2048]{2,1,0:T(8,128)(2,1)}, f32[8,128]{1,0:T(8,128)S(1)}) custom-call(f32[16,16,1536]{2,1,0:T(8,128)S(1)} %get-tuple-element.29.own_i, bf16[16,16,1536]{2,1,0:T(8,128)(2,1)S(1)} %collective-permute-done.got_i.refs_3_, f32[16,16,1024]{2,1,0:T(8,128)S(1)} %get-tuple-element.37.own_o, ...), custom_call_target="tpu_custom_call", output_to_operand_aliasing={{0}: (4, {})} | custom-call | flops 1 | bytes 1 | tf_op jit(solution)/shard_map/pallas_call | solution.py:350
  (24 shorter events, 3.8 us)
Async XLA Ops:
  2.6 22.7 %collective-permute-start.2 = (bf16[56,2048]{1,0:T(8,128)(2,1)S(1)}, bf16[56,2048]{1,0:T(8,128)(2,1)S(1)}, u32[]{:S(2)}, u32[]{:S(2)}) collective-permute-start(bf16[56,2048]{1,0:T(8,128)(2,1)S(1)} %get-tuple-element.33), channel_id=1, source_target_pairs={{2,4},{6,8},{10,12},{14,16},{18,20},{22,24},{26,28},{30,32},{34,36... | collective-permute-start | bytes 688136 | tf_op jit(solution)/shard_map/ppermute | solution.py:438
  11.5 21.5 %collective-permute-start.3 = (bf16[16,16,512]{2,1,0:T(8,128)(2,1)S(1)}, bf16[16,16,512]{2,1,0:T(8,128)(2,1)S(1)}, u32[]{:S(2)}, u32[]{:S(2)}) collective-permute-start(bf16[16,16,512]{2,1,0:T(8,128)(2,1)S(1)} %get-tuple-element.35), channel_id=1, source_target_pairs={{0,1},{1,0},{2,3},{3,2},{4,5},{5,4},{6,7},{7,6},{8,9},{9,8},{10,11... | collective-permute-start | bytes 786440 | tf_op jit(solution)/shard_map/ppermute | solution.py:423
  14.4 10.9 %collective-permute-start.1 = (bf16[19,4,2048]{2,1,0:T(4,128)(2,1)S(1)}, bf16[19,4,2048]{2,1,0:T(4,128)(2,1)S(1)}, u32[]{:S(2)}, u32[]{:S(2)}) collective-permute-start(bf16[19,4,2048]{2,1,0:T(4,128)(2,1)S(1)} %get-tuple-element.32), channel_id=1, source_target_pairs={{0,2},{4,6},{8,10},{12,14},{16,18},{20,22},{24,26},{28,30},{32,34}... | collective-permute-start | bytes 933896 | tf_op jit(solution)/shard_map/ppermute | solution.py:438
  19.7 21.9 %collective-permute-start = (bf16[16,16,1536]{2,1,0:T(8,128)(2,1)S(1)}, bf16[16,16,1536]{2,1,0:T(8,128)(2,1)S(1)}, u32[]{:S(2)}, u32[]{:S(2)}) collective-permute-start(bf16[16,16,1536]{2,1,0:T(8,128)(2,1)S(1)} %get-tuple-element.30), channel_id=1, source_target_pairs={{0,1},{1,0},{2,3},{3,2},{4,5},{5,4},{6,7},{7,6},{8,9},{9,8},{10,11... | collective-permute-start | bytes 2359304 | tf_op jit(solution)/shard_map/ppermute | solution.py:423
  20.4 2.2 %copy-start = (bf16[32,32,2048]{2,1,0:T(8,128)(2,1)S(1)}, bf16[32,32,2048]{2,1,0:T(8,128)(2,1)}, u32[]{:S(2)}) copy-start(bf16[32,32,2048]{2,1,0:T(8,128)(2,1)} %f_ref.3) | copy-start | bytes 12582916
  30.0 22.9 %collective-permute-start.5 = (bf16[16,16,1024]{2,1,0:T(8,128)(2,1)S(1)}, bf16[16,16,1024]{2,1,0:T(8,128)(2,1)S(1)}, u32[]{:S(2)}, u32[]{:S(2)}) collective-permute-start(bf16[16,16,1024]{2,1,0:T(8,128)(2,1)S(1)} %get-tuple-element.40), channel_id=1, source_target_pairs={{0,1},{1,0},{2,3},{3,2},{4,5},{5,4},{6,7},{7,6},{8,9},{9,8},{10,11... | collective-permute-start | bytes 1572872 | tf_op jit(solution)/shard_map/ppermute | solution.py:423
  37.7 26.4 %collective-permute-start.4 = (bf16[16,16,1024]{2,1,0:T(8,128)(2,1)S(1)}, bf16[16,16,1024]{2,1,0:T(8,128)(2,1)S(1)}, u32[]{:S(2)}, u32[]{:S(2)}) collective-permute-start(bf16[16,16,1024]{2,1,0:T(8,128)(2,1)S(1)} %get-tuple-element.38), channel_id=1, source_target_pairs={{0,1},{1,0},{2,3},{3,2},{4,5},{5,4},{6,7},{7,6},{8,9},{9,8},{10,11... | collective-permute-start | bytes 1572872 | tf_op jit(solution)/shard_map/ppermute | solution.py:423
  41.7 5.3 %collective-permute-start.8 = (f32[64,32]{1,0:T(8,128)S(1)}, f32[64,32]{1,0:T(8,128)S(1)}, u32[]{:S(2)}, u32[]{:S(2)}) collective-permute-start(f32[64,32]{1,0:T(8,128)S(1)} %shard_map.89.refs_0_), channel_id=1, source_target_pairs={{0,24},{2,26},{4,28},{6,30},{8,16},{10,18},{12,20},{14,22},{16,8},... | collective-permute-start | bytes 24584 | tf_op jit(solution)/shard_map/ppermute | solution.py:395
  42.4 5.4 %collective-permute-start.7 = (f32[64,32]{1,0:T(8,128)S(1)}, f32[64,32]{1,0:T(8,128)S(1)}, u32[]{:S(2)}, u32[]{:S(2)}) collective-permute-start(f32[64,32]{1,0:T(8,128)S(1)} %shard_map.89.refs_0_), channel_id=1, source_target_pairs={{0,16},{2,18},{4,20},{6,22},{8,24},{10,26},{12,28},{14,30},{16,0},... | collective-permute-start | bytes 24584 | tf_op jit(solution)/shard_map/ppermute | solution.py:395
  42.4 5.6 %collective-permute-start.6 = (f32[64,32]{1,0:T(8,128)S(1)}, f32[64,32]{1,0:T(8,128)S(1)}, u32[]{:S(2)}, u32[]{:S(2)}) collective-permute-start(f32[64,32]{1,0:T(8,128)S(1)} %shard_map.89.refs_0_), channel_id=1, source_target_pairs={{0,8},{2,10},{4,12},{6,14},{8,0},{10,2},{12,4},{14,6},{16,24},{18,... | collective-permute-start | bytes 24584 | tf_op jit(solution)/shard_map/ppermute | solution.py:395
  48.0 7.2 %collective-permute-start.11 = (f32[64,32]{1,0:T(8,128)S(1)}, f32[64,32]{1,0:T(8,128)S(1)}, u32[]{:S(2)}, u32[]{:S(2)}) collective-permute-start(f32[64,32]{1,0:T(8,128)S(1)} %shard_map.90.refs_0_), channel_id=1, source_target_pairs={{0,96},{2,98},{4,100},{6,102},{8,104},{10,106},{12,108},{14,110},{... | collective-permute-start | bytes 24584 | tf_op jit(solution)/shard_map/ppermute | solution.py:395
  48.4 6.8 %collective-permute-start.10 = (f32[64,32]{1,0:T(8,128)S(1)}, f32[64,32]{1,0:T(8,128)S(1)}, u32[]{:S(2)}, u32[]{:S(2)}) collective-permute-start(f32[64,32]{1,0:T(8,128)S(1)} %shard_map.90.refs_0_), channel_id=1, source_target_pairs={{0,64},{2,66},{4,68},{6,70},{8,72},{10,74},{12,76},{14,78},{16,80}... | collective-permute-start | bytes 24584 | tf_op jit(solution)/shard_map/ppermute | solution.py:395
  50.8 4.4 %collective-permute-start.9 = (f32[64,32]{1,0:T(8,128)S(1)}, f32[64,32]{1,0:T(8,128)S(1)}, u32[]{:S(2)}, u32[]{:S(2)}) collective-permute-start(f32[64,32]{1,0:T(8,128)S(1)} %shard_map.90.refs_0_), channel_id=1, source_target_pairs={{0,32},{2,34},{4,36},{6,38},{8,40},{10,42},{12,44},{14,46},{16,48}... | collective-permute-start | bytes 24584 | tf_op jit(solution)/shard_map/ppermute | solution.py:395
  55.3 9.9 %collective-permute-start.14 = (f32[64,32]{1,0:T(8,128)S(1)}, f32[64,32]{1,0:T(8,128)S(1)}, u32[]{:S(2)}, u32[]{:S(2)}) collective-permute-start(f32[64,32]{1,0:T(8,128)S(1)} %shard_map.91.refs_0_), channel_id=1, source_target_pairs={{0,6},{2,4},{4,2},{6,0},{8,14},{10,12},{12,10},{14,8},{16,22},{18,... | collective-permute-start | bytes 24584 | tf_op jit(solution)/shard_map/ppermute | solution.py:395
  55.4 9.8 %collective-permute-start.13 = (f32[64,32]{1,0:T(8,128)S(1)}, f32[64,32]{1,0:T(8,128)S(1)}, u32[]{:S(2)}, u32[]{:S(2)}) collective-permute-start(f32[64,32]{1,0:T(8,128)S(1)} %shard_map.91.refs_0_), channel_id=1, source_target_pairs={{0,4},{2,6},{4,0},{6,2},{8,12},{10,14},{12,8},{14,10},{16,20},{18,... | collective-permute-start | bytes 24584 | tf_op jit(solution)/shard_map/ppermute | solution.py:395
  56.3 8.9 %collective-permute-start.12 = (f32[64,32]{1,0:T(8,128)S(1)}, f32[64,32]{1,0:T(8,128)S(1)}, u32[]{:S(2)}, u32[]{:S(2)}) collective-permute-start(f32[64,32]{1,0:T(8,128)S(1)} %shard_map.91.refs_0_), channel_id=1, source_target_pairs={{0,2},{2,0},{4,6},{6,4},{8,10},{10,8},{12,14},{14,12},{16,18},{18,... | collective-permute-start | bytes 24584 | tf_op jit(solution)/shard_map/ppermute | solution.py:395

commit v7 on v5

--- a/solution.py
+++ b/solution.py
@@ -203,7 +203,7 @@
             v = jnp.concatenate([v[:TILE], v[2 * TILE : 3 * TILE]], axis=0)
         return v[:SUB].astype(BF16)
 
-    group = 4
+    group = 8
 
     def channels(step, carry):
         chans = [step * group + n for n in range(group)]

time: 63 us -> 62.9 us (level)
  no operation moved by 1% of the time
where the time goes in v7:
time: 62.9 us; the launch traced here: 62.7 us
  Pallas kernels  30.7 us (49%)
  starting transfers between devices  24 us (38%)
  waiting for transfers between devices  6.32 us (10%)
  local copies, waits for them, and re-layouts  0.94 us (1%)
  between operations  0.79 us (1%)
    pallas_call x4, Pallas kernels, chunk_terms(): pl.pallas_call(functools.partial(terms_kernel, outer, start - lo, lo, hi,...  16.6 us
    ppermute x9, starting transfers between devices, sum_over_pix(): lax.ppermute(value, 'pix', [(i, i ^ x * step) for i in range(size)])  12.9 us
    ppermute x4, starting transfers between devices, chunks(): got = lax.ppermute(send, 'ch', [(i, i ^ 1) for i in range(sides)])  6.44 us
    pallas_call x2, Pallas kernels, weights(): pl.pallas_call(functools.partial(weights_kernel, places), out_shape=jax.S...  5.43 us
    ppermute x2, starting transfers between devices, swap(): return lax.ppermute(x, 'pix', pairs + [(j, i) for i, j in pairs])  4.69 us
    ppermute x4, waiting for transfers between devices, chunks(): got = lax.ppermute(send, 'ch', [(i, i ^ 1) for i in range(sides)])  4 us
    pallas_call x3, Pallas kernels, finish(): pl.pallas_call(functools.partial(finish_kernel, start, width, start - inn...  3.37 us
    pallas_call x2, Pallas kernels, own_parts(): pl.pallas_call(own_kernel, out_shape=[jax.ShapeDtypeStruct((kept, *t.shap...  2.48 us
  transfers between devices with their start and end apart: 15, of which 6 were waited for; matrix products, arithmetic and copies ran while one was open for 0% of the time, Pallas kernels for 45%

profile of v7, /device:TPU:1, one launch (start us, length us, event | category | flops | bytes accessed | tf_op | source)
XLA Modules:
  0.0 62.7 jit_solution(12003291616987595523)
XLA Ops:
  0.6 2.1 %shard_map.77 = (bf16[512,1024]{1,0:T(8,128)(2,1)S(1)}, bf16[16,32,2048]{2,1,0:T(8,128)(2,1)S(1)}, f32[3,32,2048]{2,1,0:T(8,128)S(1)}, bf16[19,4,2048]{2,1,0:T(4,128)(2,1)S(1)}, bf16[56,2048]{1,0:T(8,128)(2,1)S(1)}) custom-call(bf16[4,16,32]{2,1,0:T(8,128)(2,1)} %bitcast.5, bf16[16,32,2048]{2,1,0:T(8,128)(2,1)} %g_ref.1, f32[32,2048]{1,0:T(8,128)} %east_ref.1, ...), custom_call_target="tpu_custom_call" | custom-call | flops 1 | bytes 1 | tf_op jit(solution)/shard_map/pallas_call | solution.py:102
  2.7 1.5 %collective-permute-start.1 = (bf16[19,4,2048]{2,1,0:T(4,128)(2,1)S(1)}, bf16[19,4,2048]{2,1,0:T(4,128)(2,1)S(1)}, u32[]{:S(2)}, u32[]{:S(2)}) collective-permute-start(bf16[19,4,2048]{2,1,0:T(4,128)(2,1)S(1)} %get-tuple-element.32), channel_id=1, source_target_pairs={{0,2},{4,6},{8,10},{12,14},{16,18},{20,22},{24,26},{28,30},{32,34}... | collective-permute-start | bytes 933896 | tf_op jit(solution)/shard_map/ppermute | solution.py:429
  4.2 3.2 %collective-permute-start.2 = (bf16[56,2048]{1,0:T(8,128)(2,1)S(1)}, bf16[56,2048]{1,0:T(8,128)(2,1)S(1)}, u32[]{:S(2)}, u32[]{:S(2)}) collective-permute-start(bf16[56,2048]{1,0:T(8,128)(2,1)S(1)} %get-tuple-element.33), channel_id=1, source_target_pairs={{2,4},{6,8},{10,12},{14,16},{18,20},{22,24},{26,28},{30,32},{34,36... | collective-permute-start | bytes 688136 | tf_op jit(solution)/shard_map/ppermute | solution.py:429
  7.4 2.0 %shard_map.78 = (bf16[64,16,512]{2,1,0:T(8,128)(2,1)S(1)}, bf16[16,16,512]{2,1,0:T(8,128)(2,1)S(1)}) custom-call(bf16[16,32,2048]{2,1,0:T(8,128)(2,1)S(1)} %get-tuple-element.25.refs_0_.refs_1_.refs_3_.refs_2_, f32[3,32,2048]{2,1,0:T(8,128)S(1)} %get-tuple-element.26.refs_1_.refs_2_.refs_4_.refs_3_, ...), custom_call_target="tpu_custom_call" | custom-call | flops 1 | bytes 1 | tf_op jit(solution)/shard_map/pallas_call | solution.py:239
  9.5 2.7 %collective-permute-start.3 = (bf16[16,16,512]{2,1,0:T(8,128)(2,1)S(1)}, bf16[16,16,512]{2,1,0:T(8,128)(2,1)S(1)}, u32[]{:S(2)}, u32[]{:S(2)}) collective-permute-start(bf16[16,16,512]{2,1,0:T(8,128)(2,1)S(1)} %get-tuple-element.35), channel_id=1, source_target_pairs={{0,1},{1,0},{2,3},{3,2},{4,5},{5,4},{6,7},{7,6},{8,9},{9,8},{10,11... | collective-permute-start | bytes 786440 | tf_op jit(solution)/shard_map/ppermute | solution.py:415
  12.2 5.2 %shard_map.79 = (bf16[64,16,1536]{2,1,0:T(8,128)(2,1)S(1)}, bf16[16,16,1536]{2,1,0:T(8,128)(2,1)S(1)}) custom-call(bf16[64,16,512]{2,1,0:T(8,128)(2,1)S(1)} %get-tuple-element.27.refs_0_, bf16[16,32,2048]{2,1,0:T(8,128)(2,1)S(1)} %get-tuple-element.25.refs_0_.refs_1_.refs_3_.refs_2_, f32[3,32,2048]{2,1,0:T(8,128)S(1)} %get-tuple-element.26.refs_1_.refs_2_.refs_4_.refs_3_, ...), custom_call_target="tpu_custom_call" | custom-call | flops 1 | bytes 1 | tf_op jit(solution)/shard_map/pallas_call | solution.py:239
  17.9 1.2 %shard_map.80 = (f32[16,16,512]{2,1,0:T(8,128)S(1)}, f32[16,16,1536]{2,1,0:T(8,128)S(1)}) custom-call(bf16[512,1024]{1,0:T(8,128)(2,1)S(1)} %get-tuple-element.24.refs_2_.refs_3_.mix_ref.refs_5_.refs_4_, bf16[64,16,512]{2,1,0:T(8,128)(2,1)S(1)} %get-tuple-element.27.refs_0_, bf16[64,16,1536]{2,1,0:T(8,128)(2,1)S(1)} %get-tuple-element.28.refs_1_.refs_0_), custom_call_target="tpu_custom_call" | custom-call | flops 1 | bytes 1 | tf_op jit(solution)/shard_map/pallas_call | solution.py:305
  19.1 0.9 %copy-done = bf16[32,32,2048]{2,1,0:T(8,128)(2,1)S(1)} copy-done((bf16[32,32,2048]{2,1,0:T(8,128)(2,1)S(1)}, bf16[32,32,2048]{2,1,0:T(8,128)(2,1)}, u32[]{:S(2)}) %copy-start) | copy-done | bytes 4194328
  20.0 2.7 %shard_map.81.refs_2_.refs_0_ = f32[64,32]{1,0:T(8,128)S(1)} custom-call(bf16[32,32,2048]{2,1,0:T(8,128)(2,1)S(1)} %copy-done, bf16[64,16,512]{2,1,0:T(8,128)(2,1)S(1)} %get-tuple-element.27.refs_0_, bf16[64,16,1536]{2,1,0:T(8,128)(2,1)S(1)} %get-tuple-element.28.refs_1_.refs_0_), custom_call_target="tpu_custom_call" | custom-call | flops 1 | bytes 1 | tf_op jit(solution)/shard_map/pallas_call | solution.py:283
  22.8 4.7 %shard_map.82 = (bf16[64,16,1024]{2,1,0:T(8,128)(2,1)S(1)}, bf16[16,16,1024]{2,1,0:T(8,128)(2,1)S(1)}) custom-call(bf16[64,16,1536]{2,1,0:T(8,128)(2,1)S(1)} %get-tuple-element.28.refs_1_.refs_0_, f32[16,16,512]{2,1,0:T(8,128)S(1)} %get-tuple-element.31.refs_1_.own_i, f32[64,32]{1,0:T(8,128)S(1)} %shard_map.81.refs_2_.refs_0_, ...), custom_call_target="tpu_custom_call" | custom-call | flops 10000000000 | bytes 100000000 | tf_op jit(solution)/shard_map/pallas_call | solution.py:239
  27.4 2.9 %collective-permute-start.5 = (bf16[16,16,1024]{2,1,0:T(8,128)(2,1)S(1)}, bf16[16,16,1024]{2,1,0:T(8,128)(2,1)S(1)}, u32[]{:S(2)}, u32[]{:S(2)}) collective-permute-start(bf16[16,16,1024]{2,1,0:T(8,128)(2,1)S(1)} %get-tuple-element.40), channel_id=1, source_target_pairs={{0,1},{1,0},{2,3},{3,2},{4,5},{5,4},{6,7},{7,6},{8,9},{9,8},{10,11... | collective-permute-start | bytes 1572872 | tf_op jit(solution)/shard_map/ppermute | solution.py:415
  30.3 4.7 %shard_map.83 = (bf16[64,16,1024]{2,1,0:T(8,128)(2,1)S(1)}, bf16[16,16,1024]{2,1,0:T(8,128)(2,1)S(1)}) custom-call(bf16[64,16,1024]{2,1,0:T(8,128)(2,1)S(1)} %get-tuple-element.34.refs_0_, bf16[16,16,512]{2,1,0:T(8,128)(2,1)S(1)} %collective-permute-done.3.refs_1_.got_i.refs_2_, bf16[16,32,2048]{2,1,0:T(8,128)(2,1)S(1)} %get-tuple-element.25.refs_0_.refs_1_.refs_3_.refs_2_, ...), custom_call_target="tpu_custom_call" | custom-call | flops 1 | bytes 1 | tf_op jit(solution)/shard_map/pallas_call | solution.py:239
  35.5 2.7 %shard_map.88.refs_1_ = f32[64,32]{1,0:T(8,128)S(1)} custom-call(bf16[32,32,2048]{2,1,0:T(8,128)(2,1)S(1)} %copy-done, bf16[64,16,1024]{2,1,0:T(8,128)(2,1)S(1)} %get-tuple-element.34.refs_0_, bf16[64,16,1024]{2,1,0:T(8,128)(2,1)S(1)} %get-tuple-element.36.refs_1_), custom_call_target="tpu_custom_call" | custom-call | flops 1 | bytes 1 | tf_op jit(solution)/shard_map/pallas_call | solution.py:283
  38.2 1.9 %collective-permute-done.got_i.refs_3_ = bf16[16,16,1536]{2,1,0:T(8,128)(2,1)S(1)} collective-permute-done((bf16[16,16,1536]{2,1,0:T(8,128)(2,1)S(1)}, bf16[16,16,1536]{2,1,0:T(8,128)(2,1)S(1)}, u32[]{:S(2)}, u32[]{:S(2)}) %collective-permute-start) | collective-permute-done | bytes 786464 | tf_op jit(solution)/shard_map/ppermute | solution.py:415
  40.1 2.0 %collective-permute-start.8 = (f32[64,32]{1,0:T(8,128)S(1)}, f32[64,32]{1,0:T(8,128)S(1)}, u32[]{:S(2)}, u32[]{:S(2)}) collective-permute-start(f32[64,32]{1,0:T(8,128)S(1)} %shard_map.89.refs_0_), channel_id=1, source_target_pairs={{0,24},{2,26},{4,28},{6,30},{8,16},{10,18},{12,20},{14,22},{16,8},... | collective-permute-start | bytes 24584 | tf_op jit(solution)/shard_map/ppermute | solution.py:387
  42.0 1.3 %collective-permute-start.6 = (f32[64,32]{1,0:T(8,128)S(1)}, f32[64,32]{1,0:T(8,128)S(1)}, u32[]{:S(2)}, u32[]{:S(2)}) collective-permute-start(f32[64,32]{1,0:T(8,128)S(1)} %shard_map.89.refs_0_), channel_id=1, source_target_pairs={{0,8},{2,10},{4,12},{6,14},{8,0},{10,2},{12,4},{14,6},{16,24},{18,... | collective-permute-start | bytes 24584 | tf_op jit(solution)/shard_map/ppermute | solution.py:387
  43.3 1.2 %shard_map.84 = (f32[16,16,1024]{2,1,0:T(8,128)S(1)}, f32[16,16,1024]{2,1,0:T(8,128)S(1)}) custom-call(bf16[512,1024]{1,0:T(8,128)(2,1)S(1)} %get-tuple-element.24.refs_2_.refs_3_.mix_ref.refs_5_.refs_4_, bf16[64,16,1024]{2,1,0:T(8,128)(2,1)S(1)} %get-tuple-element.34.refs_0_, bf16[64,16,1024]{2,1,0:T(8,128)(2,1)S(1)} %get-tuple-element.36.refs_1_), custom_call_target="tpu_custom_call" | custom-call | flops 1 | bytes 1 | tf_op jit(solution)/shard_map/pallas_call | solution.py:305
  44.6 2.0 %collective-permute-done.7.refs_2_ = f32[64,32]{1,0:T(8,128)S(1)} collective-permute-done((f32[64,32]{1,0:T(8,128)S(1)}, f32[64,32]{1,0:T(8,128)S(1)}, u32[]{:S(2)}, u32[]{:S(2)}) %collective-permute-start.7) | collective-permute-done | bytes 8224 | tf_op jit(solution)/shard_map/ppermute | solution.py:387
  46.6 2.6 %collective-permute-start.11 = (f32[64,32]{1,0:T(8,128)S(1)}, f32[64,32]{1,0:T(8,128)S(1)}, u32[]{:S(2)}, u32[]{:S(2)}) collective-permute-start(f32[64,32]{1,0:T(8,128)S(1)} %shard_map.90.refs_0_), channel_id=1, source_target_pairs={{0,96},{2,98},{4,100},{6,102},{8,104},{10,106},{12,108},{14,110},{... | collective-permute-start | bytes 24584 | tf_op jit(solution)/shard_map/ppermute | solution.py:387
  50.0 1.3 %collective-permute-done.5.got_o = bf16[16,16,1024]{2,1,0:T(8,128)(2,1)S(1)} collective-permute-done((bf16[16,16,1024]{2,1,0:T(8,128)(2,1)S(1)}, bf16[16,16,1024]{2,1,0:T(8,128)(2,1)S(1)}, u32[]{:S(2)}, u32[]{:S(2)}) %collective-permute-start.5) | collective-permute-done | bytes 524320 | tf_op jit(solution)/shard_map/ppermute | solution.py:415
  51.3 1.5 %shard_map.85 = (bf16[16,32,2048]{2,1,0:T(8,128)(2,1)}, f32[8,128]{1,0:T(8,128)}) custom-call(f32[16,16,512]{2,1,0:T(8,128)S(1)} %get-tuple-element.31.refs_1_.own_i, bf16[16,16,512]{2,1,0:T(8,128)(2,1)S(1)} %collective-permute-done.3.refs_1_.got_i.refs_2_, f32[16,16,1024]{2,1,0:T(8,128)S(1)} %get-tuple-element.39.own_o.refs_4_, ...), custom_call_target="tpu_custom_call" | custom-call | flops 1 | bytes 1 | tf_op jit(solution)/shard_map/pallas_call | solution.py:342
  53.8 4.3 %collective-permute-start.14 = (f32[64,32]{1,0:T(8,128)S(1)}, f32[64,32]{1,0:T(8,128)S(1)}, u32[]{:S(2)}, u32[]{:S(2)}) collective-permute-start(f32[64,32]{1,0:T(8,128)S(1)} %shard_map.91.refs_0_), channel_id=1, source_target_pairs={{0,6},{2,4},{4,2},{6,0},{8,14},{10,12},{12,10},{14,8},{16,22},{18,... | collective-permute-start | bytes 24584 | tf_op jit(solution)/shard_map/ppermute | solution.py:387
  58.1 2.0 %collective-permute-start.13 = (f32[64,32]{1,0:T(8,128)S(1)}, f32[64,32]{1,0:T(8,128)S(1)}, u32[]{:S(2)}, u32[]{:S(2)}) collective-permute-start(f32[64,32]{1,0:T(8,128)S(1)} %shard_map.91.refs_0_), channel_id=1, source_target_pairs={{0,4},{2,6},{4,0},{6,2},{8,12},{10,14},{12,8},{14,10},{16,20},{18,... | collective-permute-start | bytes 24584 | tf_op jit(solution)/shard_map/ppermute | solution.py:387
  60.8 1.1 %shard_map.87 = (bf16[16,32,2048]{2,1,0:T(8,128)(2,1)}, f32[8,128]{1,0:T(8,128)S(1)}) custom-call(f32[16,16,1536]{2,1,0:T(8,128)S(1)} %get-tuple-element.29.own_i, bf16[16,16,1536]{2,1,0:T(8,128)(2,1)S(1)} %collective-permute-done.got_i.refs_3_, f32[16,16,1024]{2,1,0:T(8,128)S(1)} %get-tuple-element.37.own_o, ...), custom_call_target="tpu_custom_call", output_to_operand_aliasing={{0}: (4, {})} | custom-call | flops 1 | bytes 1 | tf_op jit(solution)/shard_map/pallas_call | solution.py:342
  (24 shorter events, 4.2 us)
Async XLA Ops:
  2.7 20.0 %collective-permute-start.1 = (bf16[19,4,2048]{2,1,0:T(4,128)(2,1)S(1)}, bf16[19,4,2048]{2,1,0:T(4,128)(2,1)S(1)}, u32[]{:S(2)}, u32[]{:S(2)}) collective-permute-start(bf16[19,4,2048]{2,1,0:T(4,128)(2,1)S(1)} %get-tuple-element.32), channel_id=1, source_target_pairs={{0,2},{4,6},{8,10},{12,14},{16,18},{20,22},{24,26},{28,30},{32,34}... | collective-permute-start | bytes 933896 | tf_op jit(solution)/shard_map/ppermute | solution.py:429
  4.2 18.5 %collective-permute-start.2 = (bf16[56,2048]{1,0:T(8,128)(2,1)S(1)}, bf16[56,2048]{1,0:T(8,128)(2,1)S(1)}, u32[]{:S(2)}, u32[]{:S(2)}) collective-permute-start(bf16[56,2048]{1,0:T(8,128)(2,1)S(1)} %get-tuple-element.33), channel_id=1, source_target_pairs={{2,4},{6,8},{10,12},{14,16},{18,20},{22,24},{26,28},{30,32},{34,36... | collective-permute-start | bytes 688136 | tf_op jit(solution)/shard_map/ppermute | solution.py:429
  9.5 20.8 %collective-permute-start.3 = (bf16[16,16,512]{2,1,0:T(8,128)(2,1)S(1)}, bf16[16,16,512]{2,1,0:T(8,128)(2,1)S(1)}, u32[]{:S(2)}, u32[]{:S(2)}) collective-permute-start(bf16[16,16,512]{2,1,0:T(8,128)(2,1)S(1)} %get-tuple-element.35), channel_id=1, source_target_pairs={{0,1},{1,0},{2,3},{3,2},{4,5},{5,4},{6,7},{7,6},{8,9},{9,8},{10,11... | collective-permute-start | bytes 786440 | tf_op jit(solution)/shard_map/ppermute | solution.py:415
  17.4 22.6 %collective-permute-start = (bf16[16,16,1536]{2,1,0:T(8,128)(2,1)S(1)}, bf16[16,16,1536]{2,1,0:T(8,128)(2,1)S(1)}, u32[]{:S(2)}, u32[]{:S(2)}) collective-permute-start(bf16[16,16,1536]{2,1,0:T(8,128)(2,1)S(1)} %get-tuple-element.30), channel_id=1, source_target_pairs={{0,1},{1,0},{2,3},{3,2},{4,5},{5,4},{6,7},{7,6},{8,9},{9,8},{10,11... | collective-permute-start | bytes 2359304 | tf_op jit(solution)/shard_map/ppermute | solution.py:415
  17.8 2.2 %copy-start = (bf16[32,32,2048]{2,1,0:T(8,128)(2,1)S(1)}, bf16[32,32,2048]{2,1,0:T(8,128)(2,1)}, u32[]{:S(2)}) copy-start(bf16[32,32,2048]{2,1,0:T(8,128)(2,1)} %f_ref.3) | copy-start | bytes 12582916
  27.4 23.9 %collective-permute-start.5 = (bf16[16,16,1024]{2,1,0:T(8,128)(2,1)S(1)}, bf16[16,16,1024]{2,1,0:T(8,128)(2,1)S(1)}, u32[]{:S(2)}, u32[]{:S(2)}) collective-permute-start(bf16[16,16,1024]{2,1,0:T(8,128)(2,1)S(1)} %get-tuple-element.40), channel_id=1, source_target_pairs={{0,1},{1,0},{2,3},{3,2},{4,5},{5,4},{6,7},{7,6},{8,9},{9,8},{10,11... | collective-permute-start | bytes 1572872 | tf_op jit(solution)/shard_map/ppermute | solution.py:415
  35.0 25.8 %collective-permute-start.4 = (bf16[16,16,1024]{2,1,0:T(8,128)(2,1)S(1)}, bf16[16,16,1024]{2,1,0:T(8,128)(2,1)S(1)}, u32[]{:S(2)}, u32[]{:S(2)}) collective-permute-start(bf16[16,16,1024]{2,1,0:T(8,128)(2,1)S(1)} %get-tuple-element.38), channel_id=1, source_target_pairs={{0,1},{1,0},{2,3},{3,2},{4,5},{5,4},{6,7},{7,6},{8,9},{9,8},{10,11... | collective-permute-start | bytes 1572872 | tf_op jit(solution)/shard_map/ppermute | solution.py:415
  40.1 4.5 %collective-permute-start.8 = (f32[64,32]{1,0:T(8,128)S(1)}, f32[64,32]{1,0:T(8,128)S(1)}, u32[]{:S(2)}, u32[]{:S(2)}) collective-permute-start(f32[64,32]{1,0:T(8,128)S(1)} %shard_map.89.refs_0_), channel_id=1, source_target_pairs={{0,24},{2,26},{4,28},{6,30},{8,16},{10,18},{12,20},{14,22},{16,8},... | collective-permute-start | bytes 24584 | tf_op jit(solution)/shard_map/ppermute | solution.py:387
  42.0 4.6 %collective-permute-start.7 = (f32[64,32]{1,0:T(8,128)S(1)}, f32[64,32]{1,0:T(8,128)S(1)}, u32[]{:S(2)}, u32[]{:S(2)}) collective-permute-start(f32[64,32]{1,0:T(8,128)S(1)} %shard_map.89.refs_0_), channel_id=1, source_target_pairs={{0,16},{2,18},{4,20},{6,22},{8,24},{10,26},{12,28},{14,30},{16,0},... | collective-permute-start | bytes 24584 | tf_op jit(solution)/shard_map/ppermute | solution.py:387
  42.0 4.6 %collective-permute-start.6 = (f32[64,32]{1,0:T(8,128)S(1)}, f32[64,32]{1,0:T(8,128)S(1)}, u32[]{:S(2)}, u32[]{:S(2)}) collective-permute-start(f32[64,32]{1,0:T(8,128)S(1)} %shard_map.89.refs_0_), channel_id=1, source_target_pairs={{0,8},{2,10},{4,12},{6,14},{8,0},{10,2},{12,4},{14,6},{16,24},{18,... | collective-permute-start | bytes 24584 | tf_op jit(solution)/shard_map/ppermute | solution.py:387
  46.6 7.0 %collective-permute-start.11 = (f32[64,32]{1,0:T(8,128)S(1)}, f32[64,32]{1,0:T(8,128)S(1)}, u32[]{:S(2)}, u32[]{:S(2)}) collective-permute-start(f32[64,32]{1,0:T(8,128)S(1)} %shard_map.90.refs_0_), channel_id=1, source_target_pairs={{0,96},{2,98},{4,100},{6,102},{8,104},{10,106},{12,108},{14,110},{... | collective-permute-start | bytes 24584 | tf_op jit(solution)/shard_map/ppermute | solution.py:387
  49.2 4.6 %collective-permute-start.10 = (f32[64,32]{1,0:T(8,128)S(1)}, f32[64,32]{1,0:T(8,128)S(1)}, u32[]{:S(2)}, u32[]{:S(2)}) collective-permute-start(f32[64,32]{1,0:T(8,128)S(1)} %shard_map.90.refs_0_), channel_id=1, source_target_pairs={{0,64},{2,66},{4,68},{6,70},{8,72},{10,74},{12,76},{14,78},{16,80}... | collective-permute-start | bytes 24584 | tf_op jit(solution)/shard_map/ppermute | solution.py:387
  49.7 4.0 %collective-permute-start.9 = (f32[64,32]{1,0:T(8,128)S(1)}, f32[64,32]{1,0:T(8,128)S(1)}, u32[]{:S(2)}, u32[]{:S(2)}) collective-permute-start(f32[64,32]{1,0:T(8,128)S(1)} %shard_map.90.refs_0_), channel_id=1, source_target_pairs={{0,32},{2,34},{4,36},{6,38},{8,40},{10,42},{12,44},{14,46},{16,48}... | collective-permute-start | bytes 24584 | tf_op jit(solution)/shard_map/ppermute | solution.py:387
  53.8 8.1 %collective-permute-start.14 = (f32[64,32]{1,0:T(8,128)S(1)}, f32[64,32]{1,0:T(8,128)S(1)}, u32[]{:S(2)}, u32[]{:S(2)}) collective-permute-start(f32[64,32]{1,0:T(8,128)S(1)} %shard_map.91.refs_0_), channel_id=1, source_target_pairs={{0,6},{2,4},{4,2},{6,0},{8,14},{10,12},{12,10},{14,8},{16,22},{18,... | collective-permute-start | bytes 24584 | tf_op jit(solution)/shard_map/ppermute | solution.py:387
  58.1 4.0 %collective-permute-start.13 = (f32[64,32]{1,0:T(8,128)S(1)}, f32[64,32]{1,0:T(8,128)S(1)}, u32[]{:S(2)}, u32[]{:S(2)}) collective-permute-start(f32[64,32]{1,0:T(8,128)S(1)} %shard_map.91.refs_0_), channel_id=1, source_target_pairs={{0,4},{2,6},{4,0},{6,2},{8,12},{10,14},{12,8},{14,10},{16,20},{18,... | collective-permute-start | bytes 24584 | tf_op jit(solution)/shard_map/ppermute | solution.py:387
  60.0 2.0 %collective-permute-start.12 = (f32[64,32]{1,0:T(8,128)S(1)}, f32[64,32]{1,0:T(8,128)S(1)}, u32[]{:S(2)}, u32[]{:S(2)}) collective-permute-start(f32[64,32]{1,0:T(8,128)S(1)} %shard_map.91.refs_0_), channel_id=1, source_target_pairs={{0,2},{2,0},{4,6},{6,4},{8,10},{10,8},{12,14},{14,12},{16,18},{18,... | collective-permute-start | bytes 24584 | tf_op jit(solution)/shard_map/ppermute | solution.py:387
